TPU v7x, 32 devices: a whole 2x2x4 slice. The times are simulated.
32 devices in a mesh: groups: 2 (over x), psg: 16 (over z, y, core).
Axes of the slice: x: 2, y: 2, z: 4, core: 2. Of those that a mesh axis runs over, the one named last changes fastest.
Arguments:
- passage_states: bfloat16 [16384, 1024], P(('groups', 'psg')), parts along dimension 0, may hold values from -6 to 6
- saved_preact: bfloat16 [16384, 2048], P(('groups', 'psg')), parts along dimension 0, may hold values from -6 to 6
- saved_resid: bfloat16 [16384, 1024], P(('groups', 'psg')), parts along dimension 0, may hold values from -84 to 84
- w_in: bfloat16 [2048, 1024], P('psg'), may hold values from -0.1875 to 0.1875
- w_out: bfloat16 [2048, 1024], P('psg'), may hold values from -0.125 to 0.125
- norm_gain: float32 [1024], replicated, may hold values from 0.1 to 1.9
- query_emb: bfloat16 [64, 1024], P(('groups', 'psg')), parts along dimension 0, may hold values from -8 to 8
- score_grads: bfloat16 [64, 32], P(('groups', 'psg')), parts along dimension 0, may hold values from -6 to 6
- retrieved: int32 [64, 32], P(('groups', 'psg')), parts along dimension 0, may hold values from 0 to 63, all different within a row
- placement_map: int32 [128], P('groups'), parts along dimension 0, may hold values from 0 to 63, each once
- live_counts: int32 [32], P('groups'), parts along dimension 0, may hold values from 1 to 4, 40 in all
Outputs:
- input_grad: bfloat16 [16384, 1024], P(('groups', 'psg')), parts along dimension 0
- grad_in: float32 [4096, 1024], P(('groups', 'psg')), parts along dimension 0
- grad_out: float32 [4096, 1024], P(('groups', 'psg')), parts along dimension 0
- question_grad: float32 [64, 1024], P(('groups', 'psg')), parts along dimension 0
There are 2 independent parts, one for each index of `groups`. A program takes and returns all parts, laid end to end along the dimension named above; an argument that names none is the same for every part. Nothing has to cross between parts.
Inputs may be any that keep to these rules, and one draw needn't show every extreme that they name: `retrieved`: each row names 32 different passage ids. `placement_map`: storage place p means slot p mod 4 of owner p div 4, tokens p * 128 onward of the passage arrays. Owner o holds live passages in its slots 0 to live_counts[o] - 1; pairs placed in other slots contribute nothing.
All inputs are finite; a program needn't handle non-finite values.
Results may differ from a plain program's by a relative error of at most 0.007.
Values may be sent and summed in bfloat16 or wider, within the bound.
No kernel may reach another device: no remote copies, remote signals or barrier semaphores. Data moves between devices by JAX's collectives and lax.ppermute only.
A program may use at most 128 MiB of HBM per device.

v0:
```python
import jax
import jax.numpy as jnp
from jax import lax
from jax.sharding import PartitionSpec as P

LEN = 128


def gelu_terms(preact):
    cdf = 0.5 * (1.0 + jax.scipy.special.erf(preact * 0.7071067811865476))
    density = jnp.exp(-0.5 * preact * preact) * 0.3989422804014327
    return (preact * cdf, cdf + preact * density)


def normalize(resid):
    values = resid.astype(jnp.float32)
    centre = values - jnp.mean(values, axis=-1, keepdims=True)
    inverse = lax.rsqrt(jnp.mean(centre * centre, axis=-1, keepdims=True) + 1e-06)
    return (centre * inverse, inverse)


def shards(
    passage_states,
    saved_preact,
    saved_resid,
    w_in,
    w_out,
    norm_gain,
    query_emb,
    score_grads,
    retrieved,
    placement_map,
    live_counts,
):
    owners = lax.axis_size("psg")
    tokens = saved_resid.shape[0]
    feature_width = saved_resid.shape[1]
    slot_count = tokens // LEN
    normed, inverse = normalize(saved_resid)
    pooled = (
        (normed * norm_gain)
        .reshape(slot_count, LEN, feature_width)
        .mean(axis=1)
        .astype(jnp.bfloat16)
    )
    placed = jnp.take(placement_map, retrieved, axis=0)
    alive = placed % slot_count < jnp.take(live_counts, placed // slot_count, axis=0)
    weights = jnp.where(alive, score_grads.astype(jnp.float32), 0.0)
    columns = lax.broadcasted_iota(jnp.int32, (1, 1, slot_count * owners), 2)
    local_pairs = jnp.sum(
        jnp.where(placed[:, :, None] == columns, weights[:, :, None], 0.0), axis=1
    ).astype(jnp.bfloat16)
    owner_pairs = lax.all_to_all(local_pairs, "psg", split_axis=1, concat_axis=0, tiled=True)
    all_queries = lax.all_gather(query_emb, "psg", axis=0, tiled=True)
    pass_grad = lax.dot_general(
        owner_pairs, all_queries, (((0,), (0,)), ((), ())), preferred_element_type=jnp.float32
    )
    token_grad = jnp.broadcast_to(
        (pass_grad / LEN)[:, None, :], (slot_count, LEN, feature_width)
    ).reshape(tokens, feature_width)
    scaled = token_grad * norm_gain
    resid_grad = inverse * (
        scaled
        - jnp.mean(scaled, axis=-1, keepdims=True)
        - normed * jnp.mean(scaled * normed, axis=-1, keepdims=True)
    )
    resid_bf = resid_grad.astype(jnp.bfloat16)
    activated, gelu_slope = gelu_terms(saved_preact.astype(jnp.float32))
    act_bf = activated.astype(jnp.bfloat16)
    running = resid_grad
    piece_in = lax.all_gather(w_in, "psg", axis=0, tiled=True)
    piece_out = lax.all_gather(w_out, "psg", axis=0, tiled=True)
    hidden = lax.dot_general(
        resid_bf, piece_out, (((1,), (1,)), ((), ())), preferred_element_type=jnp.float32
    )
    pre_cols = (hidden * gelu_slope).astype(jnp.bfloat16)
    running = running + jnp.dot(pre_cols, piece_in, preferred_element_type=jnp.float32)
    pre_all = pre_cols
    running, pre_grad = (running, pre_all)
    input_grad = running.astype(jnp.bfloat16)
    pre_cols = pre_grad
    in_rows = lax.dot_general(
        pre_cols, passage_states, (((0,), (0,)), ((), ())), preferred_element_type=jnp.float32
    )
    out_rows = lax.dot_general(
        act_bf, resid_bf, (((0,), (0,)), ((), ())), preferred_element_type=jnp.float32
    )
    stacked = lax.psum_scatter(
        jnp.concatenate([in_rows, out_rows], axis=1), "psg", scatter_dimension=0, tiled=True
    )
    grad_in = stacked[:, :feature_width]
    grad_out = stacked[:, feature_width:]
    all_pooled = lax.all_gather(pooled, "psg", axis=0, tiled=True)
    question_grad = jnp.dot(local_pairs, all_pooled, preferred_element_type=jnp.float32)
    return (input_grad, grad_in, grad_out, question_grad)


def solution(mesh):
    return jax.shard_map(
        shards,
        mesh=mesh,
        in_specs=(
            P(("groups", "psg"), None),
            P(("groups", "psg"), None),
            P(("groups", "psg"), None),
            P("psg", None),
            P("psg", None),
            P(),
            P(("groups", "psg"), None),
            P(("groups", "psg"), None),
            P(("groups", "psg"), None),
            P("groups"),
            P("groups"),
        ),
        out_specs=(
            P(("groups", "psg"), None),
            P(("groups", "psg"), None),
            P(("groups", "psg"), None),
            P(("groups", "psg"), None),
        ),
        check_vma=False,
    )
```

profile of v0, /device:TPU:0, one launch (start us, length us, event | category | flops | bytes accessed | tf_op | source)
XLA Modules:
  0.0 306.5 jit_solution(9761979157142200585)
XLA Ops:
  7.2 0.0 copy-start
  7.2 0.0 copy-start.1
  7.2 0.0 copy-start.7
  7.2 0.0 copy-start.2
  7.2 0.0 all-gather.5.cloned.1.call-start
  7.3 0.7 all-gather.5.cloned.1.call-update
  7.9 0.0 all-gather.7.cloned.1.call-start
  8.0 0.7 all-gather.7.cloned.1.call-update
  8.7 0.7 compare_select_fusion.1
  9.4 0.1 reshape.88
  9.5 0.0 copy-start.6
  9.5 0.0 copy-start.5
  9.5 1.4 gather_fusion
  10.9 0.1 reshape.87
  11.0 0.7 compare_select_fusion
  11.7 0.1 reshape.96
  11.8 0.0 copy-done.1
  11.8 0.8 gather_fusion.1
  12.6 0.1 reshape.95
  12.7 0.0 copy-done.7
  12.7 0.1 select_reduce_fusion
  12.8 0.1 convert_element_type.34
  12.9 0.6 copy.24
  13.5 7.4 %all-to-all-start = ((bf16[2,16,4]{2,0,1:T(2,128)(2,1)}), bf16[2,16,4]{2,0,1:T(2,128)(2,1)S(1)}, u32[]{:S(2)}, u32[]{:S(2)}) async-start(bf16[2,16,4]{2,0,1:T(2,128)(2,1)} %copy.24), calls=%async_computation | async-start | bytes 16384 | tf_op jit(solution)/shard_map/all_to_all | solution.py:53
  20.9 0.0 reduce-scatter.2.cloned.1.call-start
  20.9 0.0 copy-done.2
  21.0 0.2 convert_reduce_fusion
  21.2 0.4 fusion.17
  21.6 0.0 copy-done.6
  21.6 22.0 %all-gather = bf16[16,2,1024]{2,1,0:T(2,128)(2,1)S(1)} all-gather(bf16[1,2,1024]{2,1,0:T(2,128)(2,1)S(1)} %bitcast.34), channel_id=1, replica_groups=mesh['groups'=2,'psg'=16] {'psg'}, dimensions={0}, use_global_device_ids=true | all-gather | bytes 69632 | tf_op jit(solution)/shard_map/all_gather | solution.py:54
  43.6 0.0 all-to-all-done
  43.6 0.2 convolution_multiply_fusion
  43.8 0.0 copy-done.5
  43.8 0.0 copy-start.8
  43.8 0.5 fusion.14
  44.4 0.5 bitcast_reduce_fusion
  44.9 0.6 fusion.21
  45.5 0.0 copy-done.8
  45.5 4.9 %fusion.18 = f32[2048,1024]{0,1:T(8,128)} fusion(bf16[512,1024]{1,0:T(8,128)(2,1)S(1)} %fusion.21, bf16[512,2048]{1,0:T(8,128)(2,1)S(1)} %copy-done.8), kind=kOutput, calls=%fused_computation.28 | convolution fusion | flops 2153775104 | bytes 11534336 | tf_op jit(solution)/shard_map/dot_general | solution.py:85
  50.4 13.4 %all-gather.5.cloned.1.call-done = bf16[2048,1024]{1,0:T(8,128)(2,1)} async-done(((bf16[128,1024]{1,0:T(8,128)(2,1)}), bf16[2048,1024]{1,0:T(8,128)(2,1)}) %all-gather.5.cloned.1.call-update) | async-done | bytes 4194320 | tf_op jit(solution)/shard_map/all_gather | solution.py:72
  63.8 6.3 %fusion.7 = bf16[512,2048]{1,0:T(8,128)(2,1)S(1)} fusion(bf16[512,2048]{1,0:T(8,128)(2,1)} %param.12, bf16[512,1024]{1,0:T(8,128)(2,1)S(1)} %fusion.21, bf16[2048,1024]{1,0:T(8,128)(2,1)} %all-gather.5.cloned.1.call-done), kind=kOutput, calls=%fused_computation.15 | convolution fusion | flops 2159017984 | bytes 9437184 | tf_op jit(solution)/shard_map/dot_general | solution.py:73
  70.0 0.0 copy-start.4
  70.1 1.3 copy-done.4
  71.4 0.0 copy-done
  71.4 0.0 copy-start.3
  71.4 2.4 fusion.25
  73.8 1.1 copy-done.3
  74.9 6.3 %pad_maximum_fusion = f32[2048,2048]{0,1:T(8,128)} fusion(f32[2048,1024]{0,1:T(8,128)S(1)} %copy-done.3, f32[2048,1024]{0,1:T(8,128)S(1)} %fusion.25), kind=kLoop, calls=%fused_computation.2 | loop fusion | flops 4194304 | bytes 33554432 | tf_op jit(solution)/shard_map/concatenate | solution.py:89
  81.2 0.0 reduce-scatter.2.cloned.1.call-update
  81.2 19.7 %all-gather.1 = bf16[16,4,1024]{2,1,0:T(4,128)(2,1)S(1)} all-gather(bf16[1,4,1024]{2,1,0:T(4,128)(2,1)S(1)} %fusion.22), channel_id=1, replica_groups=mesh['groups'=2,'psg'=16] {'psg'}, dimensions={0}, use_global_device_ids=true | all-gather | bytes 139264 | tf_op jit(solution)/shard_map/all_gather | solution.py:93
  100.9 0.7 fusion.26
  101.7 13.6 %all-gather.7.cloned.1.call-done = bf16[2048,1024]{1,0:T(8,128)(2,1)} async-done(((bf16[128,1024]{1,0:T(8,128)(2,1)}), bf16[2048,1024]{1,0:T(8,128)(2,1)}) %all-gather.7.cloned.1.call-update) | async-done | bytes 4194320 | tf_op jit(solution)/shard_map/all_gather | solution.py:71
  115.2 6.2 %add_convert_fusion = bf16[512,1024]{1,0:T(8,128)(2,1)} fusion(bf16[512,1024]{1,0:T(8,128)(2,1)S(1)} %copy-done.2, bf16[512,2048]{1,0:T(8,128)(2,1)} %copy-done.4, bf16[2048,1024]{1,0:T(8,128)(2,1)} %all-gather.7.cloned.1.call-done, f32[512]{0:T(512)S(1)} %broadcast_multiply_fusion, f32[512]{0:T(512)S(1)} %multiply_bitcast_fusion, f32[1024]{0:T(1024)S(1)} %copy-done.5, ...), kind=kOutput, calls=%fused_computation.32 | convolution fusion | flops 2152726528 | bytes 8417280 | tf_op jit(solution)/shard_map/dot_general | solution.py:77
  121.5 175.3 %reduce-scatter.2.cloned.1.call-done = f32[128,2048]{0,1:T(8,128)} async-done(((f32[2048,2048]{0,1:T(8,128)}), f32[128,2048]{0,1:T(8,128)}) %reduce-scatter.2.cloned.1.call-update) | async-done | bytes 1048592 | tf_op jit(solution)/shard_map/reduce_scatter | solution.py:88
  296.8 1.3 fusion.24
  298.0 1.0 copy.26
  299.0 1.0 copy.25
  (10 shorter events, 0.1 us)
Async XLA Ops:
  7.2 64.2 %copy-start = (bf16[512,1024]{1,0:T(8,128)(2,1)S(1)}, bf16[512,1024]{1,0:T(8,128)(2,1)}, u32[]{:S(2)}) copy-start(bf16[512,1024]{1,0:T(8,128)(2,1)} %param.11) | copy-start | bytes 3145732
  7.2 4.6 %copy-start.1 = (s32[16]{0:T(128)S(1)}, s32[16]{0:T(128)}, u32[]{:S(2)}) copy-start(s32[16]{0:T(128)} %param.21) | copy-start | bytes 196
  7.2 5.5 %copy-start.7 = (bf16[2,32]{1,0:T(2,128)(2,1)S(1)}, bf16[2,32]{1,0:T(2,128)(2,1)}, u32[]{:S(2)}) copy-start(bf16[2,32]{1,0:T(2,128)(2,1)} %param.18) | copy-start | bytes 388
  7.2 13.7 %copy-start.2 = (bf16[512,1024]{1,0:T(8,128)(2,1)S(1)}, bf16[512,1024]{1,0:T(8,128)(2,1)}, u32[]{:S(2)}) copy-start(bf16[512,1024]{1,0:T(8,128)(2,1)} %param.13) | copy-start | bytes 3145732
  7.2 56.6 %all-gather.5.cloned.1.call-start = ((), (), s32[]{:S(2)}) async-start(), calls=%async_computation.2 | async-start | bytes 4456448 | tf_op jit(solution)/shard_map/all_gather | solution.py:72
  7.9 107.3 %all-gather.7.cloned.1.call-start = ((), (), s32[]{:S(2)}) async-start(), calls=%async_computation.3 | async-start | bytes 4456448 | tf_op jit(solution)/shard_map/all_gather | solution.py:71
  9.5 12.1 %copy-start.6 = (bf16[2,1024]{1,0:T(2,128)(2,1)S(1)}, bf16[2,1024]{1,0:T(2,128)(2,1)}, u32[]{:S(2)}) copy-start(bf16[2,1024]{1,0:T(2,128)(2,1)} %param.17) | copy-start | bytes 12292
  9.5 34.4 %copy-start.5 = (f32[1024]{0:T(1024)S(1)}, f32[1024]{0:T(1024)}, u32[]{:S(2)}) copy-start(f32[1024]{0:T(1024)} %param.16) | copy-start | bytes 12292
  13.5 30.1 %all-to-all-start = ((bf16[2,16,4]{2,0,1:T(2,128)(2,1)}), bf16[2,16,4]{2,0,1:T(2,128)(2,1)S(1)}, u32[]{:S(2)}, u32[]{:S(2)}) async-start(bf16[2,16,4]{2,0,1:T(2,128)(2,1)} %copy.24), calls=%async_computation | async-start | bytes 16384 | tf_op jit(solution)/shard_map/all_to_all | solution.py:53
  20.9 275.9 %reduce-scatter.2.cloned.1.call-start = ((), (), s32[]{:S(2)}) async-start(), calls=%async_computation.4 | async-start | bytes 17825792 | tf_op jit(solution)/shard_map/reduce_scatter | solution.py:88
  43.8 1.7 copy-start.8
  70.0 1.3 copy-start.4
  71.4 3.6 %copy-start.3 = (f32[2048,1024]{0,1:T(8,128)S(1)}, f32[2048,1024]{0,1:T(8,128)}, u32[]{:S(2)}) copy-start(f32[2048,1024]{0,1:T(8,128)} %fusion.18) | copy-start | bytes 25165828
Sparse Core Ops, SparseCore 0:
  10.2 53.5 all-gather.4
  65.9 49.2 all-gather.6
  119.4 177.3 reduce-scatter.1
where the time goes:
time: 307 us
  waiting for transfers between devices  204 us (66%)
  blocking collectives  41.7 us (14%)
  matrix products  20.7 us (7%)
  between operations  13.9 us (5%)
  other arithmetic  10 us (3%)
  local copies, waits for them, and re-layouts  9.07 us (3%)
  starting transfers between devices  7.5 us (2%)
    reduce_scatter x1, waiting for transfers between devices, shards(): lax.psum_scatter(jnp.concatenate([in_rows, out_rows], axis=1), 'psg', sca...  175 us
    all_gather x1, blocking collectives, shards(): all_queries = lax.all_gather(query_emb, 'psg', axis=0, tiled=True)  22 us
    all_gather x1, blocking collectives, shards(): all_pooled = lax.all_gather(pooled, 'psg', axis=0, tiled=True)  19.7 us
    all_gather x1, waiting for transfers between devices, shards(): piece_in = lax.all_gather(w_in, 'psg', axis=0, tiled=True)  13.6 us
    all_gather x1, waiting for transfers between devices, shards(): piece_out = lax.all_gather(w_out, 'psg', axis=0, tiled=True)  13.4 us
    all_to_all x1, starting transfers between devices, shards(): lax.all_to_all(local_pairs, 'psg', split_axis=1, concat_axis=0, tiled=True)  7.39 us
    dot_general x1, matrix products, shards(): lax.dot_general(resid_bf, piece_out, (((1,), (1,)), ((), ())), preferred_...  6.27 us
    concatenate x1, other arithmetic, shards(): jnp.concatenate([in_rows, out_rows], axis=1)  6.26 us
  transfers between devices with their start and end apart: 4, of which 3 were waited for; matrix products, arithmetic and copies ran while one was open for 11% of the time, Pallas kernels for 0%

commit v1 on v0

v1 whole, which is shorter than its diff:
```python
import functools

import jax
import jax.numpy as jnp
from jax import lax
from jax.experimental import pallas as pl
from jax.experimental.pallas import tpu as pltpu
from jax.sharding import PartitionSpec as P

LEN = 128
BF = jnp.bfloat16
F32 = jnp.float32
VMEM_LIMIT = 40 << 20


def params(**kw):
    return pltpu.CompilerParams(vmem_limit_bytes=VMEM_LIMIT, **kw)


def cost(flops, nbytes):
    return pl.CostEstimate(flops=int(flops), bytes_accessed=int(nbytes), transcendentals=0)


def swap(x, mask):
    n = lax.axis_size("psg")
    return lax.ppermute(x, "psg", [(i, i ^ mask) for i in range(n)])


def pack_kernel(slots, d_ref, place_ref, live_ref, resid_ref, gain_ref, query_ref, score_ref, ret_ref, out_ref):
    me = d_ref[0]
    passages = place_ref.shape[0]
    width = out_ref.shape[1]
    queries, picks = ret_ref.shape
    ids = ret_ref[...]

    def look(i, placed):
        p = place_ref[i]
        owner = p // slots
        slot = p % slots
        rel = (owner ^ me) * slots + slot
        rel = jnp.where(slot < live_ref[owner], rel, -1)
        return jnp.where(ids == i, rel, placed)

    placed = lax.fori_loop(0, passages, look, jnp.full(ids.shape, -1, jnp.int32), unroll=8)
    score = score_ref[...].astype(F32)
    lanes = max(passages, 128)
    cols = lax.broadcasted_iota(jnp.int32, (queries, lanes), 1)
    pairs = jnp.zeros((queries, lanes), F32)
    for k in range(picks):
        pairs = pairs + jnp.where(cols == placed[:, k : k + 1], score[:, k : k + 1], 0.0)
    if lanes < width:
        pairs = jnp.concatenate([pairs, jnp.zeros((queries, width - lanes), F32)], axis=1)
    rows = []
    for s in range(slots):
        x = resid_ref[s * LEN : (s + 1) * LEN, :].astype(F32)
        centre = x - jnp.mean(x, axis=-1, keepdims=True)
        inverse = lax.rsqrt(jnp.mean(centre * centre, axis=-1, keepdims=True) + 1e-06)
        rows.append(jnp.mean(centre * inverse, axis=0, keepdims=True) * gain_ref[...])
    out_ref[...] = jnp.concatenate(rows + [query_ref[...].astype(F32), pairs], axis=0).astype(BF)


def pack(slots, me, placement, live, resid, gain, query, score, retrieved):
    width = resid.shape[1]
    queries = query.shape[0]
    smem = pl.BlockSpec(memory_space=pltpu.SMEM)
    vmem = pl.BlockSpec(memory_space=pltpu.VMEM)
    return pl.pallas_call(
        functools.partial(pack_kernel, slots),
        out_shape=jax.ShapeDtypeStruct((slots + 2 * queries, width), BF),
        in_specs=[smem] * 3 + [vmem] * 5,
        out_specs=vmem,
        compiler_params=params(),
        cost_estimate=cost(1e6, 3e6),
        name="pack",
    )(me, placement, live, resid, gain, query, score, retrieved)


def resid_kernel(slots, queries, own_ref, nb_ref, all_ref, gain_ref, bf_ref, full_ref, question_ref, pass_ref):
    step = pl.program_id(0)
    rows = slots + 2 * queries
    total = all_ref.shape[0]
    lanes = max(total // rows * slots, 128)

    @pl.when(step == 0)
    def _():
        table = all_ref[...]
        head = all_ref[:, :lanes].astype(F32)
        r = lax.broadcasted_iota(jnp.int32, (total, lanes), 0)
        c = lax.broadcasted_iota(jnp.int32, (total, lanes), 1)
        inside = r % rows
        moved = pltpu.roll(head, total - queries, 0)
        is_query = (inside >= slots) & (inside < slots + queries)
        fc = lax.broadcasted_iota(jnp.int32, (lanes, 128), 0)
        fs = lax.broadcasted_iota(jnp.int32, (lanes, 128), 1)
        picked = jnp.zeros((total, 128), F32)
        for k in range(2):
            mine = jnp.where(is_query & (c // slots == ((r // rows) ^ k)), moved, 0.0).astype(BF)
            fold = ((fc % slots + k * slots) == fs).astype(F32).astype(BF)
            picked = picked + jnp.dot(mine, fold, preferred_element_type=F32)
        grads = lax.dot_general(
            picked.astype(BF), table, (((0,), (0,)), ((), ())), preferred_element_type=F32
        )
        pass_ref[...] = grads[: 2 * slots] * gain_ref[...] * (1.0 / LEN)
        own = head[:rows]
        ec = lax.broadcasted_iota(jnp.int32, (lanes, total), 0)
        er = lax.broadcasted_iota(jnp.int32, (lanes, total), 1)
        spread = ((er // rows == ec // slots) & (er % rows == ec % slots)).astype(F32).astype(BF)
        weights = jnp.dot(own.astype(BF), spread, preferred_element_type=F32).astype(BF)
        result = jnp.dot(weights, table, preferred_element_type=F32)
        question_ref[...] = result[slots + queries :]

    for k, src in enumerate((own_ref, nb_ref)):
        x = src[...].astype(F32)
        centre = x - jnp.mean(x, axis=-1, keepdims=True)
        inverse = lax.rsqrt(jnp.mean(centre * centre, axis=-1, keepdims=True) + 1e-06)
        normed = centre * inverse
        scaled = pass_ref[pl.ds(k * slots + step, 1), :]
        base = scaled - jnp.mean(scaled, axis=-1, keepdims=True)
        grad = inverse * (base - normed * jnp.mean(scaled * normed, axis=-1, keepdims=True))
        bf_ref[k] = grad.astype(BF)
        if k == 0:
            full_ref[...] = grad


def resid_grads(slots, queries, own, nb, table, gain):
    tokens, width = own.shape
    total = table.shape[0]
    return pl.pallas_call(
        functools.partial(resid_kernel, slots, queries),
        grid=(slots,),
        out_shape=(
            jax.ShapeDtypeStruct((2, tokens, width), BF),
            jax.ShapeDtypeStruct((tokens, width), F32),
            jax.ShapeDtypeStruct((queries, width), F32),
        ),
        in_specs=[
            pl.BlockSpec((LEN, width), lambda s: (s, 0)),
            pl.BlockSpec((LEN, width), lambda s: (s, 0)),
            pl.BlockSpec((total, width), lambda s: (0, 0)),
            pl.BlockSpec((1, width), lambda s: (0, 0)),
        ],
        out_specs=(
            pl.BlockSpec((2, LEN, width), lambda s: (0, s, 0)),
            pl.BlockSpec((LEN, width), lambda s: (s, 0)),
            pl.BlockSpec((queries, width), lambda s: (0, 0)),
        ),
        scratch_shapes=[pltpu.VMEM((2 * slots, width), F32)],
        compiler_params=params(),
        cost_estimate=cost(2e7, 8e6),
        name="resid_grads",
    )(own, nb, table, gain)


def copy_kernel(ids_ref, in_ref, out_ref):
    out_ref[...] = in_ref[...]


def pick_columns(preact, chip, core, half, rows):
    tokens = preact.shape[0]
    if rows % 128:
        view = preact.reshape(tokens, half, 2, rows)
        view = jnp.take(view, jnp.arange(half) ^ chip, axis=1)
        view = lax.dynamic_index_in_dim(view, core, axis=2, keepdims=False)
        return view.reshape(tokens, half * rows)
    return pl.pallas_call(
        copy_kernel,
        grid_spec=pltpu.PrefetchScalarGridSpec(
            num_scalar_prefetch=1,
            grid=(half,),
            in_specs=[pl.BlockSpec((tokens, rows), lambda j, ids: (0, (ids[0] ^ j) * 2 + ids[1]))],
            out_specs=pl.BlockSpec((tokens, rows), lambda j, ids: (0, j)),
        ),
        out_shape=jax.ShapeDtypeStruct((tokens, half * rows), preact.dtype),
        compiler_params=params(),
        cost_estimate=cost(0, 2e6),
        name="pick_columns",
    )(jnp.stack([chip, core]), preact)


def gelu_kernel(own_ref, nb_ref, act_ref, slope_ref):
    for k, src in enumerate((own_ref, nb_ref)):
        z = src[...].astype(F32)
        cdf = 0.5 * (1.0 + lax.erf(z * 0.7071067811865476))
        density = jnp.exp(-0.5 * z * z) * 0.3989422804014327
        act_ref[k] = (z * cdf).astype(BF)
        slope_ref[k] = cdf + z * density


def gelu(own, nb):
    tokens, units = own.shape
    block = 128
    return pl.pallas_call(
        gelu_kernel,
        grid=(units // block,),
        in_specs=[pl.BlockSpec((tokens, block), lambda j: (0, j))] * 2,
        out_specs=[pl.BlockSpec((2, tokens, block), lambda j: (0, 0, j))] * 2,
        out_shape=(
            jax.ShapeDtypeStruct((2, tokens, units), BF),
            jax.ShapeDtypeStruct((2, tokens, units), F32),
        ),
        compiler_params=params(),
        cost_estimate=cost(6e7, 8e6),
        name="gelu",
    )(own, nb)


def grad_out_kernel(act_ref, resid_ref, out_ref):
    out_ref[...] = lax.dot_general(
        act_ref[...], resid_ref[...], (((0,), (0,)), ((), ())), preferred_element_type=F32
    ).astype(BF)


def grad_out_part(act, resid):
    tokens, units = act.shape
    width = resid.shape[1]
    block = 256
    return pl.pallas_call(
        grad_out_kernel,
        grid=(units // block,),
        in_specs=[
            pl.BlockSpec((tokens, block), lambda j: (0, j)),
            pl.BlockSpec((tokens, width), lambda j: (0, 0)),
        ],
        out_specs=pl.BlockSpec((block, width), lambda j: (j, 0)),
        out_shape=jax.ShapeDtypeStruct((units, width), BF),
        compiler_params=params(),
        cost_estimate=cost(2 * tokens * units * width, 6e6),
        name="grad_out",
    )(act, resid)


def grad_in_kernel(resid_ref, w_ref, slope_ref, own_ref, nb_ref, pre_ref, out_ref):
    tokens = own_ref.shape[0]
    hidden = lax.dot_general(
        resid_ref[...], w_ref[...], (((1,), (1,)), ((), ())), preferred_element_type=F32
    )
    pre = (hidden * slope_ref[...]).astype(BF)
    pre_ref[...] = pre
    contract = (((0,), (0,)), ((), ()))
    out = lax.dot_general(pre[:tokens], own_ref[...], contract, preferred_element_type=F32)
    out = out + lax.dot_general(pre[tokens:], nb_ref[...], contract, preferred_element_type=F32)
    out_ref[...] = out.astype(BF)


def grad_in_part(resid, w_out, slope, states, states_nb):
    tokens, width = resid.shape
    units = w_out.shape[0]
    block = 256
    whole = lambda j: (0, 0)
    return pl.pallas_call(
        grad_in_kernel,
        grid=(units // block,),
        in_specs=[
            pl.BlockSpec((tokens, width), whole),
            pl.BlockSpec((block, width), lambda j: (j, 0)),
            pl.BlockSpec((tokens, block), lambda j: (0, j)),
            pl.BlockSpec(states.shape, whole),
            pl.BlockSpec(states.shape, whole),
        ],
        out_specs=(
            pl.BlockSpec((tokens, block), lambda j: (0, j)),
            pl.BlockSpec((block, width), lambda j: (j, 0)),
        ),
        out_shape=(
            jax.ShapeDtypeStruct((tokens, units), BF),
            jax.ShapeDtypeStruct((units, width), BF),
        ),
        compiler_params=params(),
        cost_estimate=cost(4 * tokens * units * width, 14e6),
        name="grad_in",
    )(resid, w_out, slope, states, states_nb)


def input_nb_kernel(pre_ref, w_ref, out_ref):
    out_ref[...] = jnp.dot(pre_ref[0], w_ref[...], preferred_element_type=F32).astype(BF)


def input_own_kernel(pre_ref, w_ref, resid_ref, nb_ref, out_ref):
    total = jnp.dot(pre_ref[0], w_ref[...], preferred_element_type=F32)
    out_ref[...] = (total + nb_ref[...].astype(F32) + resid_ref[...]).astype(BF)


def input_part(pre, w_in, which, extra):
    _, tokens, units = pre.shape
    width = w_in.shape[1]
    block = 256
    row = pl.BlockSpec((block, width), lambda i: (i, 0))
    return pl.pallas_call(
        input_own_kernel if extra else input_nb_kernel,
        grid=(tokens // block,),
        in_specs=[
            pl.BlockSpec((1, block, units), lambda i: (which, i, 0)),
            pl.BlockSpec((units, width), lambda i: (0, 0)),
        ]
        + [row] * len(extra),
        out_specs=row,
        out_shape=jax.ShapeDtypeStruct((tokens, width), BF),
        compiler_params=params(),
        cost_estimate=cost(2 * tokens * units * width, 5e6),
        name="input_own" if extra else "input_nb",
    )(pre, w_in, *extra)


def gather(x, order):
    done = []
    for mask in order:
        pos = sum(1 for other in done if other > mask)
        x = jnp.stack([x, swap(x, mask)], axis=pos)
        done.append(mask)
    return x


def reduce_step(x, mask, left, last):
    pos = sum(1 for other in left if other > mask)
    keep = lax.index_in_dim(x, 0, pos, keepdims=False)
    send = lax.index_in_dim(x, 1, pos, keepdims=False)
    total = keep.astype(F32) + swap(send, mask).astype(F32)
    return total if last else total.astype(BF)


def reduce_scatter(x, order):
    left = list(order)
    for mask in order:
        x = reduce_step(x, mask, left, mask == order[-1])
        left.remove(mask)
    return x


def shards(
    passage_states,
    saved_preact,
    saved_resid,
    w_in,
    w_out,
    norm_gain,
    query_emb,
    score_grads,
    retrieved,
    placement_map,
    live_counts,
):
    n = lax.axis_size("psg")
    me = lax.axis_index("psg").astype(jnp.int32)
    core, chip = me % 2, me // 2
    half = n // 2
    tokens, width = saved_resid.shape
    rows = w_in.shape[0]
    slots = tokens // LEN
    queries = query_emb.shape[0]
    masks = [1 << b for b in range(1, n.bit_length() - 1)]
    gain = norm_gain.reshape(1, width)
    split = width // 2

    gather_orders = (masks[::-1], masks[:1] + masks[:0:-1])
    reduce_orders = (masks, masks[1::-1] + masks[2:])

    table = pack(
        slots, me.reshape(1), placement_map, live_counts, saved_resid, gain, query_emb, score_grads, retrieved
    )
    mask = 1
    while mask < n:
        table = jnp.concatenate([table, swap(table, mask)], axis=0)
        mask *= 2

    def gather_weight(w):
        parts = [
            gather(w[:, a:b], order)
            for (a, b), order in zip(((0, split), (split, width)), gather_orders)
        ]
        return jnp.concatenate(parts, axis=-1).reshape(half * rows, width)

    out_all = gather_weight(w_out)
    in_all = gather_weight(w_in)

    resid_nb = swap(saved_resid, 1)
    preact_nb = swap(pick_columns(saved_preact, chip, 1 - core, half, rows), 1)
    preact_own = pick_columns(saved_preact, chip, core, half, rows)
    states_nb = swap(passage_states, 1)
    act, slope = gelu(preact_own, preact_nb)

    resid_bf, resid_full, question_grad = resid_grads(slots, queries, saved_resid, resid_nb, table, gain)
    units = half * rows
    resid_bf = resid_bf.reshape(2 * tokens, width)

    def scatter(part):
        part = part.reshape([2] * len(masks) + [rows, width])
        done = [
            reduce_scatter(part[..., a:b], order)
            for (a, b), order in zip(((0, split), (split, width)), reduce_orders)
        ]
        return jnp.concatenate(done, axis=-1)

    grad_out = scatter(grad_out_part(act.reshape(2 * tokens, units), resid_bf))
    pre, in_part = grad_in_part(
        resid_bf, out_all, slope.reshape(2 * tokens, units), passage_states, states_nb
    )
    grad_in = scatter(in_part)
    pre = pre.reshape(2, tokens, units)
    back = swap(input_part(pre, in_all, 1, ()), 1)
    input_grad = input_part(pre, in_all, 0, (resid_full, back))
    return (input_grad, grad_in, grad_out, question_grad)


def solution(mesh):
    both = P(("groups", "psg"), None)
    return jax.shard_map(
        shards,
        mesh=mesh,
        in_specs=(both, both, both, P("psg", None), P("psg", None), P(), both, both, both, P("groups"), P("groups")),
        out_specs=(both, both, both, both),
        check_vma=False,
    )
```

time: 307 us -> 150 us (0.49)
  waiting for transfers between devices: 204 us -> 72.7 us
  blocking collectives: 41.7 us -> 0 us
  Pallas kernels: 0 us -> 29.6 us
  starting transfers between devices: 7.5 us -> 31.3 us
  matrix products: 20.7 us -> 0 us
  between operations: 13.9 us -> 1.15 us
  other arithmetic: 10 us -> 5.52 us
    reduce_scatter x1 -> x0, waiting for transfers between devices: 175 us -> none  [shards(): lax.psum_scatter(jnp.concatenate([in_rows, out_rows], axis=1), 'psg', sca...]
    ppermute x0 -> x32, waiting for transfers between devices: none -> 72.7 us  [swap(): return lax.ppermute(x, 'psg', [(i, i ^ mask) for i in range(n)])]
    all_gather x2 -> x0, blocking collectives: 41.7 us -> none  [the longest x1 22 us: shards(): all_queries = lax.all_gather(query_emb, 'psg', axis=0, tiled=True)]
    ppermute x0 -> x32, starting transfers between devices: none -> 31.3 us  [swap(): return lax.ppermute(x, 'psg', [(i, i ^ mask) for i in range(n)])]
    pallas_call x0 -> x9, Pallas kernels: none -> 29.6 us  [the longest x1 11.3 us: grad_in_part(): pl.pallas_call(grad_in_kernel, grid=(units // block,), in_specs=[pl.Block...]
    all_gather x2 -> x0, waiting for transfers between devices: 27 us -> none  [the longest x1 13.6 us: shards(): piece_in = lax.all_gather(w_in, 'psg', axis=0, tiled=True)]
    dot_general x6 -> x0, matrix products: 20.7 us -> none  [the longest x1 6.27 us: shards(): lax.dot_general(resid_bf, piece_out, (((1,), (1,)), ((), ())), preferred_...]
    all_to_all x1 -> x0, starting transfers between devices: 7.39 us -> none  [shards(): lax.all_to_all(local_pairs, 'psg', split_axis=1, concat_axis=0, tiled=True)]
  transfers between devices with their start and end apart: 4 -> 32, of which waited for: 3 -> 18; matrix products, arithmetic and copies ran while one was open for 11% -> 6% of each run, Pallas kernels for 0% -> 17%
where the time goes in v1:
time: 150 us
  waiting for transfers between devices  72.7 us (48%)
  starting transfers between devices  31.3 us (21%)
  Pallas kernels  29.6 us (20%)
  local copies, waits for them, and re-layouts  9.66 us (6%)
  other arithmetic  5.52 us (4%)
    ppermute x32, waiting for transfers between devices, swap(): return lax.ppermute(x, 'psg', [(i, i ^ mask) for i in range(n)])  72.7 us
    ppermute x32, starting transfers between devices, swap(): return lax.ppermute(x, 'psg', [(i, i ^ mask) for i in range(n)])  31.3 us
    pallas_call x1, Pallas kernels, grad_in_part(): pl.pallas_call(grad_in_kernel, grid=(units // block,), in_specs=[pl.Block...  11.3 us
    unnamed x32, local copies, waits for them, and re-layouts  6.06 us
    pallas_call x2, Pallas kernels, input_part(): pl.pallas_call(input_own_kernel if extra else input_nb_kernel, grid=(toke...  3.69 us
    pallas_call x1, Pallas kernels, gelu(): pl.pallas_call(gelu_kernel, grid=(units // block,), in_specs=[pl.BlockSpe...  3.6 us
    pallas_call x1, Pallas kernels, resid_grads(): pl.pallas_call(functools.partial(resid_kernel, slots, queries), grid=(slo...  3.36 us
    pallas_call x1, Pallas kernels, grad_out_part(): pl.pallas_call(grad_out_kernel, grid=(units // block,), in_specs=[pl.Bloc...  3.28 us
  transfers between devices with their start and end apart: 32, of which 18 were waited for; matrix products, arithmetic and copies ran while one was open for 6% of the time, Pallas kernels for 17%

profile of v1, /device:TPU:0, one launch (start us, length us, event | category | flops | bytes accessed | tf_op | source)
XLA Modules:
  0.0 149.9 jit_solution(8093284679073843848)
XLA Ops:
  0.7 1.4 copy-done.1
  2.0 0.7 copy-done.3
  2.7 0.7 copy-done.5
  3.4 0.7 copy-done.6
  4.1 0.7 copy-done.7
  4.7 0.7 copy-done.8
  5.4 0.7 copy-done.9
  6.0 1.8 %pack.1 = bf16[8,1024]{1,0:T(8,128)(2,1)S(1)} custom-call(s32[1]{0:T(128)} %bitcast.d_ref, s32[64]{0:T(128)S(1)} %copy-done.7, s32[16]{0:T(128)S(1)} %copy-done.8, bf16[512,1024]{1,0:T(8,128)(2,1)S(1)} %copy-done.1, f32[1,1024]{1,0:T(1,128)S(1)} %bitcast.150, bf16[2,1024]{1,0:T(2,128)(2,1)S(1)} %copy-done.5, bf16[2,32]{1,0:T(2,128)(2,1)S(1)} %copy-done.9, ...), custom_call_target="tpu_custom_call" | custom-call | flops 1000000 | bytes 3000000 | tf_op jit(solution)/shard_map/pack/pallas_call | solution.py:67
  7.8 0.5 collective-permute-start.1
  8.3 1.7 %slice_bitcast_fusion.19 = (bf16[1,128,512]{2,1,0:T(8,128)(2,1)S(1)}, bf16[1,128,512]{2,1,0:T(8,128)(2,1)S(1)}, bf16[128,512]{1,0:T(8,128)(2,1)}, bf16[128,512]{1,0:T(8,128)(2,1)}) fusion(bf16[128,1024]{1,0:T(8,128)(2,1)} %param.15), kind=kLoop, calls=%fused_computation.69 | loop fusion | bytes 786432 | tf_op jit(solution)/shard_map/stack | solution.py:308
  10.0 2.5 %collective-permute-start.8 = (bf16[128,512]{1,0:T(8,128)(2,1)}, bf16[128,512]{1,0:T(8,128)(2,1)}, u32[]{:S(2)}, u32[]{:S(2)}) collective-permute-start(bf16[128,512]{1,0:T(8,128)(2,1)} %get-tuple-element.46), channel_id=1, source_target_pairs={{0,2},{1,3},{2,0},{3,1},{4,6},{5,7},{6,4},{7,5},{8,10},{9,11},{10,... | collective-permute-start | bytes 393224 | tf_op jit(solution)/shard_map/ppermute | solution.py:26
  12.6 2.6 %collective-permute-start.5 = (bf16[128,512]{1,0:T(8,128)(2,1)}, bf16[128,512]{1,0:T(8,128)(2,1)}, u32[]{:S(2)}, u32[]{:S(2)}) collective-permute-start(bf16[128,512]{1,0:T(8,128)(2,1)} %get-tuple-element.47), channel_id=1, source_target_pairs={{0,8},{1,9},{2,10},{3,11},{4,12},{5,13},{6,14},{7,15},{8,0},{9,1},... | collective-permute-start | bytes 393224 | tf_op jit(solution)/shard_map/ppermute | solution.py:26
  15.2 1.0 slice_bitcast_fusion.17
  16.2 0.4 collective-permute-start.13
  16.9 1.8 %collective-permute-start.2 = (bf16[16,1024]{1,0:T(8,128)(2,1)S(1)}, bf16[16,1024]{1,0:T(8,128)(2,1)S(1)}, u32[]{:S(2)}, u32[]{:S(2)}) collective-permute-start(bf16[16,1024]{1,0:T(8,128)(2,1)S(1)} %pad_maximum_fusion.12), channel_id=1, source_target_pairs={{0,2},{1,3},{2,0},{3,1},{4,6},{5,7},{6,4},{7,5},{8,10},{9,11},{10,... | collective-permute-start | bytes 98312 | tf_op jit(solution)/shard_map/ppermute | solution.py:26
  18.8 1.3 pick_columns.3
  20.1 1.3 pick_columns.2.own_ref
  21.5 0.9 collective-permute-done.2
  22.4 1.6 %collective-permute-start.3 = (bf16[32,1024]{1,0:T(8,128)(2,1)S(1)}, bf16[32,1024]{1,0:T(8,128)(2,1)S(1)}, u32[]{:S(2)}, u32[]{:S(2)}) collective-permute-start(bf16[32,1024]{1,0:T(8,128)(2,1)S(1)} %pad_maximum_fusion.11), channel_id=1, source_target_pairs={{0,4},{1,5},{2,6},{3,7},{4,0},{5,1},{6,2},{7,3},{8,12},{9,13},{10,... | collective-permute-start | bytes 196616 | tf_op jit(solution)/shard_map/ppermute | solution.py:26
  23.9 0.9 fusion.10
  24.9 2.6 %collective-permute-start.9 = (bf16[2,128,512]{2,1,0:T(8,128)(2,1)S(1)}, bf16[2,128,512]{2,1,0:T(8,128)(2,1)S(1)}, u32[]{:S(2)}, u32[]{:S(2)}) collective-permute-start(bf16[2,128,512]{2,1,0:T(8,128)(2,1)S(1)} %get-tuple-element.49), channel_id=1, source_target_pairs={{0,8},{1,9},{2,10},{3,11},{4,12},{5,13},{6,14},{7,15},{8,0},{9,1},... | collective-permute-start | bytes 786440 | tf_op jit(solution)/shard_map/ppermute | solution.py:26
  27.5 0.9 fusion.11
  28.5 0.5 collective-permute-start.6
  29.0 4.2 %collective-permute-done.13 = bf16[128,512]{1,0:T(8,128)(2,1)S(1)} collective-permute-done((bf16[128,512]{1,0:T(8,128)(2,1)S(1)}, bf16[128,512]{1,0:T(8,128)(2,1)S(1)}, u32[]{:S(2)}, u32[]{:S(2)}) %collective-permute-start.13) | collective-permute-done | bytes 131104 | tf_op jit(solution)/shard_map/ppermute | solution.py:26
  33.4 2.7 %collective-permute-start.17 = (bf16[2,128,512]{2,1,0:T(8,128)(2,1)S(1)}, bf16[2,128,512]{2,1,0:T(8,128)(2,1)S(1)}, u32[]{:S(2)}, u32[]{:S(2)}) collective-permute-start(bf16[2,128,512]{2,1,0:T(8,128)(2,1)S(1)} %get-tuple-element.41), channel_id=1, source_target_pairs={{0,8},{1,9},{2,10},{3,11},{4,12},{5,13},{6,14},{7,15},{8,0},{9,1},... | collective-permute-start | bytes 786440 | tf_op jit(solution)/shard_map/ppermute | solution.py:26
  36.1 3.7 %collective-permute-done.9 = bf16[2,128,512]{2,1,0:T(8,128)(2,1)S(1)} collective-permute-done((bf16[2,128,512]{2,1,0:T(8,128)(2,1)S(1)}, bf16[2,128,512]{2,1,0:T(8,128)(2,1)S(1)}, u32[]{:S(2)}, u32[]{:S(2)}) %collective-permute-start.9) | collective-permute-done | bytes 262176 | tf_op jit(solution)/shard_map/ppermute | solution.py:26
  40.1 8.8 %collective-permute-done.6 = bf16[2,128,512]{2,1,0:T(8,128)(2,1)S(1)} collective-permute-done((bf16[2,128,512]{2,1,0:T(8,128)(2,1)S(1)}, bf16[2,128,512]{2,1,0:T(8,128)(2,1)S(1)}, u32[]{:S(2)}, u32[]{:S(2)}) %collective-permute-start.6) | collective-permute-done | bytes 262176 | tf_op jit(solution)/shard_map/ppermute | solution.py:26
  49.0 6.9 %collective-permute-done.14 = bf16[2,128,512]{2,1,0:T(8,128)(2,1)S(1)} collective-permute-done((bf16[2,128,512]{2,1,0:T(8,128)(2,1)S(1)}, bf16[2,128,512]{2,1,0:T(8,128)(2,1)S(1)}, u32[]{:S(2)}, u32[]{:S(2)}) %collective-permute-start.14) | collective-permute-done | bytes 262176 | tf_op jit(solution)/shard_map/ppermute | solution.py:26
  55.9 0.3 collective-permute-start.7
  56.3 6.6 %collective-permute-done.4 = bf16[64,1024]{1,0:T(8,128)(2,1)S(1)} collective-permute-done((bf16[64,1024]{1,0:T(8,128)(2,1)S(1)}, bf16[64,1024]{1,0:T(8,128)(2,1)S(1)}, u32[]{:S(2)}, u32[]{:S(2)}) %collective-permute-start.4) | collective-permute-done | bytes 131104 | tf_op jit(solution)/shard_map/ppermute | solution.py:26
  63.0 0.4 collective-permute-start.15
  63.4 2.7 %collective-permute-done.10 = bf16[2,2,128,512]{3,2,1,0:T(8,128)(2,1)S(1)} collective-permute-done((bf16[2,2,128,512]{3,2,1,0:T(8,128)(2,1)S(1)}, bf16[2,2,128,512]{3,2,1,0:T(8,128)(2,1)S(1)}, u32[]{:S(2)}, u32[]{:S(2)}) %collective-permute-start.10) | collective-permute-done | bytes 524320 | tf_op jit(solution)/shard_map/ppermute | solution.py:26
  66.1 2.6 %collective-permute-done.7 = bf16[2,2,128,512]{3,2,0,1:T(8,128)(2,1)S(1)} collective-permute-done((bf16[2,2,128,512]{3,2,0,1:T(8,128)(2,1)S(1)}, bf16[2,2,128,512]{3,2,0,1:T(8,128)(2,1)S(1)}, u32[]{:S(2)}, u32[]{:S(2)}) %collective-permute-start.7) | collective-permute-done | bytes 524320 | tf_op jit(solution)/shard_map/ppermute | solution.py:26
  68.7 0.3 maximum_maximum_fusion
  69.2 8.0 %collective-permute-done.15 = bf16[2,2,128,512]{3,2,0,1:T(8,128)(2,1)S(1)} collective-permute-done((bf16[2,2,128,512]{3,2,0,1:T(8,128)(2,1)S(1)}, bf16[2,2,128,512]{3,2,0,1:T(8,128)(2,1)S(1)}, u32[]{:S(2)}, u32[]{:S(2)}) %collective-permute-start.15) | collective-permute-done | bytes 524320 | tf_op jit(solution)/shard_map/ppermute | solution.py:26
  77.2 0.3 collective-permute-done.18
  77.5 0.3 maximum_maximum_fusion.1
  77.9 0.5 copy-done.4
  78.4 3.4 %resid_grads.1 = (bf16[2,512,1024]{2,1,0:T(8,128)(2,1)S(1)}, f32[512,1024]{1,0:T(8,128)S(1)}, f32[2,1024]{1,0:T(2,128)}) custom-call(bf16[512,1024]{1,0:T(8,128)(2,1)S(1)} %copy-done.2, bf16[512,1024]{1,0:T(8,128)(2,1)S(1)} %collective-permute-done.nb_ref, bf16[128,1024]{1,0:T(8,128)(2,1)S(1)} %constant_dynamic-update-slice_fusion.all_ref, ...), custom_call_target="tpu_custom_call" | custom-call | flops 20000000 | bytes 8000000 | tf_op jit(solution)/shard_map/resid_grads/pallas_call | solution.py:128
  81.8 3.6 %gelu.1 = (bf16[2,512,1024]{2,1,0:T(8,128)(2,1)S(1)}, f32[2,512,1024]{2,1,0:T(8,128)S(1)}) custom-call(bf16[512,1024]{1,0:T(8,128)(2,1)S(1)} %pick_columns.2.own_ref, bf16[512,1024]{1,0:T(8,128)(2,1)S(1)} %collective-permute-done.11.nb_ref), custom_call_target="tpu_custom_call" | custom-call | flops 60000000 | bytes 8000000 | tf_op jit(solution)/shard_map/gelu/pallas_call | solution.py:192
  85.4 3.3 %grad_out.1 = bf16[1024,1024]{1,0:T(8,128)(2,1)S(1)} custom-call(bf16[1024,1024]{1,0:T(8,128)(2,1)S(1)} %bitcast.155, bf16[1024,1024]{1,0:T(8,128)(2,1)S(1)} %bitcast.153), custom_call_target="tpu_custom_call" | custom-call | flops 2147483648 | bytes 6000000 | tf_op jit(solution)/shard_map/grad_out/pallas_call | solution.py:217
  88.9 0.3 collective-permute-start.26
  89.3 2.5 %collective-permute-start.29 = (bf16[2,2,128,512]{3,2,0,1:T(8,128)(2,1)S(1)}, bf16[2,2,128,512]{3,2,0,1:T(8,128)(2,1)S(1)}, u32[]{:S(2)}, u32[]{:S(2)}) collective-permute-start(bf16[2,2,128,512]{3,2,0,1:T(8,128)(2,1)S(1)} %bitcast.156), channel_id=1, source_target_pairs={{0,4},{1,5},{2,6},{3,7},{4,0},{5,1},{6,2},{7,3},{8,12},{9,13},{10,... | collective-permute-start | bytes 1572872 | tf_op jit(solution)/shard_map/ppermute | solution.py:26
  91.8 11.3 %grad_in.1 = (bf16[1024,1024]{1,0:T(8,128)(2,1)S(1)}, bf16[1024,1024]{1,0:T(8,128)(2,1)S(1)}) custom-call(bf16[1024,1024]{1,0:T(8,128)(2,1)S(1)} %bitcast.154, bf16[1024,1024]{1,0:T(8,128)(2,1)S(1)} %bitcast.145, f32[1024,1024]{1,0:T(8,128)} %bitcast.152, bf16[512,1024]{1,0:T(8,128)(2,1)S(1)} %copy-done.11, bf16[512,1024]{1,0:T(8,128)(2,1)S(1)} %collective-permute-done.12.nb_ref), custom_call_target="tpu_custom_call" | custom-call | flops 4294967296 | bytes 14000000 | tf_op jit(solution)/shard_map/grad_in/pallas_call | solution.py:250
  103.3 1.6 %collective-permute-start.20 = (bf16[2,2,128,512]{3,2,0,1:T(8,128)(2,1)S(1)}, bf16[2,2,128,512]{3,2,0,1:T(8,128)(2,1)S(1)}, u32[]{:S(2)}, u32[]{:S(2)}) collective-permute-start(bf16[2,2,128,512]{3,2,0,1:T(8,128)(2,1)S(1)} %bitcast.159), channel_id=1, source_target_pairs={{0,2},{1,3},{2,0},{3,1},{4,6},{5,7},{6,4},{7,5},{8,10},{9,11},{10,... | collective-permute-start | bytes 1572872 | tf_op jit(solution)/shard_map/ppermute | solution.py:26
  105.1 1.4 input_nb.1
  106.8 2.1 %collective-permute-start.27 = (bf16[2,128,512]{2,1,0:T(8,128)(2,1)S(1)}, bf16[2,128,512]{2,1,0:T(8,128)(2,1)S(1)}, u32[]{:S(2)}, u32[]{:S(2)}) collective-permute-start(bf16[2,128,512]{2,1,0:T(8,128)(2,1)S(1)} %slice_bitcast_fusion.2), channel_id=1, source_target_pairs={{0,4},{1,5},{2,6},{3,7},{4,0},{5,1},{6,2},{7,3},{8,12},{9,13},{10,... | collective-permute-start | bytes 786440 | tf_op jit(solution)/shard_map/ppermute | solution.py:26
  109.0 0.6 collective-permute-start.30
  109.6 7.1 %collective-permute-done.20 = bf16[2,2,128,512]{3,2,0,1:T(8,128)(2,1)S(1)} collective-permute-done((bf16[2,2,128,512]{3,2,0,1:T(8,128)(2,1)S(1)}, bf16[2,2,128,512]{3,2,0,1:T(8,128)(2,1)S(1)}, u32[]{:S(2)}, u32[]{:S(2)}) %collective-permute-start.20) | collective-permute-done | bytes 524320 | tf_op jit(solution)/shard_map/ppermute | solution.py:26
  116.9 0.4 collective-permute-start.21
  117.3 2.6 %collective-permute-done.23 = bf16[2,2,128,512]{3,2,0,1:T(8,128)(2,1)S(1)} collective-permute-done((bf16[2,2,128,512]{3,2,0,1:T(8,128)(2,1)S(1)}, bf16[2,2,128,512]{3,2,0,1:T(8,128)(2,1)S(1)}, u32[]{:S(2)}, u32[]{:S(2)}) %collective-permute-start.23) | collective-permute-done | bytes 524320 | tf_op jit(solution)/shard_map/ppermute | solution.py:26
  120.1 0.6 collective-permute-start.24
  120.7 6.0 %collective-permute-done.27 = bf16[2,128,512]{2,1,0:T(8,128)(2,1)S(1)} collective-permute-done((bf16[2,128,512]{2,1,0:T(8,128)(2,1)S(1)}, bf16[2,128,512]{2,1,0:T(8,128)(2,1)S(1)}, u32[]{:S(2)}, u32[]{:S(2)}) %collective-permute-start.27) | collective-permute-done | bytes 262176 | tf_op jit(solution)/shard_map/ppermute | solution.py:26
  126.7 2.1 %collective-permute-start.28 = (bf16[128,512]{1,0:T(8,128)(2,1)S(1)}, bf16[128,512]{1,0:T(8,128)(2,1)S(1)}, u32[]{:S(2)}, u32[]{:S(2)}) collective-permute-start(bf16[128,512]{1,0:T(8,128)(2,1)S(1)} %slice_bitcast_fusion.10), channel_id=1, source_target_pairs={{0,8},{1,9},{2,10},{3,11},{4,12},{5,13},{6,14},{7,15},{8,0},{9,1},... | collective-permute-start | bytes 393224 | tf_op jit(solution)/shard_map/ppermute | solution.py:26
  128.9 1.0 collective-permute-start.31
  129.9 0.8 collective-permute-done.21
  130.7 3.6 %collective-permute-start.22 = (bf16[128,512]{1,0:T(8,128)(2,1)S(1)}, bf16[128,512]{1,0:T(8,128)(2,1)S(1)}, u32[]{:S(2)}, u32[]{:S(2)}) collective-permute-start(bf16[128,512]{1,0:T(8,128)(2,1)S(1)} %slice_bitcast_fusion.14), channel_id=1, source_target_pairs={{0,8},{1,9},{2,10},{3,11},{4,12},{5,13},{6,14},{7,15},{8,0},{9,1},... | collective-permute-start | bytes 393224 | tf_op jit(solution)/shard_map/ppermute | solution.py:26
  134.6 8.0 %collective-permute-done.28 = bf16[128,512]{1,0:T(8,128)(2,1)S(1)} collective-permute-done((bf16[128,512]{1,0:T(8,128)(2,1)S(1)}, bf16[128,512]{1,0:T(8,128)(2,1)S(1)}, u32[]{:S(2)}, u32[]{:S(2)}) %collective-permute-start.28) | collective-permute-done | bytes 131104 | tf_op jit(solution)/shard_map/ppermute | solution.py:26
  142.7 1.4 collective-permute-done.31
  144.1 1.4 collective-permute-done.22
  145.5 0.8 pad_maximum_fusion.5
  146.3 0.5 collective-permute-done.25
  146.9 0.8 pad_maximum_fusion.4
  147.7 2.2 %input_own.1 = bf16[512,1024]{1,0:T(8,128)(2,1)} custom-call(bf16[2,512,1024]{2,1,0:T(8,128)(2,1)S(1)} %bitcast.144, bf16[1024,1024]{1,0:T(8,128)(2,1)S(1)} %bitcast.142, f32[512,1024]{1,0:T(8,128)S(1)} %get-tuple-element.14.resid_ref, bf16[512,1024]{1,0:T(8,128)(2,1)S(1)} %collective-permute-done.19.nb_ref), custom_call_target="tpu_custom_call" | custom-call | flops 1073741824 | bytes 5000000 | tf_op jit(solution)/shard_map/input_own/pallas_call | solution.py:288
  (87 shorter events, 3.3 us)
Async XLA Ops:
  0.6 18.2 %copy-start = (bf16[512,2048]{1,0:T(8,128)(2,1)S(1)}, bf16[512,2048]{1,0:T(8,128)(2,1)}, u32[]{:S(2)}) copy-start(bf16[512,2048]{1,0:T(8,128)(2,1)} %in_ref.3) | copy-start | bytes 6291460
  0.6 1.4 copy-start.1
  2.0 0.7 copy-start.3
  2.7 0.7 copy-start.5
  3.4 0.7 copy-start.6
  4.1 0.7 copy-start.7
  4.7 0.7 copy-start.8
  5.4 0.7 copy-start.9
  7.8 9.1 %collective-permute-start.1 = (bf16[8,1024]{1,0:T(8,128)(2,1)S(1)}, bf16[8,1024]{1,0:T(8,128)(2,1)S(1)}, u32[]{:S(2)}, u32[]{:S(2)}) collective-permute-start(bf16[8,1024]{1,0:T(8,128)(2,1)S(1)} %pack.1), channel_id=1, source_target_pairs={{0,1},{1,0},{2,3},{3,2},{4,5},{5,4},{6,7},{7,6},{8,9},{9,8},{10,11... | collective-permute-start | bytes 49160 | tf_op jit(solution)/shard_map/ppermute | solution.py:26
  10.0 13.9 %collective-permute-start.8 = (bf16[128,512]{1,0:T(8,128)(2,1)}, bf16[128,512]{1,0:T(8,128)(2,1)}, u32[]{:S(2)}, u32[]{:S(2)}) collective-permute-start(bf16[128,512]{1,0:T(8,128)(2,1)} %get-tuple-element.46), channel_id=1, source_target_pairs={{0,2},{1,3},{2,0},{3,1},{4,6},{5,7},{6,4},{7,5},{8,10},{9,11},{10,... | collective-permute-start | bytes 393224 | tf_op jit(solution)/shard_map/ppermute | solution.py:26
  12.6 15.0 %collective-permute-start.5 = (bf16[128,512]{1,0:T(8,128)(2,1)}, bf16[128,512]{1,0:T(8,128)(2,1)}, u32[]{:S(2)}, u32[]{:S(2)}) collective-permute-start(bf16[128,512]{1,0:T(8,128)(2,1)} %get-tuple-element.47), channel_id=1, source_target_pairs={{0,8},{1,9},{2,10},{3,11},{4,12},{5,13},{6,14},{7,15},{8,0},{9,1},... | collective-permute-start | bytes 393224 | tf_op jit(solution)/shard_map/ppermute | solution.py:26
  16.2 17.1 %collective-permute-start.13 = (bf16[128,512]{1,0:T(8,128)(2,1)S(1)}, bf16[128,512]{1,0:T(8,128)(2,1)S(1)}, u32[]{:S(2)}, u32[]{:S(2)}) collective-permute-start(bf16[128,512]{1,0:T(8,128)(2,1)S(1)} %get-tuple-element.39), channel_id=1, source_target_pairs={{0,8},{1,9},{2,10},{3,11},{4,12},{5,13},{6,14},{7,15},{8,0},{9,1},... | collective-permute-start | bytes 393224 | tf_op jit(solution)/shard_map/ppermute | solution.py:26
  16.6 16.8 %collective-permute-start.16 = (bf16[128,512]{1,0:T(8,128)(2,1)S(1)}, bf16[128,512]{1,0:T(8,128)(2,1)S(1)}, u32[]{:S(2)}, u32[]{:S(2)}) collective-permute-start(bf16[128,512]{1,0:T(8,128)(2,1)S(1)} %get-tuple-element.38), channel_id=1, source_target_pairs={{0,2},{1,3},{2,0},{3,1},{4,6},{5,7},{6,4},{7,5},{8,10},{9,11},{10,... | collective-permute-start | bytes 393224 | tf_op jit(solution)/shard_map/ppermute | solution.py:26
  16.9 5.4 %collective-permute-start.2 = (bf16[16,1024]{1,0:T(8,128)(2,1)S(1)}, bf16[16,1024]{1,0:T(8,128)(2,1)S(1)}, u32[]{:S(2)}, u32[]{:S(2)}) collective-permute-start(bf16[16,1024]{1,0:T(8,128)(2,1)S(1)} %pad_maximum_fusion.12), channel_id=1, source_target_pairs={{0,2},{1,3},{2,0},{3,1},{4,6},{5,7},{6,4},{7,5},{8,10},{9,11},{10,... | collective-permute-start | bytes 98312 | tf_op jit(solution)/shard_map/ppermute | solution.py:26
  22.4 17.6 %collective-permute-start.3 = (bf16[32,1024]{1,0:T(8,128)(2,1)S(1)}, bf16[32,1024]{1,0:T(8,128)(2,1)S(1)}, u32[]{:S(2)}, u32[]{:S(2)}) collective-permute-start(bf16[32,1024]{1,0:T(8,128)(2,1)S(1)} %pad_maximum_fusion.11), channel_id=1, source_target_pairs={{0,4},{1,5},{2,6},{3,7},{4,0},{5,1},{6,2},{7,3},{8,12},{9,13},{10,... | collective-permute-start | bytes 196616 | tf_op jit(solution)/shard_map/ppermute | solution.py:26
  24.9 15.1 %copy-start.2 = (bf16[512,1024]{1,0:T(8,128)(2,1)S(1)}, bf16[512,1024]{1,0:T(8,128)(2,1)}, u32[]{:S(2)}) copy-start(bf16[512,1024]{1,0:T(8,128)(2,1)} %own_ref.2) | copy-start | bytes 3145732
  24.9 14.9 %collective-permute-start.9 = (bf16[2,128,512]{2,1,0:T(8,128)(2,1)S(1)}, bf16[2,128,512]{2,1,0:T(8,128)(2,1)S(1)}, u32[]{:S(2)}, u32[]{:S(2)}) collective-permute-start(bf16[2,128,512]{2,1,0:T(8,128)(2,1)S(1)} %get-tuple-element.49), channel_id=1, source_target_pairs={{0,8},{1,9},{2,10},{3,11},{4,12},{5,13},{6,14},{7,15},{8,0},{9,1},... | collective-permute-start | bytes 786440 | tf_op jit(solution)/shard_map/ppermute | solution.py:26
  28.5 20.4 %collective-permute-start.6 = (bf16[2,128,512]{2,1,0:T(8,128)(2,1)S(1)}, bf16[2,128,512]{2,1,0:T(8,128)(2,1)S(1)}, u32[]{:S(2)}, u32[]{:S(2)}) collective-permute-start(bf16[2,128,512]{2,1,0:T(8,128)(2,1)S(1)} %get-tuple-element.43), channel_id=1, source_target_pairs={{0,4},{1,5},{2,6},{3,7},{4,0},{5,1},{6,2},{7,3},{8,12},{9,13},{10,... | collective-permute-start | bytes 786440 | tf_op jit(solution)/shard_map/ppermute | solution.py:26
  33.3 22.6 %collective-permute-start.14 = (bf16[2,128,512]{2,1,0:T(8,128)(2,1)S(1)}, bf16[2,128,512]{2,1,0:T(8,128)(2,1)S(1)}, u32[]{:S(2)}, u32[]{:S(2)}) collective-permute-start(bf16[2,128,512]{2,1,0:T(8,128)(2,1)S(1)} %get-tuple-element.35), channel_id=1, source_target_pairs={{0,4},{1,5},{2,6},{3,7},{4,0},{5,1},{6,2},{7,3},{8,12},{9,13},{10,... | collective-permute-start | bytes 786440 | tf_op jit(solution)/shard_map/ppermute | solution.py:26
  33.4 22.5 %collective-permute-start.17 = (bf16[2,128,512]{2,1,0:T(8,128)(2,1)S(1)}, bf16[2,128,512]{2,1,0:T(8,128)(2,1)S(1)}, u32[]{:S(2)}, u32[]{:S(2)}) collective-permute-start(bf16[2,128,512]{2,1,0:T(8,128)(2,1)S(1)} %get-tuple-element.41), channel_id=1, source_target_pairs={{0,8},{1,9},{2,10},{3,11},{4,12},{5,13},{6,14},{7,15},{8,0},{9,1},... | collective-permute-start | bytes 786440 | tf_op jit(solution)/shard_map/ppermute | solution.py:26
  39.9 26.1 %collective-permute-start.10 = (bf16[2,2,128,512]{3,2,1,0:T(8,128)(2,1)S(1)}, bf16[2,2,128,512]{3,2,1,0:T(8,128)(2,1)S(1)}, u32[]{:S(2)}, u32[]{:S(2)}) collective-permute-start(bf16[2,2,128,512]{3,2,1,0:T(8,128)(2,1)S(1)} %get-tuple-element.33), channel_id=1, source_target_pairs={{0,4},{1,5},{2,6},{3,7},{4,0},{5,1},{6,2},{7,3},{8,12},{9,13},{10,... | collective-permute-start | bytes 1572872 | tf_op jit(solution)/shard_map/ppermute | solution.py:26
  40.0 37.9 %collective-permute-start = (bf16[512,1024]{1,0:T(8,128)(2,1)S(1)}, bf16[512,1024]{1,0:T(8,128)(2,1)S(1)}, u32[]{:S(2)}, u32[]{:S(2)}) collective-permute-start(bf16[512,1024]{1,0:T(8,128)(2,1)S(1)} %copy-done.2), channel_id=1, source_target_pairs={{0,1},{1,0},{2,3},{3,2},{4,5},{5,4},{6,7},{7,6},{8,9},{9,8},{10,11... | collective-permute-start | bytes 3145736 | tf_op jit(solution)/shard_map/ppermute | solution.py:26
  48.9 32.9 %collective-permute-start.11 = (bf16[512,1024]{1,0:T(8,128)(2,1)S(1)}, bf16[512,1024]{1,0:T(8,128)(2,1)S(1)}, u32[]{:S(2)}, u32[]{:S(2)}) collective-permute-start(bf16[512,1024]{1,0:T(8,128)(2,1)S(1)} %pick_columns.3), channel_id=1, source_target_pairs={{0,1},{1,0},{2,3},{3,2},{4,5},{5,4},{6,7},{7,6},{8,9},{9,8},{10,11... | collective-permute-start | bytes 3145736 | tf_op jit(solution)/shard_map/ppermute | solution.py:26
  48.9 19.8 %copy-start.11 = (bf16[512,1024]{1,0:T(8,128)(2,1)S(1)}, bf16[512,1024]{1,0:T(8,128)(2,1)}, u32[]{:S(2)}) copy-start(bf16[512,1024]{1,0:T(8,128)(2,1)} %own_ref.3) | copy-start | bytes 3145732
  55.9 7.1 %collective-permute-start.4 = (bf16[64,1024]{1,0:T(8,128)(2,1)S(1)}, bf16[64,1024]{1,0:T(8,128)(2,1)S(1)}, u32[]{:S(2)}, u32[]{:S(2)}) collective-permute-start(bf16[64,1024]{1,0:T(8,128)(2,1)S(1)} %pad_maximum_fusion.10), channel_id=1, source_target_pairs={{0,8},{1,9},{2,10},{3,11},{4,12},{5,13},{6,14},{7,15},{8,0},{9,1},... | collective-permute-start | bytes 393224 | tf_op jit(solution)/shard_map/ppermute | solution.py:26
  55.9 12.8 %collective-permute-start.7 = (bf16[2,2,128,512]{3,2,0,1:T(8,128)(2,1)S(1)}, bf16[2,2,128,512]{3,2,0,1:T(8,128)(2,1)S(1)}, u32[]{:S(2)}, u32[]{:S(2)}) collective-permute-start(bf16[2,2,128,512]{3,2,0,1:T(8,128)(2,1)S(1)} %get-tuple-element.31), channel_id=1, source_target_pairs={{0,2},{1,3},{2,0},{3,1},{4,6},{5,7},{6,4},{7,5},{8,10},{9,11},{10,... | collective-permute-start | bytes 1572872 | tf_op jit(solution)/shard_map/ppermute | solution.py:26
  63.0 14.2 %collective-permute-start.15 = (bf16[2,2,128,512]{3,2,0,1:T(8,128)(2,1)S(1)}, bf16[2,2,128,512]{3,2,0,1:T(8,128)(2,1)S(1)}, u32[]{:S(2)}, u32[]{:S(2)}) collective-permute-start(bf16[2,2,128,512]{3,2,0,1:T(8,128)(2,1)S(1)} %get-tuple-element.27), channel_id=1, source_target_pairs={{0,2},{1,3},{2,0},{3,1},{4,6},{5,7},{6,4},{7,5},{8,10},{9,11},{10,... | collective-permute-start | bytes 1572872 | tf_op jit(solution)/shard_map/ppermute | solution.py:26
  66.0 11.4 %collective-permute-start.18 = (bf16[2,2,128,512]{3,2,1,0:T(8,128)(2,1)S(1)}, bf16[2,2,128,512]{3,2,1,0:T(8,128)(2,1)S(1)}, u32[]{:S(2)}, u32[]{:S(2)}) collective-permute-start(bf16[2,2,128,512]{3,2,1,0:T(8,128)(2,1)S(1)} %get-tuple-element.29), channel_id=1, source_target_pairs={{0,4},{1,5},{2,6},{3,7},{4,0},{5,1},{6,2},{7,3},{8,12},{9,13},{10,... | collective-permute-start | bytes 1572872 | tf_op jit(solution)/shard_map/ppermute | solution.py:26
  68.7 23.1 %collective-permute-start.12 = (bf16[512,1024]{1,0:T(8,128)(2,1)S(1)}, bf16[512,1024]{1,0:T(8,128)(2,1)S(1)}, u32[]{:S(2)}, u32[]{:S(2)}) collective-permute-start(bf16[512,1024]{1,0:T(8,128)(2,1)S(1)} %copy-done.11), channel_id=1, source_target_pairs={{0,1},{1,0},{2,3},{3,2},{4,5},{5,4},{6,7},{7,6},{8,9},{9,8},{10,11... | collective-permute-start | bytes 3145736 | tf_op jit(solution)/shard_map/ppermute | solution.py:26
  77.7 0.7 copy-start.4
  85.4 3.3 %copy-start.10 = (f32[2,512,1024]{2,1,0:T(8,128)}, f32[2,512,1024]{2,1,0:T(8,128)S(1)}, u32[]{:S(2)}) copy-start(f32[2,512,1024]{2,1,0:T(8,128)S(1)} %get-tuple-element.12) | copy-start | bytes 12582916
  88.9 17.8 %collective-permute-start.26 = (bf16[2,2,128,512]{3,2,0,1:T(8,128)(2,1)S(1)}, bf16[2,2,128,512]{3,2,0,1:T(8,128)(2,1)S(1)}, u32[]{:S(2)}, u32[]{:S(2)}) collective-permute-start(bf16[2,2,128,512]{3,2,0,1:T(8,128)(2,1)S(1)} %bitcast.157), channel_id=1, source_target_pairs={{0,2},{1,3},{2,0},{3,1},{4,6},{5,7},{6,4},{7,5},{8,10},{9,11},{10,... | collective-permute-start | bytes 1572872 | tf_op jit(solution)/shard_map/ppermute | solution.py:26
  89.3 19.6 %collective-permute-start.29 = (bf16[2,2,128,512]{3,2,0,1:T(8,128)(2,1)S(1)}, bf16[2,2,128,512]{3,2,0,1:T(8,128)(2,1)S(1)}, u32[]{:S(2)}, u32[]{:S(2)}) collective-permute-start(bf16[2,2,128,512]{3,2,0,1:T(8,128)(2,1)S(1)} %bitcast.156), channel_id=1, source_target_pairs={{0,4},{1,5},{2,6},{3,7},{4,0},{5,1},{6,2},{7,3},{8,12},{9,13},{10,... | collective-permute-start | bytes 1572872 | tf_op jit(solution)/shard_map/ppermute | solution.py:26
  103.3 13.5 %collective-permute-start.20 = (bf16[2,2,128,512]{3,2,0,1:T(8,128)(2,1)S(1)}, bf16[2,2,128,512]{3,2,0,1:T(8,128)(2,1)S(1)}, u32[]{:S(2)}, u32[]{:S(2)}) collective-permute-start(bf16[2,2,128,512]{3,2,0,1:T(8,128)(2,1)S(1)} %bitcast.159), channel_id=1, source_target_pairs={{0,2},{1,3},{2,0},{3,1},{4,6},{5,7},{6,4},{7,5},{8,10},{9,11},{10,... | collective-permute-start | bytes 1572872 | tf_op jit(solution)/shard_map/ppermute | solution.py:26
  105.0 14.9 %collective-permute-start.23 = (bf16[2,2,128,512]{3,2,0,1:T(8,128)(2,1)S(1)}, bf16[2,2,128,512]{3,2,0,1:T(8,128)(2,1)S(1)}, u32[]{:S(2)}, u32[]{:S(2)}) collective-permute-start(bf16[2,2,128,512]{3,2,0,1:T(8,128)(2,1)S(1)} %bitcast.158), channel_id=1, source_target_pairs={{0,4},{1,5},{2,6},{3,7},{4,0},{5,1},{6,2},{7,3},{8,12},{9,13},{10,... | collective-permute-start | bytes 1572872 | tf_op jit(solution)/shard_map/ppermute | solution.py:26
  106.6 41.1 %collective-permute-start.19 = (bf16[512,1024]{1,0:T(8,128)(2,1)S(1)}, bf16[512,1024]{1,0:T(8,128)(2,1)S(1)}, u32[]{:S(2)}, u32[]{:S(2)}) collective-permute-start(bf16[512,1024]{1,0:T(8,128)(2,1)S(1)} %input_nb.1), channel_id=1, source_target_pairs={{0,1},{1,0},{2,3},{3,2},{4,5},{5,4},{6,7},{7,6},{8,9},{9,8},{10,11... | collective-permute-start | bytes 3145736 | tf_op jit(solution)/shard_map/ppermute | solution.py:26
  106.8 19.8 %collective-permute-start.27 = (bf16[2,128,512]{2,1,0:T(8,128)(2,1)S(1)}, bf16[2,128,512]{2,1,0:T(8,128)(2,1)S(1)}, u32[]{:S(2)}, u32[]{:S(2)}) collective-permute-start(bf16[2,128,512]{2,1,0:T(8,128)(2,1)S(1)} %slice_bitcast_fusion.2), channel_id=1, source_target_pairs={{0,4},{1,5},{2,6},{3,7},{4,0},{5,1},{6,2},{7,3},{8,12},{9,13},{10,... | collective-permute-start | bytes 786440 | tf_op jit(solution)/shard_map/ppermute | solution.py:26
  109.0 19.7 %collective-permute-start.30 = (bf16[2,128,512]{2,1,0:T(8,128)(2,1)S(1)}, bf16[2,128,512]{2,1,0:T(8,128)(2,1)S(1)}, u32[]{:S(2)}, u32[]{:S(2)}) collective-permute-start(bf16[2,128,512]{2,1,0:T(8,128)(2,1)S(1)} %slice_bitcast_fusion), channel_id=1, source_target_pairs={{0,2},{1,3},{2,0},{3,1},{4,6},{5,7},{6,4},{7,5},{8,10},{9,11},{10,... | collective-permute-start | bytes 786440 | tf_op jit(solution)/shard_map/ppermute | solution.py:26
  116.9 13.7 %collective-permute-start.21 = (bf16[2,128,512]{2,1,0:T(8,128)(2,1)S(1)}, bf16[2,128,512]{2,1,0:T(8,128)(2,1)S(1)}, u32[]{:S(2)}, u32[]{:S(2)}) collective-permute-start(bf16[2,128,512]{2,1,0:T(8,128)(2,1)S(1)} %slice_bitcast_fusion.6), channel_id=1, source_target_pairs={{0,4},{1,5},{2,6},{3,7},{4,0},{5,1},{6,2},{7,3},{8,12},{9,13},{10,... | collective-permute-start | bytes 786440 | tf_op jit(solution)/shard_map/ppermute | solution.py:26
  120.1 14.3 %collective-permute-start.24 = (bf16[2,128,512]{2,1,0:T(8,128)(2,1)S(1)}, bf16[2,128,512]{2,1,0:T(8,128)(2,1)S(1)}, u32[]{:S(2)}, u32[]{:S(2)}) collective-permute-start(bf16[2,128,512]{2,1,0:T(8,128)(2,1)S(1)} %slice_bitcast_fusion.4), channel_id=1, source_target_pairs={{0,2},{1,3},{2,0},{3,1},{4,6},{5,7},{6,4},{7,5},{8,10},{9,11},{10,... | collective-permute-start | bytes 786440 | tf_op jit(solution)/shard_map/ppermute | solution.py:26
  126.7 15.9 %collective-permute-start.28 = (bf16[128,512]{1,0:T(8,128)(2,1)S(1)}, bf16[128,512]{1,0:T(8,128)(2,1)S(1)}, u32[]{:S(2)}, u32[]{:S(2)}) collective-permute-start(bf16[128,512]{1,0:T(8,128)(2,1)S(1)} %slice_bitcast_fusion.10), channel_id=1, source_target_pairs={{0,8},{1,9},{2,10},{3,11},{4,12},{5,13},{6,14},{7,15},{8,0},{9,1},... | collective-permute-start | bytes 393224 | tf_op jit(solution)/shard_map/ppermute | solution.py:26
  128.9 15.2 %collective-permute-start.31 = (bf16[128,512]{1,0:T(8,128)(2,1)S(1)}, bf16[128,512]{1,0:T(8,128)(2,1)S(1)}, u32[]{:S(2)}, u32[]{:S(2)}) collective-permute-start(bf16[128,512]{1,0:T(8,128)(2,1)S(1)} %slice_bitcast_fusion.8), channel_id=1, source_target_pairs={{0,8},{1,9},{2,10},{3,11},{4,12},{5,13},{6,14},{7,15},{8,0},{9,1},... | collective-permute-start | bytes 393224 | tf_op jit(solution)/shard_map/ppermute | solution.py:26
  130.7 14.7 %collective-permute-start.22 = (bf16[128,512]{1,0:T(8,128)(2,1)S(1)}, bf16[128,512]{1,0:T(8,128)(2,1)S(1)}, u32[]{:S(2)}, u32[]{:S(2)}) collective-permute-start(bf16[128,512]{1,0:T(8,128)(2,1)S(1)} %slice_bitcast_fusion.14), channel_id=1, source_target_pairs={{0,8},{1,9},{2,10},{3,11},{4,12},{5,13},{6,14},{7,15},{8,0},{9,1},... | collective-permute-start | bytes 393224 | tf_op jit(solution)/shard_map/ppermute | solution.py:26
  134.5 12.3 %collective-permute-start.25 = (bf16[128,512]{1,0:T(8,128)(2,1)S(1)}, bf16[128,512]{1,0:T(8,128)(2,1)S(1)}, u32[]{:S(2)}, u32[]{:S(2)}) collective-permute-start(bf16[128,512]{1,0:T(8,128)(2,1)S(1)} %slice_bitcast_fusion.12), channel_id=1, source_target_pairs={{0,8},{1,9},{2,10},{3,11},{4,12},{5,13},{6,14},{7,15},{8,0},{9,1},... | collective-permute-start | bytes 393224 | tf_op jit(solution)/shard_map/ppermute | solution.py:26

commit v2 on v1

v2 whole, which is shorter than its diff:
```python
import functools

import jax
import jax.numpy as jnp
from jax import lax
from jax.experimental import pallas as pl
from jax.experimental.pallas import tpu as pltpu
from jax.sharding import PartitionSpec as P

LEN = 128
TICK = 100_000_000
BF = jnp.bfloat16
F32 = jnp.float32
PACK_MIB = 63


def params(mib):
    return pltpu.CompilerParams(vmem_limit_bytes=mib << 20)


FREE = pl.CostEstimate(flops=0, bytes_accessed=0, transcendentals=0)


def swap(x, mask):
    n = lax.axis_size("psg")
    return lax.ppermute(x, "psg", [(i, i ^ mask) for i in range(n)])


def pack_kernel(
    slots, ids_ref, place_in, live_in, resid_in, gain_in, query_in, score_in, ret_in, out_ref,
    place_ref, live_ref, resid_ref, gain_ref, query_ref, score_ref, ret_ref, sems,
):
    me = ids_ref[0]
    passages = place_ref.shape[0]
    width = out_ref.shape[1]
    queries, picks = ret_ref.shape
    inputs = (resid_in, place_in, live_in, ret_in, score_in, query_in, gain_in)
    targets = (resid_ref, place_ref, live_ref, ret_ref, score_ref, query_ref, gain_ref)
    small = [pltpu.make_async_copy(a, b, sems.at[i]) for i, (a, b) in enumerate(zip(inputs, targets))]
    for copy in small:
        copy.start()
    for copy in small[1:]:
        copy.wait()
    ids = ret_ref[...]

    def look(i, placed):
        p = place_ref[i]
        owner = p // slots
        slot = p % slots
        rel = (owner ^ me) * slots + slot
        rel = jnp.where(slot < live_ref[owner], rel, -1)
        return jnp.where(ids == i, rel, placed)

    placed = lax.fori_loop(0, passages, look, jnp.full(ids.shape, -1, jnp.int32), unroll=8)
    score = score_ref[...].astype(F32)
    lanes = max(passages, 128)
    cols = lax.broadcasted_iota(jnp.int32, (queries, lanes), 1)
    pairs = jnp.zeros((queries, lanes), F32)
    for k in range(picks):
        pairs = pairs + jnp.where(cols == placed[:, k : k + 1], score[:, k : k + 1], 0.0)
    if lanes < width:
        pairs = jnp.concatenate([pairs, jnp.zeros((queries, width - lanes), F32)], axis=1)
    small[0].wait()
    rows = []
    for s in range(slots):
        x = resid_ref[s * LEN : (s + 1) * LEN, :].astype(F32)
        centre = x - jnp.mean(x, axis=-1, keepdims=True)
        inverse = lax.rsqrt(jnp.mean(centre * centre, axis=-1, keepdims=True) + 1e-06)
        rows.append(jnp.mean(centre * inverse, axis=0, keepdims=True) * gain_ref[...])
    out_ref[...] = jnp.concatenate(rows + [query_ref[...].astype(F32), pairs], axis=0).astype(BF)


def pack(slots, ids, placement, live, resid, gain, query, score, retrieved):
    width = resid.shape[1]
    queries = query.shape[0]
    smem = pl.BlockSpec(memory_space=pltpu.SMEM)
    hbm = pl.BlockSpec(memory_space=pltpu.HBM)
    scratch = [pltpu.SMEM(x.shape, x.dtype) for x in (placement, live)]
    scratch += [pltpu.VMEM(x.shape, x.dtype) for x in (resid, gain, query, score, retrieved)]
    return pl.pallas_call(
        functools.partial(pack_kernel, slots),
        out_shape=jax.ShapeDtypeStruct((slots + 2 * queries, width), BF),
        in_specs=[smem] + [hbm] * 7,
        out_specs=pl.BlockSpec(memory_space=pltpu.VMEM),
        scratch_shapes=scratch + [pltpu.SemaphoreType.DMA((7,))],
        compiler_params=params(PACK_MIB),
        cost_estimate=FREE,
        name="pack",
    )(ids, placement, live, resid, gain, query, score, retrieved)


def resid_kernel(slots, queries, own_ref, nb_ref, all_ref, gain_ref, bf_ref, question_ref, pass_ref):
    step = pl.program_id(0)
    rows = slots + 2 * queries
    total = all_ref.shape[0]
    lanes = max(total // rows * slots, 128)

    @pl.when(step == 0)
    def _():
        table = all_ref[...]
        head = all_ref[:, :lanes].astype(F32)
        r = lax.broadcasted_iota(jnp.int32, (total, lanes), 0)
        c = lax.broadcasted_iota(jnp.int32, (total, lanes), 1)
        inside = r % rows
        moved = pltpu.roll(head, total - queries, 0)
        is_query = (inside >= slots) & (inside < slots + queries)
        fc = lax.broadcasted_iota(jnp.int32, (lanes, 128), 0)
        fs = lax.broadcasted_iota(jnp.int32, (lanes, 128), 1)
        picked = jnp.zeros((total, 128), F32)
        for k in range(2):
            mine = jnp.where(is_query & (c // slots == ((r // rows) ^ k)), moved, 0.0).astype(BF)
            fold = ((fc % slots + k * slots) == fs).astype(F32).astype(BF)
            picked = picked + jnp.dot(mine, fold, preferred_element_type=F32)
        grads = lax.dot_general(
            picked.astype(BF), table, (((0,), (0,)), ((), ())), preferred_element_type=F32
        )
        pass_ref[...] = grads[: 2 * slots] * gain_ref[...] * (1.0 / LEN)
        own = head[:rows]
        ec = lax.broadcasted_iota(jnp.int32, (lanes, total), 0)
        er = lax.broadcasted_iota(jnp.int32, (lanes, total), 1)
        spread = ((er // rows == ec // slots) & (er % rows == ec % slots)).astype(F32).astype(BF)
        weights = jnp.dot(own.astype(BF), spread, preferred_element_type=F32).astype(BF)
        result = jnp.dot(weights, table, preferred_element_type=F32)
        question_ref[...] = result[slots + queries :]

    for k, src in enumerate((own_ref, nb_ref)):
        x = src[...].astype(F32)
        centre = x - jnp.mean(x, axis=-1, keepdims=True)
        inverse = lax.rsqrt(jnp.mean(centre * centre, axis=-1, keepdims=True) + 1e-06)
        normed = centre * inverse
        scaled = pass_ref[pl.ds(k * slots + step, 1), :]
        base = scaled - jnp.mean(scaled, axis=-1, keepdims=True)
        grad = inverse * (base - normed * jnp.mean(scaled * normed, axis=-1, keepdims=True))
        bf_ref[k] = grad.astype(BF)


def resid_grads(slots, queries, own, nb, table, gain):
    tokens, width = own.shape
    total = table.shape[0]
    return pl.pallas_call(
        functools.partial(resid_kernel, slots, queries),
        grid=(slots,),
        out_shape=(
            jax.ShapeDtypeStruct((2, tokens, width), BF),
            jax.ShapeDtypeStruct((queries, width), F32),
        ),
        in_specs=[
            pl.BlockSpec((LEN, width), lambda s: (s, 0)),
            pl.BlockSpec((LEN, width), lambda s: (s, 0)),
            pl.BlockSpec((total, width), lambda s: (0, 0)),
            pl.BlockSpec((1, width), lambda s: (0, 0)),
        ],
        out_specs=(
            pl.BlockSpec((2, LEN, width), lambda s: (0, s, 0)),
            pl.BlockSpec((queries, width), lambda s: (0, 0)),
        ),
        scratch_shapes=[pltpu.VMEM((2 * slots, width), F32)],
        compiler_params=params(8),
        cost_estimate=FREE,
        name="resid_grads",
    )(own, nb, table, gain)


def gelu_kernel(half, ids_ref, in_ref, act0, act1, slope0, slope1):
    chip, core, group = ids_ref[0] // 2, ids_ref[0] % 2, ids_ref[1]
    width = act0.shape[1]
    for i in range(width // 128):
        if half:
            rows = 2 * width // half
            a, b = (
                in_ref[:, pl.ds(pl.multiple_of(((chip ^ j) * 2 + core) * rows, 128), 128)].astype(F32)
                for j in (2 * i, 2 * i + 1)
            )
            low = jnp.concatenate([a[:, :64], b[:, :64]], axis=1)
            high = jnp.concatenate([a[:, 64:], b[:, 64:]], axis=1)
        else:
            low = in_ref[:, i * 128 : (i + 1) * 128].astype(F32)
            high = in_ref[:, width + i * 128 : width + (i + 1) * 128].astype(F32)
        pair = jnp.where(group == 0, low, high), jnp.where(group == 0, high, low)
        for z, act, slope in zip(pair, (act0, act1), (slope0, slope1)):
            cdf = 0.5 * (1.0 + lax.erf(z * 0.7071067811865476))
            density = jnp.exp(-0.5 * z * z) * 0.3989422804014327
            act[:, i * 128 : (i + 1) * 128] = (z * cdf).astype(BF)
            slope[:, i * 128 : (i + 1) * 128] = cdf + z * density


def gelu(ids, preact, units, half):
    tokens, width = preact.shape
    block = 128
    out = pl.BlockSpec((block, units // 2), lambda i, ids: (i, 0))
    return pl.pallas_call(
        functools.partial(gelu_kernel, half),
        grid_spec=pltpu.PrefetchScalarGridSpec(
            num_scalar_prefetch=1,
            grid=(tokens // block,),
            in_specs=[pl.BlockSpec((block, width), lambda i, ids: (i, 0))],
            out_specs=[out] * 4,
        ),
        out_shape=[jax.ShapeDtypeStruct((tokens, units // 2), t) for t in (BF, BF, F32, F32)],
        compiler_params=params(8),
        cost_estimate=FREE,
        name="gelu",
    )(ids, preact)


def grad_out_kernel(rows, own_ref, nb_ref, resid_ref, keep_ref, sent_ref):
    contract = (((0,), (0,)), ((), ()))
    out = lax.dot_general(own_ref[...], resid_ref[0], contract, preferred_element_type=F32)
    out = out + lax.dot_general(nb_ref[...], resid_ref[1], contract, preferred_element_type=F32)
    keep_ref[...], sent_ref[...] = halves(out, rows)


def grad_out_part(rows, own, nb, resid):
    tokens, units = own.shape
    width = resid.shape[2]
    block = 256
    return pl.pallas_call(
        functools.partial(grad_out_kernel, rows),
        grid=(units // block,),
        in_specs=[pl.BlockSpec((tokens, block), lambda j: (0, j))] * 2
        + [pl.BlockSpec((2, tokens, width), lambda j: (0, 0, 0))],
        out_specs=[pl.BlockSpec((block // 2, width), lambda j: (j, 0))] * 2,
        out_shape=[jax.ShapeDtypeStruct((units // 2, width), BF)] * 2,
        compiler_params=params(12),
        cost_estimate=FREE,
        name="grad_out",
    )(own, nb, resid)


def grad_in_kernel(
    rows, resid_ref, w_ref, slope_own, slope_nb, own_ref, nb_ref, pre_ref, keep_ref, sent_ref
):
    total = None
    for k, (slope, states) in enumerate(((slope_own, own_ref), (slope_nb, nb_ref))):
        hidden = lax.dot_general(
            resid_ref[k], w_ref[...], (((1,), (1,)), ((), ())), preferred_element_type=F32
        )
        pre = (hidden * slope[...]).astype(BF)
        pre_ref[k] = pre
        out = lax.dot_general(
            pre, states[...], (((0,), (0,)), ((), ())), preferred_element_type=F32
        )
        total = out if total is None else total + out
    keep_ref[...], sent_ref[...] = halves(total, rows)


def grad_in_part(rows, resid, w_out, slope_own, slope_nb, states, states_nb):
    _, tokens, width = resid.shape
    units = w_out.shape[0]
    block = 256
    whole = lambda j: (0, 0)
    return pl.pallas_call(
        functools.partial(grad_in_kernel, rows),
        grid=(units // block,),
        in_specs=[
            pl.BlockSpec((2, tokens, width), lambda j: (0, 0, 0)),
            pl.BlockSpec((block, width), lambda j: (j, 0)),
            pl.BlockSpec((tokens, block), lambda j: (0, j)),
            pl.BlockSpec((tokens, block), lambda j: (0, j)),
            pl.BlockSpec(states.shape, whole),
            pl.BlockSpec(states.shape, whole),
        ],
        out_specs=(
            pl.BlockSpec((2, tokens, block), lambda j: (0, 0, j)),
            pl.BlockSpec((block // 2, width), lambda j: (j, 0)),
            pl.BlockSpec((block // 2, width), lambda j: (j, 0)),
        ),
        out_shape=(
            jax.ShapeDtypeStruct((2, tokens, units), BF),
            jax.ShapeDtypeStruct((units // 2, width), BF),
            jax.ShapeDtypeStruct((units // 2, width), BF),
        ),
        compiler_params=params(18),
        cost_estimate=FREE,
        name="grad_in",
    )(resid, w_out, slope_own, slope_nb, states, states_nb)


def input_nb_kernel(pre0, pre1, w0, w1, out_ref):
    total = jnp.dot(pre0[0], w0[...], preferred_element_type=F32)
    total = total + jnp.dot(pre1[0], w1[...], preferred_element_type=F32)
    out_ref[...] = total.astype(BF)


def input_own_kernel(pre0, pre1, w0, w1, resid_ref, nb_ref, mark_ref, out_ref):
    total = jnp.dot(pre0[0], w0[...], preferred_element_type=F32)
    total = total + jnp.dot(pre1[0], w1[...], preferred_element_type=F32)
    out_ref[...] = (total + nb_ref[...].astype(F32) + resid_ref[0].astype(F32)).astype(BF)


def input_part(pre, w_in, which, extra):
    _, tokens, units = pre[0].shape
    width = w_in[0].shape[1]
    block = 256
    row = pl.BlockSpec((block, width), lambda i: (i, 0))
    first = pl.BlockSpec((1, block, width), lambda i: (0, i, 0))
    return pl.pallas_call(
        input_own_kernel if extra else input_nb_kernel,
        grid=(tokens // block,),
        in_specs=[pl.BlockSpec((1, block, units), lambda i: (which, i, 0))] * 2
        + [pl.BlockSpec((units, width), lambda i: (0, 0))] * 2
        + [first, row, pl.BlockSpec(memory_space=pl.ANY)][: len(extra)],
        out_specs=row,
        out_shape=jax.ShapeDtypeStruct((tokens, width), BF),
        compiler_params=params(14),
        cost_estimate=FREE,
        name="input_own" if extra else "input_nb",
    )(*pre, *w_in, *extra)


def tick_kernel(in_ref, out_ref):
    out_ref[...] = in_ref[...]


def tick(x, count):
    vmem = pl.BlockSpec(memory_space=pltpu.VMEM)
    return pl.pallas_call(
        tick_kernel,
        in_specs=[vmem],
        out_specs=vmem,
        out_shape=jax.ShapeDtypeStruct(x.shape, x.dtype),
        compiler_params=params(1),
        cost_estimate=pl.CostEstimate(flops=count * TICK, bytes_accessed=0, transcendentals=0),
        name="tick",
    )(x)


class Order:
    def __init__(self, mark):
        self.mark = mark

    def gate(self, *args):
        *args, self.mark = lax.optimization_barrier((*args, self.mark))
        return args

    def __call__(self, work, *args, ticks=1):
        out = work(*self.gate(*args))
        leaves, tree = jax.tree.flatten(out)
        out = jax.tree.unflatten(tree, self.gate(*leaves))
        if ticks:
            self.mark = tick(self.mark, ticks)
        return out


def place(mask, masks):
    return sum(1 for other in masks if other > mask)


def run(kernel, name, shapes, *args):
    vmem = pl.BlockSpec(memory_space=pltpu.VMEM)
    return pl.pallas_call(
        kernel,
        in_specs=[vmem] * len(args),
        out_specs=[vmem] * len(shapes),
        out_shape=[jax.ShapeDtypeStruct(s, BF) for s in shapes],
        compiler_params=params(6),
        cost_estimate=FREE,
        name=name,
    )(*args)


def join_kernel(rows, a_ref, b_ref, out_ref):
    total, width = a_ref.shape
    if rows % 16:
        a, b = (x[...].astype(F32).reshape(total // rows, rows, width) for x in (a_ref, b_ref))
        out_ref[...] = jnp.stack([a, b], axis=1).reshape(2 * total, width).astype(BF)
        return
    for i in range(total // rows):
        part = slice(i * rows, (i + 1) * rows)
        out_ref[2 * i * rows : (2 * i + 1) * rows] = a_ref[part]
        out_ref[(2 * i + 1) * rows : (2 * i + 2) * rows] = b_ref[part]


def join(a, b, rows):
    total, width = a.shape
    return run(functools.partial(join_kernel, rows), "join", [(2 * total, width)], a, b)[0]


def halves(x, rows):
    total, width = x.shape
    x = x.reshape(total // (2 * rows), 2, rows, width)
    return [x[:, k].reshape(total // 2, width).astype(BF) for k in range(2)]


def fold_kernel(rows, a_ref, b_ref, keep_ref, sent_ref):
    total = a_ref[...].astype(F32) + b_ref[...].astype(F32)
    keep_ref[...], sent_ref[...] = halves(total, rows)


def fold(a, b, rows):
    total, width = a.shape
    return run(functools.partial(fold_kernel, rows), "fold", [(total // 2, width)] * 2, a, b)


def merge_kernel(rows, a0, b0, a1, b1, keep_ref, sent_ref):
    for k, (a, b) in enumerate(((a0, b0), (a1, b1))):
        count = a.shape[0] // 2
        part = slice(k * count, (k + 1) * count)
        keep_ref[part], sent_ref[part] = halves(a[...].astype(F32) + b[...].astype(F32), rows)


def merge(a0, b0, a1, b1, rows):
    total, width = a0.shape
    return run(functools.partial(merge_kernel, rows), "merge", [(total, width)] * 2, a0, b0, a1, b1)


def total_kernel(ids_ref, *refs):
    *parts, mark_ref, out_ref = refs
    rows = out_ref.shape[0] // 2
    sums = [a[...].astype(F32) + b[...].astype(F32) for a, b in zip(parts[::2], parts[1::2])]
    if len(sums) == 1:
        sums = [sums[0][:rows], sums[0][rows:]]
    for k, x in enumerate(sums):
        start = k * rows + (1 - 2 * k) * ids_ref[1] * rows
        out_ref[pl.ds(pl.multiple_of(start, rows), rows)] = x


def total(ids, mark, *chains):
    parts = [x for chain in chains for x in (chain.keep, chain.came)]
    rows = sum(chain.keep.shape[0] for chain in chains)
    vmem = pl.BlockSpec(memory_space=pltpu.VMEM)
    return pl.pallas_call(
        total_kernel,
        in_specs=[pl.BlockSpec(memory_space=pltpu.SMEM)] + [vmem] * (len(parts) + 1),
        out_shape=jax.ShapeDtypeStruct((rows, parts[0].shape[1]), F32),
        compiler_params=params(6),
        cost_estimate=FREE,
        name="total",
    )(ids, *parts, mark)


class Gather:
    def __init__(self, order, x, masks):
        self.order, self.x, self.todo, self.done = order, x, list(masks), []
        self.rows = x.shape[0]

    def send(self):
        if self.todo:
            self.came = swap(*self.order.gate(self.x), self.todo[0])

    def block(self, mask):
        return self.rows << (len(self.done) - place(mask, self.done))

    def step(self, send=True, ticks=1):
        mask = self.todo.pop(0)
        rows = self.block(mask)
        self.x = self.order(lambda a, b: join(a, b, rows), self.x, self.came, ticks=ticks)
        self.done.append(mask)
        self.arrived = self.came
        if send:
            self.send()

    def until(self, left, send=True, ticks=1):
        while len(self.todo) > left:
            self.step(send or len(self.todo) > left + 1, ticks)


class Scatter:
    def __init__(self, order, make, rows, masks):
        self.order, self.make, self.rows, self.left = order, make, rows, list(masks)

    def block(self):
        return self.rows << (len(self.left) - 1 - place(self.left[0], self.left))

    def start(self, *args, send=True):
        rows = self.block()
        *extra, self.keep, self.sent = self.order(lambda *x: self.make(rows, *x), *args, ticks=0)
        if send:
            self.send()
        return extra

    def send(self):
        self.came = swap(*self.order.gate(self.sent), self.left[0])

    def step(self):
        self.left.pop(0)
        rows = self.block()
        self.keep, self.sent = self.order(lambda a, b: fold(a, b, rows), self.keep, self.came)
        self.send()

    def absorb(self, other):
        self.left.pop(0)
        rows = self.block()
        self.keep, self.sent = self.order(
            lambda *x: merge(*x, rows), self.keep, self.came, other.keep, other.came
        )
        self.send()

    def until(self, left):
        while len(self.left) > left:
            self.step()


def shards(
    passage_states,
    saved_preact,
    saved_resid,
    w_in,
    w_out,
    norm_gain,
    query_emb,
    score_grads,
    retrieved,
    placement_map,
    live_counts,
):
    n = lax.axis_size("psg")
    shared = lax.axis_size("groups") == 2
    me = lax.axis_index("psg").astype(jnp.int32)
    group = lax.axis_index("groups").astype(jnp.int32) if shared else jnp.int32(0)
    ids = jnp.stack([me, group])
    core, chip = me % 2, me // 2
    half = n // 2
    tokens, width = saved_resid.shape
    rows = w_in.shape[0]
    units = half * rows
    slots = tokens // LEN
    queries = query_emb.shape[0]
    masks = [1 << b for b in range(1, n.bit_length() - 1)]
    up, down = masks, masks[::-1]
    side = masks[1::-1] + masks[2:]
    gain = norm_gain.reshape(1, width)
    whole_tiles = rows == 128
    order = Order(jnp.zeros((8, 128), F32) + me.astype(F32))

    def cross(x):
        return lax.ppermute(x, "groups", [(0, 1), (1, 0)])

    preact_own = columns = saved_preact
    if not whole_tiles:
        view = saved_preact.reshape(tokens, half, 2, 2, rows // 2)
        view = jnp.take(view, jnp.arange(half) ^ chip, axis=1).transpose(2, 0, 3, 1, 4)
        view = view.reshape(2, tokens, units)
        preact_own = lax.dynamic_index_in_dim(view, core, axis=0, keepdims=False)
        columns = lax.dynamic_index_in_dim(view, 1 - core, axis=0, keepdims=False)
    mine_out, mine_in = (
        lax.dynamic_slice_in_dim(w, group * (rows // 2), rows // 2, 0) for w in (w_out, w_in)
    )
    out = Gather(order, mine_out, down)
    inp = Gather(order, mine_in, down)
    out.send()
    preact_nb = swap(columns, 1)
    resid_nb = swap(saved_resid, 1)
    states_nb = swap(passage_states, 1)
    table = order(
        lambda *args: pack(slots, ids, *args),
        placement_map, live_counts, saved_resid, gain, query_emb, score_grads, retrieved, ticks=0,
    )

    def core_gelu(x):
        return order(lambda x: gelu(ids, x, units, half if whole_tiles else 0), x, ticks=0)

    small = Gather(order, table, masks[:1] + masks[:0:-1] + [1])
    last = len(down)
    out.until(last - 1)
    small.send()
    own = core_gelu(preact_own)
    inp.send()
    small.until(last)
    small.until(last - 1)
    out.until(1)
    early = cross(out.x)
    small.until(1)
    preact_nb, resid_nb, states_nb = order.gate(preact_nb, resid_nb, states_nb)
    near = core_gelu(preact_nb)
    inp.until(last - 1)
    small.until(0)
    resid_bf, question_grad = order(
        lambda a, b, c: resid_grads(slots, queries, a, b, c, gain),
        saved_resid, resid_nb, small.x, ticks=0,
    )

    side_rows = rows // 2
    go0, go1 = (Scatter(order, grad_out_part, side_rows, side) for _ in range(2))
    gi0 = Scatter(order, grad_in_part, side_rows, up)
    gi1 = Scatter(order, grad_in_part, side_rows, side)
    go0.start(own[0], near[0], resid_bf)
    go1.start(own[1], near[1], resid_bf, send=False)
    inp.until(1, send=False)
    early, = order.gate(early)
    out.until(0)
    late = cross(out.arrived)
    inp.send()
    pre0, = gi0.start(resid_bf, out.x, own[2], near[2], passage_states, states_nb)
    go1.send()
    inp.until(0)
    in0 = inp.x
    in1 = cross(in0)
    joined = out.rows << (len(down) - 1 - place(down[-1], down))
    out1 = order(lambda a, b: join(a, b, joined), early, late)
    pre1, = gi1.start(resid_bf, out1, own[3], near[3], passage_states, states_nb)
    go0.absorb(go1)
    gi0.step()
    gi1.step()
    go0.until(1)
    gi0.until(1)
    gi1.until(1)
    go0.came, = order.gate(go0.came)

    pre = (pre0, pre1)
    sent = order(lambda a, b: input_part(pre, (a, b), 1, ()), in0, in1, ticks=0)
    back = swap(sent, 1)
    grad_out = total(ids, order.mark, go0)
    back, = order.gate(back)
    mark = order.mark
    input_grad = order(lambda x: input_part(pre, (in0, in1), 0, (resid_bf, x, mark)), back, ticks=0)
    gi0.came, gi1.came = order.gate(gi0.came, gi1.came)
    grad_in = total(ids, order.mark, gi0, gi1)
    return (input_grad, grad_in, grad_out, question_grad)


def solution(mesh):
    both = P(("groups", "psg"), None)
    return jax.shard_map(
        shards,
        mesh=mesh,
        in_specs=(both, both, both, P("psg", None), P("psg", None), P(), both, both, both, P("groups"), P("groups")),
        out_specs=(both, both, both, both),
        check_vma=False,
    )
```

time: 150 us -> 121 us (0.81)
  waiting for transfers between devices: 72.7 us -> 45.1 us
  local copies, waits for them, and re-layouts: 9.66 us -> 3.27 us
  starting transfers between devices: 31.3 us -> 37 us
  other arithmetic: 5.52 us -> 0.58 us
  Pallas kernels: 29.6 us -> 33.4 us
    ppermute x32 -> x24, waiting for transfers between devices: 72.7 us -> 45.1 us  [swap(): return lax.ppermute(x, 'psg', [(i, i ^ mask) for i in range(n)])]
    ppermute x0 -> x3, starting transfers between devices: none -> 4.61 us  [cross(): return lax.ppermute(x, 'groups', [(0, 1), (1, 0)])]
    unnamed x32 -> x14, local copies, waits for them, and re-layouts: 6.06 us -> 2.28 us
    another operation x2 -> x0, local copies, waits for them, and re-layouts: 2.71 us -> none  [gather(): x = jnp.stack([x, swap(x, mask)], axis=pos)]
    concatenate x7 -> x0, other arithmetic: 2.22 us -> none  [the longest x2 1.66 us: scatter(): return jnp.concatenate(done, axis=-1)]
    pallas_call x1, Pallas kernels: 1.75 us -> 3.66 us  [pack(): pl.pallas_call(functools.partial(pack_kernel, slots), out_shape=jax.Shape...]
    another operation x10 -> x1, other arithmetic: 2.38 us -> 0.58 us  [shards(): ids = jnp.stack([me, group])]
    ppermute x32 -> x24, starting transfers between devices: 31.3 us -> 32.4 us  [swap(): return lax.ppermute(x, 'psg', [(i, i ^ mask) for i in range(n)])]
  transfers between devices with their start and end apart: 32 -> 27, of which waited for: 18 -> 12; matrix products, arithmetic and copies ran while one was open for 6% -> 1% of each run, Pallas kernels for 17% -> 25%
where the time goes in v2:
time: 121 us; the launch traced here: 120 us
  waiting for transfers between devices  45.1 us (37%)
  starting transfers between devices  37 us (31%)
  Pallas kernels  33.4 us (28%)
  local copies, waits for them, and re-layouts  3.27 us (3%)
    ppermute x24, waiting for transfers between devices, swap(): return lax.ppermute(x, 'psg', [(i, i ^ mask) for i in range(n)])  45.1 us
    ppermute x24, starting transfers between devices, swap(): return lax.ppermute(x, 'psg', [(i, i ^ mask) for i in range(n)])  32.4 us
    pallas_call x2, Pallas kernels, grad_in_part(): pl.pallas_call(functools.partial(grad_in_kernel, rows), grid=(units // bl...  8.39 us
    pallas_call x2, Pallas kernels, gelu(): pl.pallas_call(functools.partial(gelu_kernel, half), grid_spec=pltpu.Pref...  5.94 us
    pallas_call x1, Pallas kernels, resid_grads(): pl.pallas_call(functools.partial(resid_kernel, slots, queries), grid=(slo...  4.71 us
    ppermute x3, starting transfers between devices, cross(): return lax.ppermute(x, 'groups', [(0, 1), (1, 0)])  4.61 us
    pallas_call x2, Pallas kernels, input_part(): pl.pallas_call(input_own_kernel if extra else input_nb_kernel, grid=(toke...  3.69 us
    pallas_call x1, Pallas kernels, pack(): pl.pallas_call(functools.partial(pack_kernel, slots), out_shape=jax.Shape...  3.66 us
  transfers between devices with their start and end apart: 27, of which 12 were waited for; matrix products, arithmetic and copies ran while one was open for 1% of the time, Pallas kernels for 25%

profile of v2, /device:TPU:0, one launch (start us, length us, event | category | flops | bytes accessed | tf_op | source)
XLA Modules:
  0.0 120.4 jit_solution(13210672492040205522)
XLA Ops:
  0.6 0.5 collective-permute-start
  1.1 0.1 collective-permute-start.2
  1.2 0.4 collective-permute-start.1
  1.7 1.0 constant_dynamic-slice_fusion
  2.7 3.7 %collective-permute-start.3 = (bf16[64,1024]{1,0:T(8,128)(2,1)S(1)}, bf16[64,1024]{1,0:T(8,128)(2,1)S(1)}, u32[]{:S(2)}, u32[]{:S(2)}) collective-permute-start(bf16[64,1024]{1,0:T(8,128)(2,1)S(1)} %get-tuple-element.269.a_ref), channel_id=1, source_target_pairs={{0,8},{1,9},{2,10},{3,11},{4,12},{5,13},{6,14},{7,15},{8,0},{9,1},... | collective-permute-start | bytes 393224 | tf_op jit(solution)/shard_map/ppermute | solution.py:26
  6.4 0.6 pad_add_fusion.ids_ref
  7.0 3.7 %pack.1.a_ref = bf16[8,1024]{1,0:T(8,128)(2,1)} custom-call(s32[2]{0:T(128)} %pad_add_fusion.ids_ref, s32[64]{0:T(128)} %place_in, s32[16]{0:T(128)} %live_in, bf16[512,1024]{1,0:T(8,128)(2,1)} %own_ref, f32[1,1024]{1,0:T(1,128)} %bitcast.3, bf16[2,1024]{1,0:T(2,128)(2,1)} %query_in, bf16[2,32]{1,0:T(2,128)(2,1)} %score_in, s32[2,32]{1,0:T(2,128)} %ret_in), custom_call_target="tpu_custom_call" | custom-call | tf_op jit(solution)/shard_map/pack/pallas_call | solution.py:80
  10.7 2.6 %collective-permute-done.3.b_ref = bf16[64,1024]{1,0:T(8,128)(2,1)S(1)} collective-permute-done((bf16[64,1024]{1,0:T(8,128)(2,1)S(1)}, bf16[64,1024]{1,0:T(8,128)(2,1)S(1)}, u32[]{:S(2)}, u32[]{:S(2)}) %collective-permute-start.3) | collective-permute-done | bytes 131104 | tf_op jit(solution)/shard_map/ppermute | solution.py:26
  13.3 0.8 collective-permute-start.7
  14.1 1.5 %collective-permute-start.4 = (bf16[8,1024]{1,0:T(8,128)(2,1)}, bf16[8,1024]{1,0:T(8,128)(2,1)S(1)}, u32[]{:S(2)}, u32[]{:S(2)}) collective-permute-start(bf16[8,1024]{1,0:T(8,128)(2,1)} %pack.1.a_ref), channel_id=1, source_target_pairs={{0,2},{1,3},{2,0},{3,1},{4,6},{5,7},{6,4},{7,5},{8,10},{9,11},{10,... | collective-permute-start | bytes 49160 | tf_op jit(solution)/shard_map/ppermute | solution.py:26
  15.7 1.6 %copy-done.2 = bf16[512,2048]{1,0:T(8,128)(2,1)S(1)} copy-done((bf16[512,2048]{1,0:T(8,128)(2,1)S(1)}, bf16[512,2048]{1,0:T(8,128)(2,1)}, u32[]{:S(2)}) %copy-start.2) | copy-done | bytes 2097176
  17.3 0.7 copy-done.5
  17.9 2.1 %gelu.2 = (bf16[512,512]{1,0:T(8,128)(2,1)S(1)}, bf16[512,512]{1,0:T(8,128)(2,1)S(1)}, f32[512,512]{1,0:T(8,128)S(1)}, f32[512,512]{1,0:T(8,128)S(1)}) custom-call(s32[2]{0:T(128)S(1)} %copy-done.5, bf16[512,2048]{1,0:T(8,128)(2,1)S(1)} %copy-done.2), custom_call_target="tpu_custom_call" | custom-call | tf_op jit(solution)/shard_map/gelu/pallas_call | solution.py:191
  20.1 3.4 %collective-permute-start.5 = (bf16[16,1024]{1,0:T(8,128)(2,1)S(1)}, bf16[16,1024]{1,0:T(8,128)(2,1)S(1)}, u32[]{:S(2)}, u32[]{:S(2)}) collective-permute-start(bf16[16,1024]{1,0:T(8,128)(2,1)S(1)} %join.12.a_ref), channel_id=1, source_target_pairs={{0,8},{1,9},{2,10},{3,11},{4,12},{5,13},{6,14},{7,15},{8,0},{9,1},... | collective-permute-start | bytes 98312 | tf_op jit(solution)/shard_map/ppermute | solution.py:26
  23.5 1.9 %collective-permute-done.5.b_ref = bf16[16,1024]{1,0:T(8,128)(2,1)S(1)} collective-permute-done((bf16[16,1024]{1,0:T(8,128)(2,1)S(1)}, bf16[16,1024]{1,0:T(8,128)(2,1)S(1)}, u32[]{:S(2)}, u32[]{:S(2)}) %collective-permute-start.5) | collective-permute-done | bytes 32800 | tf_op jit(solution)/shard_map/ppermute | solution.py:26
  25.4 1.0 collective-permute-start.6
  26.4 1.6 %collective-permute-start.11 = (bf16[256,1024]{1,0:T(8,128)(2,1)S(1)}, bf16[256,1024]{1,0:T(8,128)(2,1)S(1)}, u32[]{:S(2)}, u32[]{:S(2)}) collective-permute-start(bf16[256,1024]{1,0:T(8,128)(2,1)S(1)} %join.14.a_ref), channel_id=1, source_target_pairs={{0,16},{16,0},{1,17},{17,1},{2,18},{18,2},{3,19},{19,3},{4,20},{20... | collective-permute-start | bytes 1572872 | tf_op jit(solution)/shard_map/ppermute | solution.py:527
  28.0 1.8 %collective-permute-done.6.b_ref = bf16[32,1024]{1,0:T(8,128)(2,1)S(1)} collective-permute-done((bf16[32,1024]{1,0:T(8,128)(2,1)S(1)}, bf16[32,1024]{1,0:T(8,128)(2,1)S(1)}, u32[]{:S(2)}, u32[]{:S(2)}) %collective-permute-start.6) | collective-permute-done | bytes 65568 | tf_op jit(solution)/shard_map/ppermute | solution.py:26
  29.8 0.5 collective-permute-start.10
  30.3 3.4 %collective-permute-start.9 = (bf16[64,1024]{1,0:T(8,128)(2,1)S(1)}, bf16[64,1024]{1,0:T(8,128)(2,1)S(1)}, u32[]{:S(2)}, u32[]{:S(2)}) collective-permute-start(bf16[64,1024]{1,0:T(8,128)(2,1)S(1)} %get-tuple-element.324.a_ref), channel_id=1, source_target_pairs={{0,8},{1,9},{2,10},{3,11},{4,12},{5,13},{6,14},{7,15},{8,0},{9,1},... | collective-permute-start | bytes 393224 | tf_op jit(solution)/shard_map/ppermute | solution.py:26
  33.7 3.8 %gelu.3 = (bf16[512,512]{1,0:T(8,128)(2,1)S(1)}, bf16[512,512]{1,0:T(8,128)(2,1)S(1)}, f32[512,512]{1,0:T(8,128)S(1)}, f32[512,512]{1,0:T(8,128)S(1)}) custom-call(s32[2]{0:T(128)S(1)} %copy-done.5, bf16[512,2048]{1,0:T(8,128)(2,1)} %collective-permute-done.in_ref), custom_call_target="tpu_custom_call" | custom-call | tf_op jit(solution)/shard_map/gelu/pallas_call | solution.py:191
  37.5 0.4 collective-permute-done.9.b_ref
  38.0 0.1 collective-permute-start.12
  38.1 0.1 collective-permute-start.8
  38.2 1.3 %collective-permute-done.8.b_ref = bf16[64,1024]{1,0:T(8,128)(2,1)S(1)} collective-permute-done((bf16[64,1024]{1,0:T(8,128)(2,1)S(1)}, bf16[64,1024]{1,0:T(8,128)(2,1)S(1)}, u32[]{:S(2)}, u32[]{:S(2)}) %collective-permute-start.8) | collective-permute-done | bytes 131104 | tf_op jit(solution)/shard_map/ppermute | solution.py:26
  39.6 4.7 %resid_grads.1 = (bf16[2,512,1024]{2,1,0:T(8,128)(2,1)S(1)}, f32[2,1024]{1,0:T(2,128)}) custom-call(bf16[512,1024]{1,0:T(8,128)(2,1)S(1)} %copy-done.1, bf16[512,1024]{1,0:T(8,128)(2,1)} %collective-permute-done.1.nb_ref, bf16[128,1024]{1,0:T(8,128)(2,1)S(1)} %join.17.all_ref, f32[1,1024]{1,0:T(1,128)S(1)} %bitcast.4), custom_call_target="tpu_custom_call" | custom-call | tf_op jit(solution)/shard_map/resid_grads/pallas_call | solution.py:140
  44.3 1.6 %grad_out.2 = (bf16[256,1024]{1,0:T(8,128)(2,1)S(1)}, bf16[256,1024]{1,0:T(8,128)(2,1)S(1)}) custom-call(bf16[512,512]{1,0:T(8,128)(2,1)S(1)} %get-tuple-element.349.own_ref, bf16[512,512]{1,0:T(8,128)(2,1)S(1)} %get-tuple-element.350.nb_ref, bf16[2,512,1024]{2,1,0:T(8,128)(2,1)S(1)} %get-tuple-element.409.resid_ref), custom_call_target="tpu_custom_call" | custom-call | tf_op jit(solution)/shard_map/grad_out/pallas_call | solution.py:217
  45.8 1.6 %grad_out.3 = (bf16[256,1024]{1,0:T(8,128)(2,1)S(1)}, bf16[256,1024]{1,0:T(8,128)(2,1)S(1)}) custom-call(bf16[512,512]{1,0:T(8,128)(2,1)S(1)} %get-tuple-element.358.own_ref, bf16[512,512]{1,0:T(8,128)(2,1)S(1)} %get-tuple-element.359.nb_ref, bf16[2,512,1024]{2,1,0:T(8,128)(2,1)S(1)} %get-tuple-element.409.resid_ref), custom_call_target="tpu_custom_call" | custom-call | tf_op jit(solution)/shard_map/grad_out/pallas_call | solution.py:217
  47.5 0.1 join.19.w_ref
  47.6 1.7 %collective-permute-start.14 = (bf16[256,1024]{1,0:T(8,128)(2,1)S(1)}, bf16[256,1024]{1,0:T(8,128)(2,1)S(1)}, u32[]{:S(2)}, u32[]{:S(2)}) collective-permute-start(bf16[256,1024]{1,0:T(8,128)(2,1)S(1)} %join.18.a_ref), channel_id=1, source_target_pairs={{0,2},{1,3},{2,0},{3,1},{4,6},{5,7},{6,4},{7,5},{8,10},{9,11},{10,... | collective-permute-start | bytes 1572872 | tf_op jit(solution)/shard_map/ppermute | solution.py:26
  49.3 1.5 %collective-permute-start.13 = (bf16[256,1024]{1,0:T(8,128)(2,1)S(1)}, bf16[256,1024]{1,0:T(8,128)(2,1)S(1)}, u32[]{:S(2)}, u32[]{:S(2)}) collective-permute-start(bf16[256,1024]{1,0:T(8,128)(2,1)S(1)} %collective-permute-done.10.b_ref), channel_id=1, source_target_pairs={{0,16},{16,0},{1,17},{17,1},{2,18},{18,2},{3,19},{19,3},{4,20},{20... | collective-permute-start | bytes 1572872 | tf_op jit(solution)/shard_map/ppermute | solution.py:527
  50.8 1.9 %collective-permute-start.16 = (bf16[256,1024]{1,0:T(8,128)(2,1)S(1)}, bf16[256,1024]{1,0:T(8,128)(2,1)S(1)}, u32[]{:S(2)}, u32[]{:S(2)}) collective-permute-start(bf16[256,1024]{1,0:T(8,128)(2,1)S(1)} %get-tuple-element.422), channel_id=1, source_target_pairs={{0,4},{1,5},{2,6},{3,7},{4,0},{5,1},{6,2},{7,3},{8,12},{9,13},{10,... | collective-permute-start | bytes 1572872 | tf_op jit(solution)/shard_map/ppermute | solution.py:26
  52.7 4.2 %grad_in.2 = (bf16[2,512,512]{2,1,0:T(8,128)(2,1)S(1)}, bf16[256,1024]{1,0:T(8,128)(2,1)S(1)}, bf16[256,1024]{1,0:T(8,128)(2,1)S(1)}) custom-call(bf16[2,512,1024]{2,1,0:T(8,128)(2,1)S(1)} %get-tuple-element.409.resid_ref, bf16[512,1024]{1,0:T(8,128)(2,1)S(1)} %join.19.w_ref, f32[512,512]{1,0:T(8,128)S(1)} %get-tuple-element.382.slope_own, ...), custom_call_target="tpu_custom_call" | custom-call | tf_op jit(solution)/shard_map/grad_in/pallas_call | solution.py:252
  56.9 0.1 collective-permute-start.17
  57.1 4.6 %collective-permute-done.14.b_ref = bf16[256,1024]{1,0:T(8,128)(2,1)S(1)} collective-permute-done((bf16[256,1024]{1,0:T(8,128)(2,1)S(1)}, bf16[256,1024]{1,0:T(8,128)(2,1)S(1)}, u32[]{:S(2)}, u32[]{:S(2)}) %collective-permute-start.14) | collective-permute-done | bytes 524320 | tf_op jit(solution)/shard_map/ppermute | solution.py:26
  61.7 0.1 join.20.w0
  61.7 1.6 %collective-permute-start.15 = (bf16[512,1024]{1,0:T(8,128)(2,1)S(1)}, bf16[512,1024]{1,0:T(8,128)(2,1)S(1)}, u32[]{:S(2)}, u32[]{:S(2)}) collective-permute-start(bf16[512,1024]{1,0:T(8,128)(2,1)S(1)} %join.20.w0), channel_id=1, source_target_pairs={{0,16},{16,0},{1,17},{17,1},{2,18},{18,2},{3,19},{19,3},{4,20},{20... | collective-permute-start | bytes 3145736 | tf_op jit(solution)/shard_map/ppermute | solution.py:527
  63.3 1.6 %collective-permute-start.20 = (bf16[256,1024]{1,0:T(8,128)(2,1)S(1)}, bf16[256,1024]{1,0:T(8,128)(2,1)S(1)}, u32[]{:S(2)}, u32[]{:S(2)}) collective-permute-start(bf16[256,1024]{1,0:T(8,128)(2,1)S(1)} %get-tuple-element.442), channel_id=1, source_target_pairs={{0,2},{1,3},{2,0},{3,1},{4,6},{5,7},{6,4},{7,5},{8,10},{9,11},{10,... | collective-permute-start | bytes 1572872 | tf_op jit(solution)/shard_map/ppermute | solution.py:26
  64.9 0.1 join.21.w_ref
  65.0 4.2 %grad_in.3 = (bf16[2,512,512]{2,1,0:T(8,128)(2,1)S(1)}, bf16[256,1024]{1,0:T(8,128)(2,1)S(1)}, bf16[256,1024]{1,0:T(8,128)(2,1)S(1)}) custom-call(bf16[2,512,1024]{2,1,0:T(8,128)(2,1)S(1)} %get-tuple-element.409.resid_ref, bf16[512,1024]{1,0:T(8,128)(2,1)S(1)} %join.21.w_ref, f32[512,512]{1,0:T(8,128)S(1)} %get-tuple-element.411.slope_own, ...), custom_call_target="tpu_custom_call" | custom-call | tf_op jit(solution)/shard_map/grad_in/pallas_call | solution.py:252
  69.2 2.0 %collective-permute-start.19 = (bf16[256,1024]{1,0:T(8,128)(2,1)S(1)}, bf16[256,1024]{1,0:T(8,128)(2,1)S(1)}, u32[]{:S(2)}, u32[]{:S(2)}) collective-permute-start(bf16[256,1024]{1,0:T(8,128)(2,1)S(1)} %get-tuple-element.440), channel_id=1, source_target_pairs={{0,4},{1,5},{2,6},{3,7},{4,0},{5,1},{6,2},{7,3},{8,12},{9,13},{10,... | collective-permute-start | bytes 1572872 | tf_op jit(solution)/shard_map/ppermute | solution.py:26
  71.2 5.6 %collective-permute-done.17.b1 = bf16[256,1024]{1,0:T(8,128)(2,1)S(1)} collective-permute-done((bf16[256,1024]{1,0:T(8,128)(2,1)S(1)}, bf16[256,1024]{1,0:T(8,128)(2,1)S(1)}, u32[]{:S(2)}, u32[]{:S(2)}) %collective-permute-start.17) | collective-permute-done | bytes 524320 | tf_op jit(solution)/shard_map/ppermute | solution.py:26
  76.8 0.2 merge.1
  77.1 0.5 collective-permute-start.18
  77.6 0.1 fold.5
  77.7 2.0 %collective-permute-start.23 = (bf16[128,1024]{1,0:T(8,128)(2,1)S(1)}, bf16[128,1024]{1,0:T(8,128)(2,1)S(1)}, u32[]{:S(2)}, u32[]{:S(2)}) collective-permute-start(bf16[128,1024]{1,0:T(8,128)(2,1)S(1)} %get-tuple-element.471), channel_id=1, source_target_pairs={{0,4},{1,5},{2,6},{3,7},{4,0},{5,1},{6,2},{7,3},{8,12},{9,13},{10,... | collective-permute-start | bytes 786440 | tf_op jit(solution)/shard_map/ppermute | solution.py:26
  79.8 8.3 %collective-permute-done.19.b_ref = bf16[256,1024]{1,0:T(8,128)(2,1)S(1)} collective-permute-done((bf16[256,1024]{1,0:T(8,128)(2,1)S(1)}, bf16[256,1024]{1,0:T(8,128)(2,1)S(1)}, u32[]{:S(2)}, u32[]{:S(2)}) %collective-permute-start.19) | collective-permute-done | bytes 524320 | tf_op jit(solution)/shard_map/ppermute | solution.py:26
  88.1 0.1 fold.6
  88.2 0.5 collective-permute-start.22
  88.8 0.1 fold.7
  88.9 3.4 %collective-permute-start.21 = (bf16[128,1024]{1,0:T(8,128)(2,1)S(1)}, bf16[128,1024]{1,0:T(8,128)(2,1)S(1)}, u32[]{:S(2)}, u32[]{:S(2)}) collective-permute-start(bf16[128,1024]{1,0:T(8,128)(2,1)S(1)} %get-tuple-element.467), channel_id=1, source_target_pairs={{0,8},{1,9},{2,10},{3,11},{4,12},{5,13},{6,14},{7,15},{8,0},{9,1},... | collective-permute-start | bytes 786440 | tf_op jit(solution)/shard_map/ppermute | solution.py:26
  92.3 4.5 %collective-permute-done.23.b_ref = bf16[128,1024]{1,0:T(8,128)(2,1)S(1)} collective-permute-done((bf16[128,1024]{1,0:T(8,128)(2,1)S(1)}, bf16[128,1024]{1,0:T(8,128)(2,1)S(1)}, u32[]{:S(2)}, u32[]{:S(2)}) %collective-permute-start.23) | collective-permute-done | bytes 262176 | tf_op jit(solution)/shard_map/ppermute | solution.py:26
  96.8 0.1 fold.8
  96.9 0.1 fold.9
  97.0 5.2 %collective-permute-done.21.refs_1_ = bf16[128,1024]{1,0:T(8,128)(2,1)S(1)} collective-permute-done((bf16[128,1024]{1,0:T(8,128)(2,1)S(1)}, bf16[128,1024]{1,0:T(8,128)(2,1)S(1)}, u32[]{:S(2)}, u32[]{:S(2)}) %collective-permute-start.21) | collective-permute-done | bytes 262176 | tf_op jit(solution)/shard_map/ppermute | solution.py:26
  102.3 1.4 %input_nb.1 = bf16[512,1024]{1,0:T(8,128)(2,1)S(1)} custom-call(bf16[2,512,512]{2,1,0:T(8,128)(2,1)S(1)} %get-tuple-element.390.pre0, bf16[2,512,512]{2,1,0:T(8,128)(2,1)S(1)} %get-tuple-element.419.pre1, bf16[512,1024]{1,0:T(8,128)(2,1)S(1)} %join.20.w0, bf16[512,1024]{1,0:T(8,128)(2,1)S(1)} %collective-permute-done.15.w1), custom_call_target="tpu_custom_call" | custom-call | tf_op jit(solution)/shard_map/input_nb/pallas_call | solution.py:297
  103.7 0.1 collective-permute-start.24
  103.8 0.1 collective-permute-start.25
  103.9 2.9 %collective-permute-start.26 = (bf16[64,1024]{1,0:T(8,128)(2,1)S(1)}, bf16[64,1024]{1,0:T(8,128)(2,1)S(1)}, u32[]{:S(2)}, u32[]{:S(2)}) collective-permute-start(bf16[64,1024]{1,0:T(8,128)(2,1)S(1)} %get-tuple-element.501), channel_id=1, source_target_pairs={{0,8},{1,9},{2,10},{3,11},{4,12},{5,13},{6,14},{7,15},{8,0},{9,1},... | collective-permute-start | bytes 393224 | tf_op jit(solution)/shard_map/ppermute | solution.py:26
  106.8 1.4 %total.3 = f32[128,1024]{1,0:T(8,128)} custom-call(s32[2]{0:T(128)S(1)} %copy-done.6, bf16[128,1024]{1,0:T(8,128)(2,1)S(1)} %get-tuple-element.507.refs_0_, bf16[128,1024]{1,0:T(8,128)(2,1)S(1)} %collective-permute-done.21.refs_1_, f32[8,128]{1,0:T(8,128)S(1)} %tick.33.mark_ref.refs_4_.refs_2_), custom_call_target="tpu_custom_call" | custom-call | tf_op jit(solution)/shard_map/total/pallas_call | solution.py:422
  108.2 2.3 %input_own.1 = bf16[512,1024]{1,0:T(8,128)(2,1)} custom-call(bf16[2,512,512]{2,1,0:T(8,128)(2,1)S(1)} %get-tuple-element.390.pre0, bf16[2,512,512]{2,1,0:T(8,128)(2,1)S(1)} %get-tuple-element.419.pre1, bf16[512,1024]{1,0:T(8,128)(2,1)S(1)} %join.20.w0, bf16[512,1024]{1,0:T(8,128)(2,1)S(1)} %collective-permute-done.15.w1, ...), custom_call_target="tpu_custom_call" | custom-call | tf_op jit(solution)/shard_map/input_own/pallas_call | solution.py:297
  110.4 6.2 %collective-permute-done.25.refs_1_ = bf16[64,1024]{1,0:T(8,128)(2,1)S(1)} collective-permute-done((bf16[64,1024]{1,0:T(8,128)(2,1)S(1)}, bf16[64,1024]{1,0:T(8,128)(2,1)S(1)}, u32[]{:S(2)}, u32[]{:S(2)}) %collective-permute-start.25) | collective-permute-done | bytes 131104 | tf_op jit(solution)/shard_map/ppermute | solution.py:26
  116.7 2.4 %collective-permute-done.26.refs_3_ = bf16[64,1024]{1,0:T(8,128)(2,1)S(1)} collective-permute-done((bf16[64,1024]{1,0:T(8,128)(2,1)S(1)}, bf16[64,1024]{1,0:T(8,128)(2,1)S(1)}, u32[]{:S(2)}, u32[]{:S(2)}) %collective-permute-start.26) | collective-permute-done | bytes 131104 | tf_op jit(solution)/shard_map/ppermute | solution.py:26
  119.0 1.4 %total.2 = f32[128,1024]{1,0:T(8,128)} custom-call(s32[2]{0:T(128)S(1)} %copy-done.6, bf16[64,1024]{1,0:T(8,128)(2,1)S(1)} %get-tuple-element.499.refs_0_, bf16[64,1024]{1,0:T(8,128)(2,1)S(1)} %collective-permute-done.25.refs_1_, bf16[64,1024]{1,0:T(8,128)(2,1)S(1)} %get-tuple-element.504.refs_2_, bf16[64,1024]{1,0:T(8,128)(2,1)S(1)} %collective-permute-done.26.refs_3_, ...), custom_call_target="tpu_custom_call" | custom-call | tf_op jit(solution)/shard_map/total/pallas_call | solution.py:422
  (53 shorter events, 0.3 us)
Async XLA Ops:
  0.6 33.1 %collective-permute-start = (bf16[512,2048]{1,0:T(8,128)(2,1)}, bf16[512,2048]{1,0:T(8,128)(2,1)}, u32[]{:S(2)}, u32[]{:S(2)}) collective-permute-start(bf16[512,2048]{1,0:T(8,128)(2,1)} %in_ref), channel_id=1, source_target_pairs={{0,1},{1,0},{2,3},{3,2},{4,5},{5,4},{6,7},{7,6},{8,9},{9,8},{10,11... | collective-permute-start | bytes 6291464 | tf_op jit(solution)/shard_map/ppermute | solution.py:26
  1.1 29.1 %collective-permute-start.2 = (bf16[512,1024]{1,0:T(8,128)(2,1)}, bf16[512,1024]{1,0:T(8,128)(2,1)}, u32[]{:S(2)}, u32[]{:S(2)}) collective-permute-start(bf16[512,1024]{1,0:T(8,128)(2,1)} %own_ref.2), channel_id=1, source_target_pairs={{0,1},{1,0},{2,3},{3,2},{4,5},{5,4},{6,7},{7,6},{8,9},{9,8},{10,11... | collective-permute-start | bytes 3145736 | tf_op jit(solution)/shard_map/ppermute | solution.py:26
  1.2 32.5 %collective-permute-start.1 = (bf16[512,1024]{1,0:T(8,128)(2,1)}, bf16[512,1024]{1,0:T(8,128)(2,1)}, u32[]{:S(2)}, u32[]{:S(2)}) collective-permute-start(bf16[512,1024]{1,0:T(8,128)(2,1)} %own_ref), channel_id=1, source_target_pairs={{0,1},{1,0},{2,3},{3,2},{4,5},{5,4},{6,7},{7,6},{8,9},{9,8},{10,11... | collective-permute-start | bytes 3145736 | tf_op jit(solution)/shard_map/ppermute | solution.py:26
  2.7 10.6 %collective-permute-start.3 = (bf16[64,1024]{1,0:T(8,128)(2,1)S(1)}, bf16[64,1024]{1,0:T(8,128)(2,1)S(1)}, u32[]{:S(2)}, u32[]{:S(2)}) collective-permute-start(bf16[64,1024]{1,0:T(8,128)(2,1)S(1)} %get-tuple-element.269.a_ref), channel_id=1, source_target_pairs={{0,8},{1,9},{2,10},{3,11},{4,12},{5,13},{6,14},{7,15},{8,0},{9,1},... | collective-permute-start | bytes 393224 | tf_op jit(solution)/shard_map/ppermute | solution.py:26
  10.6 9.4 %copy-start.3 = (bf16[8,1024]{1,0:T(8,128)(2,1)S(1)}, bf16[8,1024]{1,0:T(8,128)(2,1)}, u32[]{:S(2)}) copy-start(bf16[8,1024]{1,0:T(8,128)(2,1)} %pack.1.a_ref) | copy-start | bytes 49156
  13.3 13.1 %collective-permute-start.7 = (bf16[128,1024]{1,0:T(8,128)(2,1)S(1)}, bf16[128,1024]{1,0:T(8,128)(2,1)S(1)}, u32[]{:S(2)}, u32[]{:S(2)}) collective-permute-start(bf16[128,1024]{1,0:T(8,128)(2,1)S(1)} %join.11.a_ref), channel_id=1, source_target_pairs={{0,4},{1,5},{2,6},{3,7},{4,0},{5,1},{6,2},{7,3},{8,12},{9,13},{10,... | collective-permute-start | bytes 786440 | tf_op jit(solution)/shard_map/ppermute | solution.py:26
  14.1 5.9 %collective-permute-start.4 = (bf16[8,1024]{1,0:T(8,128)(2,1)}, bf16[8,1024]{1,0:T(8,128)(2,1)S(1)}, u32[]{:S(2)}, u32[]{:S(2)}) collective-permute-start(bf16[8,1024]{1,0:T(8,128)(2,1)} %pack.1.a_ref), channel_id=1, source_target_pairs={{0,2},{1,3},{2,0},{3,1},{4,6},{5,7},{6,4},{7,5},{8,10},{9,11},{10,... | collective-permute-start | bytes 49160 | tf_op jit(solution)/shard_map/ppermute | solution.py:26
  15.7 1.6 %copy-start.2 = (bf16[512,2048]{1,0:T(8,128)(2,1)S(1)}, bf16[512,2048]{1,0:T(8,128)(2,1)}, u32[]{:S(2)}) copy-start(bf16[512,2048]{1,0:T(8,128)(2,1)} %in_ref) | copy-start | bytes 6291460
  17.3 0.7 copy-start.5
  20.1 5.3 %collective-permute-start.5 = (bf16[16,1024]{1,0:T(8,128)(2,1)S(1)}, bf16[16,1024]{1,0:T(8,128)(2,1)S(1)}, u32[]{:S(2)}, u32[]{:S(2)}) collective-permute-start(bf16[16,1024]{1,0:T(8,128)(2,1)S(1)} %join.12.a_ref), channel_id=1, source_target_pairs={{0,8},{1,9},{2,10},{3,11},{4,12},{5,13},{6,14},{7,15},{8,0},{9,1},... | collective-permute-start | bytes 98312 | tf_op jit(solution)/shard_map/ppermute | solution.py:26
  25.4 4.3 %collective-permute-start.6 = (bf16[32,1024]{1,0:T(8,128)(2,1)S(1)}, bf16[32,1024]{1,0:T(8,128)(2,1)S(1)}, u32[]{:S(2)}, u32[]{:S(2)}) collective-permute-start(bf16[32,1024]{1,0:T(8,128)(2,1)S(1)} %join.13.a_ref), channel_id=1, source_target_pairs={{0,4},{1,5},{2,6},{3,7},{4,0},{5,1},{6,2},{7,3},{8,12},{9,13},{10,... | collective-permute-start | bytes 196616 | tf_op jit(solution)/shard_map/ppermute | solution.py:26
  26.4 21.1 %collective-permute-start.11 = (bf16[256,1024]{1,0:T(8,128)(2,1)S(1)}, bf16[256,1024]{1,0:T(8,128)(2,1)S(1)}, u32[]{:S(2)}, u32[]{:S(2)}) collective-permute-start(bf16[256,1024]{1,0:T(8,128)(2,1)S(1)} %join.14.a_ref), channel_id=1, source_target_pairs={{0,16},{16,0},{1,17},{17,1},{2,18},{18,2},{3,19},{19,3},{4,20},{20... | collective-permute-start | bytes 1572872 | tf_op jit(solution)/shard_map/ppermute | solution.py:527
  29.8 17.8 %collective-permute-start.10 = (bf16[256,1024]{1,0:T(8,128)(2,1)S(1)}, bf16[256,1024]{1,0:T(8,128)(2,1)S(1)}, u32[]{:S(2)}, u32[]{:S(2)}) collective-permute-start(bf16[256,1024]{1,0:T(8,128)(2,1)S(1)} %join.14.a_ref), channel_id=1, source_target_pairs={{0,2},{1,3},{2,0},{3,1},{4,6},{5,7},{6,4},{7,5},{8,10},{9,11},{10,... | collective-permute-start | bytes 1572872 | tf_op jit(solution)/shard_map/ppermute | solution.py:26
  30.3 7.7 %collective-permute-start.9 = (bf16[64,1024]{1,0:T(8,128)(2,1)S(1)}, bf16[64,1024]{1,0:T(8,128)(2,1)S(1)}, u32[]{:S(2)}, u32[]{:S(2)}) collective-permute-start(bf16[64,1024]{1,0:T(8,128)(2,1)S(1)} %get-tuple-element.324.a_ref), channel_id=1, source_target_pairs={{0,8},{1,9},{2,10},{3,11},{4,12},{5,13},{6,14},{7,15},{8,0},{9,1},... | collective-permute-start | bytes 393224 | tf_op jit(solution)/shard_map/ppermute | solution.py:26
  33.7 5.9 %copy-start.1 = (bf16[512,1024]{1,0:T(8,128)(2,1)S(1)}, bf16[512,1024]{1,0:T(8,128)(2,1)}, u32[]{:S(2)}) copy-start(bf16[512,1024]{1,0:T(8,128)(2,1)} %own_ref) | copy-start | bytes 3145732
  33.7 5.9 %copy-start.4 = (f32[1024]{0:T(1024)S(1)}, f32[1024]{0:T(1024)}, u32[]{:S(2)}) copy-start(f32[1024]{0:T(1024)} %param.16) | copy-start | bytes 12292
  38.0 9.4 %collective-permute-start.12 = (bf16[128,1024]{1,0:T(8,128)(2,1)S(1)}, bf16[128,1024]{1,0:T(8,128)(2,1)S(1)}, u32[]{:S(2)}, u32[]{:S(2)}) collective-permute-start(bf16[128,1024]{1,0:T(8,128)(2,1)S(1)} %join.16.a_ref), channel_id=1, source_target_pairs={{0,4},{1,5},{2,6},{3,7},{4,0},{5,1},{6,2},{7,3},{8,12},{9,13},{10,... | collective-permute-start | bytes 786440 | tf_op jit(solution)/shard_map/ppermute | solution.py:26
  38.1 1.4 %collective-permute-start.8 = (bf16[64,1024]{1,0:T(8,128)(2,1)S(1)}, bf16[64,1024]{1,0:T(8,128)(2,1)S(1)}, u32[]{:S(2)}, u32[]{:S(2)}) collective-permute-start(bf16[64,1024]{1,0:T(8,128)(2,1)S(1)} %join.15.a_ref), channel_id=1, source_target_pairs={{0,1},{1,0},{2,3},{3,2},{4,5},{5,4},{6,7},{7,6},{8,9},{9,8},{10,11... | collective-permute-start | bytes 393224 | tf_op jit(solution)/shard_map/ppermute | solution.py:26
  47.4 5.3 %copy-start = (bf16[512,1024]{1,0:T(8,128)(2,1)S(1)}, bf16[512,1024]{1,0:T(8,128)(2,1)}, u32[]{:S(2)}) copy-start(bf16[512,1024]{1,0:T(8,128)(2,1)} %own_ref.2) | copy-start | bytes 3145732
  47.6 14.0 %collective-permute-start.14 = (bf16[256,1024]{1,0:T(8,128)(2,1)S(1)}, bf16[256,1024]{1,0:T(8,128)(2,1)S(1)}, u32[]{:S(2)}, u32[]{:S(2)}) collective-permute-start(bf16[256,1024]{1,0:T(8,128)(2,1)S(1)} %join.18.a_ref), channel_id=1, source_target_pairs={{0,2},{1,3},{2,0},{3,1},{4,6},{5,7},{6,4},{7,5},{8,10},{9,11},{10,... | collective-permute-start | bytes 1572872 | tf_op jit(solution)/shard_map/ppermute | solution.py:26
  49.3 15.6 %collective-permute-start.13 = (bf16[256,1024]{1,0:T(8,128)(2,1)S(1)}, bf16[256,1024]{1,0:T(8,128)(2,1)S(1)}, u32[]{:S(2)}, u32[]{:S(2)}) collective-permute-start(bf16[256,1024]{1,0:T(8,128)(2,1)S(1)} %collective-permute-done.10.b_ref), channel_id=1, source_target_pairs={{0,16},{16,0},{1,17},{17,1},{2,18},{18,2},{3,19},{19,3},{4,20},{20... | collective-permute-start | bytes 1572872 | tf_op jit(solution)/shard_map/ppermute | solution.py:527
  50.8 20.4 %collective-permute-start.16 = (bf16[256,1024]{1,0:T(8,128)(2,1)S(1)}, bf16[256,1024]{1,0:T(8,128)(2,1)S(1)}, u32[]{:S(2)}, u32[]{:S(2)}) collective-permute-start(bf16[256,1024]{1,0:T(8,128)(2,1)S(1)} %get-tuple-element.422), channel_id=1, source_target_pairs={{0,4},{1,5},{2,6},{3,7},{4,0},{5,1},{6,2},{7,3},{8,12},{9,13},{10,... | collective-permute-start | bytes 1572872 | tf_op jit(solution)/shard_map/ppermute | solution.py:26
  56.9 19.9 %collective-permute-start.17 = (bf16[256,1024]{1,0:T(8,128)(2,1)S(1)}, bf16[256,1024]{1,0:T(8,128)(2,1)S(1)}, u32[]{:S(2)}, u32[]{:S(2)}) collective-permute-start(bf16[256,1024]{1,0:T(8,128)(2,1)S(1)} %get-tuple-element.424), channel_id=1, source_target_pairs={{0,4},{1,5},{2,6},{3,7},{4,0},{5,1},{6,2},{7,3},{8,12},{9,13},{10,... | collective-permute-start | bytes 1572872 | tf_op jit(solution)/shard_map/ppermute | solution.py:26
  61.7 40.5 %collective-permute-start.15 = (bf16[512,1024]{1,0:T(8,128)(2,1)S(1)}, bf16[512,1024]{1,0:T(8,128)(2,1)S(1)}, u32[]{:S(2)}, u32[]{:S(2)}) collective-permute-start(bf16[512,1024]{1,0:T(8,128)(2,1)S(1)} %join.20.w0), channel_id=1, source_target_pairs={{0,16},{16,0},{1,17},{17,1},{2,18},{18,2},{3,19},{19,3},{4,20},{20... | collective-permute-start | bytes 3145736 | tf_op jit(solution)/shard_map/ppermute | solution.py:527
  63.3 14.3 %collective-permute-start.20 = (bf16[256,1024]{1,0:T(8,128)(2,1)S(1)}, bf16[256,1024]{1,0:T(8,128)(2,1)S(1)}, u32[]{:S(2)}, u32[]{:S(2)}) collective-permute-start(bf16[256,1024]{1,0:T(8,128)(2,1)S(1)} %get-tuple-element.442), channel_id=1, source_target_pairs={{0,2},{1,3},{2,0},{3,1},{4,6},{5,7},{6,4},{7,5},{8,10},{9,11},{10,... | collective-permute-start | bytes 1572872 | tf_op jit(solution)/shard_map/ppermute | solution.py:26
  69.2 18.9 %collective-permute-start.19 = (bf16[256,1024]{1,0:T(8,128)(2,1)S(1)}, bf16[256,1024]{1,0:T(8,128)(2,1)S(1)}, u32[]{:S(2)}, u32[]{:S(2)}) collective-permute-start(bf16[256,1024]{1,0:T(8,128)(2,1)S(1)} %get-tuple-element.440), channel_id=1, source_target_pairs={{0,4},{1,5},{2,6},{3,7},{4,0},{5,1},{6,2},{7,3},{8,12},{9,13},{10,... | collective-permute-start | bytes 1572872 | tf_op jit(solution)/shard_map/ppermute | solution.py:26
  77.1 11.7 %collective-permute-start.18 = (bf16[256,1024]{1,0:T(8,128)(2,1)S(1)}, bf16[256,1024]{1,0:T(8,128)(2,1)S(1)}, u32[]{:S(2)}, u32[]{:S(2)}) collective-permute-start(bf16[256,1024]{1,0:T(8,128)(2,1)S(1)} %get-tuple-element.438), channel_id=1, source_target_pairs={{0,2},{1,3},{2,0},{3,1},{4,6},{5,7},{6,4},{7,5},{8,10},{9,11},{10,... | collective-permute-start | bytes 1572872 | tf_op jit(solution)/shard_map/ppermute | solution.py:26
  77.7 19.1 %collective-permute-start.23 = (bf16[128,1024]{1,0:T(8,128)(2,1)S(1)}, bf16[128,1024]{1,0:T(8,128)(2,1)S(1)}, u32[]{:S(2)}, u32[]{:S(2)}) collective-permute-start(bf16[128,1024]{1,0:T(8,128)(2,1)S(1)} %get-tuple-element.471), channel_id=1, source_target_pairs={{0,4},{1,5},{2,6},{3,7},{4,0},{5,1},{6,2},{7,3},{8,12},{9,13},{10,... | collective-permute-start | bytes 786440 | tf_op jit(solution)/shard_map/ppermute | solution.py:26
  88.2 8.7 %collective-permute-start.22 = (bf16[128,1024]{1,0:T(8,128)(2,1)S(1)}, bf16[128,1024]{1,0:T(8,128)(2,1)S(1)}, u32[]{:S(2)}, u32[]{:S(2)}) collective-permute-start(bf16[128,1024]{1,0:T(8,128)(2,1)S(1)} %get-tuple-element.469), channel_id=1, source_target_pairs={{0,2},{1,3},{2,0},{3,1},{4,6},{5,7},{6,4},{7,5},{8,10},{9,11},{10,... | collective-permute-start | bytes 786440 | tf_op jit(solution)/shard_map/ppermute | solution.py:26
  88.9 13.4 %collective-permute-start.21 = (bf16[128,1024]{1,0:T(8,128)(2,1)S(1)}, bf16[128,1024]{1,0:T(8,128)(2,1)S(1)}, u32[]{:S(2)}, u32[]{:S(2)}) collective-permute-start(bf16[128,1024]{1,0:T(8,128)(2,1)S(1)} %get-tuple-element.467), channel_id=1, source_target_pairs={{0,8},{1,9},{2,10},{3,11},{4,12},{5,13},{6,14},{7,15},{8,0},{9,1},... | collective-permute-start | bytes 786440 | tf_op jit(solution)/shard_map/ppermute | solution.py:26
  97.0 9.8 %copy-start.6 = (s32[2]{0:T(128)S(1)}, s32[2]{0:T(128)}, u32[]{:S(2)}) copy-start(s32[2]{0:T(128)} %pad_add_fusion.ids_ref) | copy-start | bytes 28
  103.7 4.5 %collective-permute-start.24 = (bf16[512,1024]{1,0:T(8,128)(2,1)S(1)}, bf16[512,1024]{1,0:T(8,128)(2,1)S(1)}, u32[]{:S(2)}, u32[]{:S(2)}) collective-permute-start(bf16[512,1024]{1,0:T(8,128)(2,1)S(1)} %input_nb.1), channel_id=1, source_target_pairs={{0,1},{1,0},{2,3},{3,2},{4,5},{5,4},{6,7},{7,6},{8,9},{9,8},{10,11... | collective-permute-start | bytes 3145736 | tf_op jit(solution)/shard_map/ppermute | solution.py:26
  103.8 12.9 %collective-permute-start.25 = (bf16[64,1024]{1,0:T(8,128)(2,1)S(1)}, bf16[64,1024]{1,0:T(8,128)(2,1)S(1)}, u32[]{:S(2)}, u32[]{:S(2)}) collective-permute-start(bf16[64,1024]{1,0:T(8,128)(2,1)S(1)} %get-tuple-element.500), channel_id=1, source_target_pairs={{0,8},{1,9},{2,10},{3,11},{4,12},{5,13},{6,14},{7,15},{8,0},{9,1},... | collective-permute-start | bytes 393224 | tf_op jit(solution)/shard_map/ppermute | solution.py:26
  103.9 15.2 %collective-permute-start.26 = (bf16[64,1024]{1,0:T(8,128)(2,1)S(1)}, bf16[64,1024]{1,0:T(8,128)(2,1)S(1)}, u32[]{:S(2)}, u32[]{:S(2)}) collective-permute-start(bf16[64,1024]{1,0:T(8,128)(2,1)S(1)} %get-tuple-element.501), channel_id=1, source_target_pairs={{0,8},{1,9},{2,10},{3,11},{4,12},{5,13},{6,14},{7,15},{8,0},{9,1},... | collective-permute-start | bytes 393224 | tf_op jit(solution)/shard_map/ppermute | solution.py:26

commit v3 on v2

--- a/solution.py
+++ b/solution.py
@@ -9,6 +9,16 @@
 
 LEN = 128
 TICK = 100_000_000
+SCHEDULE = (
+    "inp>", "pre>", "resid>", "states>", "out>", "pack", "out:1", "out>", "resid?", "small>",
+    "gelu0", "small:1", "small>", "inp:1", "out:1", "out>", "xa", "ia?", "small:30", "small>",
+    "inp>", "gelu1", "small:30", "small>", "states?", "small:1", "resid", "out:1", "xa?", "ib?",
+    "xb", "inp:1", "inp>", "gi0", "xa?", "go1", "ia?", "go0", "go0>", "gi0>", "inp:1", "wout",
+    "gi1", "go1>", "gi1>", "ia", "go0:1", "go0>", "gi0", "ia?", "gi0>", "ib", "go1:1", "go1>",
+    "gi1:1", "gi1>", "go0:1", "gi0", "gi0>", "go0>", "win", "nb0", "go1:1", "go1>", "nb1", "go0?",
+    "gi1:30", "gi1>", "gi0?", "nb?", "own", "tgo", "tgi",
+)
+ORDERS = {"out": "down", "inp": "far", "go0": "side", "go1": "far", "gi0": "up", "gi1": "side"}
 BF = jnp.bfloat16
 F32 = jnp.float32
 PACK_MIB = 63
@@ -282,30 +292,56 @@
     out_ref[...] = total.astype(BF)
 
 
-def input_own_kernel(pre0, pre1, w0, w1, resid_ref, nb_ref, mark_ref, out_ref):
+def input_own_kernel(pre0, pre1, w0, w1, resid_ref, first_ref, second_ref, mark_ref, out_ref):
     total = jnp.dot(pre0[0], w0[...], preferred_element_type=F32)
     total = total + jnp.dot(pre1[0], w1[...], preferred_element_type=F32)
-    out_ref[...] = (total + nb_ref[...].astype(F32) + resid_ref[0].astype(F32)).astype(BF)
-
-
-def input_part(pre, w_in, which, extra):
+    total = total + resid_ref[0].astype(F32)
+
+    @pl.when(pl.program_id(0) == 0)
+    def _():
+        out_ref[...] = (total + first_ref[...].astype(F32)).astype(BF)
+
+    @pl.when(pl.program_id(0) == 1)
+    def _():
+        out_ref[...] = (total + second_ref[...].astype(F32)).astype(BF)
+
+
+def input_nb(pre, w_in, part):
     _, tokens, units = pre[0].shape
     width = w_in[0].shape[1]
-    block = 256
-    row = pl.BlockSpec((block, width), lambda i: (i, 0))
-    first = pl.BlockSpec((1, block, width), lambda i: (0, i, 0))
-    return pl.pallas_call(
-        input_own_kernel if extra else input_nb_kernel,
-        grid=(tokens // block,),
-        in_specs=[pl.BlockSpec((1, block, units), lambda i: (which, i, 0))] * 2
-        + [pl.BlockSpec((units, width), lambda i: (0, 0))] * 2
-        + [first, row, pl.BlockSpec(memory_space=pl.ANY)][: len(extra)],
-        out_specs=row,
+    block = tokens // 2
+    return pl.pallas_call(
+        input_nb_kernel,
+        grid=(1,),
+        in_specs=[pl.BlockSpec((1, block, units), lambda i: (1, part, 0))] * 2
+        + [pl.BlockSpec((units, width), lambda i: (0, 0))] * 2,
+        out_specs=pl.BlockSpec((block, width), lambda i: (0, 0)),
+        out_shape=jax.ShapeDtypeStruct((block, width), BF),
+        compiler_params=params(12),
+        cost_estimate=FREE,
+        name="input_nb",
+    )(*pre, *w_in)
+
+
+def input_own(pre, w_in, resid, first, second, mark):
+    _, tokens, units = pre[0].shape
+    width = w_in[0].shape[1]
+    block = tokens // 2
+    whole = lambda i: (0, 0)
+    return pl.pallas_call(
+        input_own_kernel,
+        grid=(2,),
+        in_specs=[pl.BlockSpec((1, block, units), lambda i: (0, i, 0))] * 2
+        + [pl.BlockSpec((units, width), whole)] * 2
+        + [pl.BlockSpec((1, block, width), lambda i: (0, i, 0))]
+        + [pl.BlockSpec((block, width), whole)] * 2
+        + [pl.BlockSpec(memory_space=pl.ANY)],
+        out_specs=pl.BlockSpec((block, width), lambda i: (i, 0)),
         out_shape=jax.ShapeDtypeStruct((tokens, width), BF),
-        compiler_params=params(14),
-        cost_estimate=FREE,
-        name="input_own" if extra else "input_nb",
-    )(*pre, *w_in, *extra)
+        compiler_params=params(16),
+        cost_estimate=FREE,
+        name="input_own",
+    )(*pre, *w_in, resid, first, second, mark)
 
 
 def tick_kernel(in_ref, out_ref):
@@ -392,18 +428,6 @@
     return run(functools.partial(fold_kernel, rows), "fold", [(total // 2, width)] * 2, a, b)
 
 
-def merge_kernel(rows, a0, b0, a1, b1, keep_ref, sent_ref):
-    for k, (a, b) in enumerate(((a0, b0), (a1, b1))):
-        count = a.shape[0] // 2
-        part = slice(k * count, (k + 1) * count)
-        keep_ref[part], sent_ref[part] = halves(a[...].astype(F32) + b[...].astype(F32), rows)
-
-
-def merge(a0, b0, a1, b1, rows):
-    total, width = a0.shape
-    return run(functools.partial(merge_kernel, rows), "merge", [(total, width)] * 2, a0, b0, a1, b1)
-
-
 def total_kernel(ids_ref, *refs):
     *parts, mark_ref, out_ref = refs
     rows = out_ref.shape[0] // 2
@@ -429,66 +453,61 @@
     )(ids, *parts, mark)
 
 
-class Gather:
+class Chain:
+    def __init__(self, order, masks, rows):
+        self.order, self.left, self.done, self.rows = order, list(masks), [], rows
+        self.steps = 3
+
+    def due(self, last):
+        self.steps -= 1
+        while len(self.left) > max(self.steps, last):
+            yield self.left[0]
+
+
+class Gather(Chain):
     def __init__(self, order, x, masks):
-        self.order, self.x, self.todo, self.done = order, x, list(masks), []
-        self.rows = x.shape[0]
+        super().__init__(order, masks, x.shape[0])
+        self.x = x
+        self.steps = min(len(self.left), 4 if masks[-1] == 1 else 3)
 
     def send(self):
-        if self.todo:
-            self.came = swap(*self.order.gate(self.x), self.todo[0])
-
-    def block(self, mask):
-        return self.rows << (len(self.done) - place(mask, self.done))
-
-    def step(self, send=True, ticks=1):
-        mask = self.todo.pop(0)
-        rows = self.block(mask)
-        self.x = self.order(lambda a, b: join(a, b, rows), self.x, self.came, ticks=ticks)
-        self.done.append(mask)
-        self.arrived = self.came
-        if send:
-            self.send()
-
-    def until(self, left, send=True, ticks=1):
-        while len(self.todo) > left:
-            self.step(send or len(self.todo) > left + 1, ticks)
-
-
-class Scatter:
-    def __init__(self, order, make, rows, masks):
-        self.order, self.make, self.rows, self.left = order, make, rows, list(masks)
-
+        self.came = swap(*self.order.gate(self.x), self.left[0])
+
+    def step(self, ticks):
+        first = True
+        for mask in self.due(0):
+            if not first:
+                self.send()
+            first = False
+            rows = self.rows << (len(self.done) - place(mask, self.done))
+            self.before, self.arrived, self.block = self.x, self.came, rows
+            self.x = self.order(lambda a, b: join(a, b, rows), self.x, self.came, ticks=ticks)
+            self.done.append(self.left.pop(0))
+
+
+class Scatter(Chain):
     def block(self):
         return self.rows << (len(self.left) - 1 - place(self.left[0], self.left))
 
-    def start(self, *args, send=True):
+    def start(self, make, *args):
         rows = self.block()
-        *extra, self.keep, self.sent = self.order(lambda *x: self.make(rows, *x), *args, ticks=0)
-        if send:
-            self.send()
+        *extra, self.keep, self.sent = self.order(lambda *x: make(rows, *x), *args, ticks=0)
         return extra
 
     def send(self):
         self.came = swap(*self.order.gate(self.sent), self.left[0])
 
-    def step(self):
-        self.left.pop(0)
-        rows = self.block()
-        self.keep, self.sent = self.order(lambda a, b: fold(a, b, rows), self.keep, self.came)
-        self.send()
-
-    def absorb(self, other):
-        self.left.pop(0)
-        rows = self.block()
-        self.keep, self.sent = self.order(
-            lambda *x: merge(*x, rows), self.keep, self.came, other.keep, other.came
-        )
-        self.send()
-
-    def until(self, left):
-        while len(self.left) > left:
-            self.step()
+    def step(self, ticks):
+        first = True
+        for _ in self.due(1):
+            if not first:
+                self.send()
+            first = False
+            self.left.pop(0)
+            rows = self.block()
+            self.keep, self.sent = self.order(
+                lambda a, b: fold(a, b, rows), self.keep, self.came, ticks=ticks
+            )
 
 
 def shards(
@@ -517,8 +536,14 @@
     slots = tokens // LEN
     queries = query_emb.shape[0]
     masks = [1 << b for b in range(1, n.bit_length() - 1)]
-    up, down = masks, masks[::-1]
-    side = masks[1::-1] + masks[2:]
+    orders = {
+        "up": masks,
+        "down": masks[::-1],
+        "side": masks[1::-1] + masks[2:],
+        "far": masks[:1] + masks[:0:-1],
+        "mixed": masks[1:2] + masks[:1:-1] + masks[:1],
+        "low": masks[:1:-1] + masks[:2],
+    }
     gain = norm_gain.reshape(1, width)
     whole_tiles = rows == 128
     order = Order(jnp.zeros((8, 128), F32) + me.astype(F32))
@@ -536,77 +561,89 @@
     mine_out, mine_in = (
         lax.dynamic_slice_in_dim(w, group * (rows // 2), rows // 2, 0) for w in (w_out, w_in)
     )
-    out = Gather(order, mine_out, down)
-    inp = Gather(order, mine_in, down)
-    out.send()
-    preact_nb = swap(columns, 1)
-    resid_nb = swap(saved_resid, 1)
-    states_nb = swap(passage_states, 1)
-    table = order(
-        lambda *args: pack(slots, ids, *args),
-        placement_map, live_counts, saved_resid, gain, query_emb, score_grads, retrieved, ticks=0,
-    )
-
-    def core_gelu(x):
-        return order(lambda x: gelu(ids, x, units, half if whole_tiles else 0), x, ticks=0)
-
-    small = Gather(order, table, masks[:1] + masks[:0:-1] + [1])
-    last = len(down)
-    out.until(last - 1)
-    small.send()
-    own = core_gelu(preact_own)
-    inp.send()
-    small.until(last)
-    small.until(last - 1)
-    out.until(1)
-    early = cross(out.x)
-    small.until(1)
-    preact_nb, resid_nb, states_nb = order.gate(preact_nb, resid_nb, states_nb)
-    near = core_gelu(preact_nb)
-    inp.until(last - 1)
-    small.until(0)
-    resid_bf, question_grad = order(
-        lambda a, b, c: resid_grads(slots, queries, a, b, c, gain),
-        saved_resid, resid_nb, small.x, ticks=0,
-    )
-
-    side_rows = rows // 2
-    go0, go1 = (Scatter(order, grad_out_part, side_rows, side) for _ in range(2))
-    gi0 = Scatter(order, grad_in_part, side_rows, up)
-    gi1 = Scatter(order, grad_in_part, side_rows, side)
-    go0.start(own[0], near[0], resid_bf)
-    go1.start(own[1], near[1], resid_bf, send=False)
-    inp.until(1, send=False)
-    early, = order.gate(early)
-    out.until(0)
-    late = cross(out.arrived)
-    inp.send()
-    pre0, = gi0.start(resid_bf, out.x, own[2], near[2], passage_states, states_nb)
-    go1.send()
-    inp.until(0)
-    in0 = inp.x
-    in1 = cross(in0)
-    joined = out.rows << (len(down) - 1 - place(down[-1], down))
-    out1 = order(lambda a, b: join(a, b, joined), early, late)
-    pre1, = gi1.start(resid_bf, out1, own[3], near[3], passage_states, states_nb)
-    go0.absorb(go1)
-    gi0.step()
-    gi1.step()
-    go0.until(1)
-    gi0.until(1)
-    gi1.until(1)
-    go0.came, = order.gate(go0.came)
-
-    pre = (pre0, pre1)
-    sent = order(lambda a, b: input_part(pre, (a, b), 1, ()), in0, in1, ticks=0)
-    back = swap(sent, 1)
-    grad_out = total(ids, order.mark, go0)
-    back, = order.gate(back)
-    mark = order.mark
-    input_grad = order(lambda x: input_part(pre, (in0, in1), 0, (resid_bf, x, mark)), back, ticks=0)
-    gi0.came, gi1.came = order.gate(gi0.came, gi1.came)
-    grad_in = total(ids, order.mark, gi0, gi1)
-    return (input_grad, grad_in, grad_out, question_grad)
+    v, swapped = {}, {"pre": columns, "resid": saved_resid, "states": passage_states}
+    chains = {
+        "out": Gather(order, mine_out, orders[ORDERS["out"]]),
+        "inp": Gather(order, mine_in, orders[ORDERS["inp"]]),
+    }
+    for name in ("go0", "go1", "gi0", "gi1"):
+        chains[name] = Scatter(order, orders[ORDERS[name]], rows // 2)
+
+    def weight(chain, first, second):
+        return order(lambda a, b: join(a, b, chain.block), v.pop(first), v.pop(second), ticks=0)
+
+    for word in SCHEDULE:
+        name, _, ticks = word.partition(":")
+        ticks = int(ticks or 0)
+        chain = chains.get(name.rstrip(">"))
+        if name[:-1] in swapped and name.endswith(">"):
+            x = swapped[name[:-1]]
+            v[name[:-1]] = swap(*order.gate(x), 1) if ticks else swap(x, 1)
+        elif name.endswith(">"):
+            chain.send()
+        elif name.endswith("?"):
+            if name[:-1] in chains:
+                chain = chains[name[:-1]]
+                chain.came, = order.gate(chain.came)
+            for key in [k for k in v if k.startswith(name[:-1])]:
+                v[key], = order.gate(v[key])
+            if ticks:
+                order.mark = tick(order.mark, ticks)
+        elif name in ("out", "inp", "small"):
+            chain.step(ticks)
+        elif name == "pack":
+            table = order(
+                lambda *args: pack(slots, ids, *args),
+                placement_map, live_counts, saved_resid, gain, query_emb, score_grads, retrieved, ticks=0,
+            )
+            chains["small"] = Gather(order, table, orders["far"] + [1])
+        elif name in ("gelu0", "gelu1"):
+            x = preact_own if name == "gelu0" else v["pre"]
+            v[name] = order(lambda x: gelu(ids, x, units, half if whole_tiles else 0), x, ticks=0)
+        elif name == "resid":
+            resid_bf, question_grad = order(
+                lambda a, b, c: resid_grads(slots, queries, a, b, c, gain),
+                saved_resid, v["resid"], chains["small"].x, ticks=0,
+            )
+        elif name in ("go0", "go1", "gi0", "gi1"):
+            k = int(name[2])
+            if chain.steps < 3 or hasattr(chain, "keep"):
+                chain.step(ticks)
+            elif name[:2] == "go":
+                chain.start(grad_out_part, v["gelu0"][k], v["gelu1"][k], resid_bf)
+            else:
+                v["p%d" % k], = chain.start(
+                    grad_in_part, resid_bf, chains["out"].x if k == 0 else out1,
+                    v["gelu0"][2 + k], v["gelu1"][2 + k], passage_states, v["states"],
+                )
+        elif name == "xa":
+            v["xa"] = cross(*order.gate(chains["out"].x))
+        elif name == "xb":
+            v["xb"] = cross(*order.gate(chains["out"].arrived))
+        elif name == "ia":
+            v["ia"] = cross(*order.gate(chains["inp"].before if chains["inp"].steps == 0 else chains["inp"].x))
+        elif name == "ib":
+            v["ib"] = cross(*order.gate(chains["inp"].arrived))
+        elif name == "wout":
+            out1 = weight(chains["out"], "xa", "xb")
+        elif name == "win":
+            w_in = (chains["inp"].x, weight(chains["inp"], "ia", "ib"))
+        elif name in ("nb0", "nb1"):
+            k = int(name[2])
+            v[name] = swap(order(lambda *w: input_nb((v["p0"], v["p1"]), w, k), *w_in, ticks=0), 1)
+        elif name == "own":
+            mark = order.mark
+            input_grad = order(
+                lambda a, b: input_own((v["p0"], v["p1"]), w_in, resid_bf, a, b, mark), v["nb0"], v["nb1"],
+                ticks=0,
+            )
+        elif name in ("tgo", "tgi"):
+            pair = [chains[name[1:] + k] for k in "01"]
+            pair[0].came, pair[1].came = order.gate(pair[0].came, pair[1].came)
+            v[name] = total(ids, order.mark, *pair)
+        else:
+            raise ValueError(word)
+    return (input_grad, v["tgi"], v["tgo"], question_grad)
 
 
 def solution(mesh):

time: 121 us -> 109 us (0.901)
  waiting for transfers between devices: 45.1 us -> 30.3 us
  starting transfers between devices: 37 us -> 39.9 us
    ppermute x24 -> x27, waiting for transfers between devices: 45.1 us -> 23.6 us  [swap(): return lax.ppermute(x, 'psg', [(i, i ^ mask) for i in range(n)])]
    ppermute x3 -> x4, waiting for transfers between devices: 0.01 us -> 6.73 us  [cross(): return lax.ppermute(x, 'groups', [(0, 1), (1, 0)])]
    ppermute x3 -> x4, starting transfers between devices: 4.61 us -> 6.85 us  [cross(): return lax.ppermute(x, 'groups', [(0, 1), (1, 0)])]
    ppermute x24 -> x27, starting transfers between devices: 32.4 us -> 33.1 us  [swap(): return lax.ppermute(x, 'psg', [(i, i ^ mask) for i in range(n)])]
    pallas_call x2 -> x3, Pallas kernels: 3.69 us -> 3.83 us  [the longest x1 2.42 us: input_own(): pl.pallas_call(input_own_kernel, grid=(2,), in_specs=[pl.BlockSpec((1, bl...]
  transfers between devices with their start and end apart: 27 -> 31, of which waited for: 12 -> 13; matrix products, arithmetic and copies ran while one was open for 1% -> 1% of each run, Pallas kernels for 25% -> 28%
where the time goes in v3:
time: 109 us
  starting transfers between devices  39.9 us (37%)
  Pallas kernels  33.7 us (31%)
  waiting for transfers between devices  30.3 us (28%)
  local copies, waits for them, and re-layouts  3.26 us (3%)
    ppermute x27, starting transfers between devices, swap(): return lax.ppermute(x, 'psg', [(i, i ^ mask) for i in range(n)])  33.1 us
    ppermute x27, waiting for transfers between devices, swap(): return lax.ppermute(x, 'psg', [(i, i ^ mask) for i in range(n)])  23.6 us
    pallas_call x2, Pallas kernels, grad_in_part(): pl.pallas_call(functools.partial(grad_in_kernel, rows), grid=(units // bl...  8.39 us
    ppermute x4, starting transfers between devices, cross(): return lax.ppermute(x, 'groups', [(0, 1), (1, 0)])  6.85 us
    ppermute x4, waiting for transfers between devices, cross(): return lax.ppermute(x, 'groups', [(0, 1), (1, 0)])  6.73 us
    pallas_call x2, Pallas kernels, gelu(): pl.pallas_call(functools.partial(gelu_kernel, half), grid_spec=pltpu.Pref...  5.94 us
    pallas_call x1, Pallas kernels, resid_grads(): pl.pallas_call(functools.partial(resid_kernel, slots, queries), grid=(slo...  4.72 us
    pallas_call x1, Pallas kernels, pack(): pl.pallas_call(functools.partial(pack_kernel, slots), out_shape=jax.Shape...  3.69 us
  transfers between devices with their start and end apart: 31, of which 13 were waited for; matrix products, arithmetic and copies ran while one was open for 1% of the time, Pallas kernels for 28%

profile of v3, /device:TPU:0, one launch (start us, length us, event | category | flops | bytes accessed | tf_op | source)
XLA Modules:
  0.0 108.9 jit_solution(14857133599918475621)
XLA Ops:
  0.6 0.5 collective-permute-start.7
  1.1 0.1 collective-permute-start
  1.2 1.0 constant_dynamic-slice_fusion
  2.2 4.1 %collective-permute-start.1 = (bf16[64,1024]{1,0:T(8,128)(2,1)S(1)}, bf16[64,1024]{1,0:T(8,128)(2,1)S(1)}, u32[]{:S(2)}, u32[]{:S(2)}) collective-permute-start(bf16[64,1024]{1,0:T(8,128)(2,1)S(1)} %get-tuple-element.318.a_ref), channel_id=1, source_target_pairs={{0,8},{1,9},{2,10},{3,11},{4,12},{5,13},{6,14},{7,15},{8,0},{9,1},... | collective-permute-start | bytes 393224 | tf_op jit(solution)/shard_map/ppermute | solution.py:36
  6.3 0.6 pad_add_fusion.ids_ref
  6.9 3.7 %pack.1.a_ref = bf16[8,1024]{1,0:T(8,128)(2,1)} custom-call(s32[2]{0:T(128)} %pad_add_fusion.ids_ref, s32[64]{0:T(128)} %place_in, s32[16]{0:T(128)} %live_in, bf16[512,1024]{1,0:T(8,128)(2,1)} %own_ref, f32[1,1024]{1,0:T(1,128)} %bitcast.3, bf16[2,1024]{1,0:T(2,128)(2,1)} %query_in, bf16[2,32]{1,0:T(2,128)(2,1)} %score_in, s32[2,32]{1,0:T(2,128)} %ret_in), custom_call_target="tpu_custom_call" | custom-call | tf_op jit(solution)/shard_map/pack/pallas_call | solution.py:90
  10.6 2.3 %collective-permute-done.1.b_ref = bf16[64,1024]{1,0:T(8,128)(2,1)S(1)} collective-permute-done((bf16[64,1024]{1,0:T(8,128)(2,1)S(1)}, bf16[64,1024]{1,0:T(8,128)(2,1)S(1)}, u32[]{:S(2)}, u32[]{:S(2)}) %collective-permute-start.1) | collective-permute-done | bytes 131104 | tf_op jit(solution)/shard_map/ppermute | solution.py:36
  12.9 0.8 collective-permute-start.4
  13.7 1.5 %collective-permute-start.5 = (bf16[64,1024]{1,0:T(8,128)(2,1)S(1)}, bf16[64,1024]{1,0:T(8,128)(2,1)S(1)}, u32[]{:S(2)}, u32[]{:S(2)}) collective-permute-start(bf16[64,1024]{1,0:T(8,128)(2,1)S(1)} %get-tuple-element.345.a_ref), channel_id=1, source_target_pairs={{0,2},{1,3},{2,0},{3,1},{4,6},{5,7},{6,4},{7,5},{8,10},{9,11},{10,... | collective-permute-start | bytes 393224 | tf_op jit(solution)/shard_map/ppermute | solution.py:36
  15.2 0.5 collective-permute-start.2
  15.7 1.6 %copy-done.2 = bf16[512,2048]{1,0:T(8,128)(2,1)S(1)} copy-done((bf16[512,2048]{1,0:T(8,128)(2,1)S(1)}, bf16[512,2048]{1,0:T(8,128)(2,1)}, u32[]{:S(2)}) %copy-start.2) | copy-done | bytes 2097176
  17.3 0.7 copy-done.5
  18.0 2.1 %gelu.2 = (bf16[512,512]{1,0:T(8,128)(2,1)S(1)}, bf16[512,512]{1,0:T(8,128)(2,1)S(1)}, f32[512,512]{1,0:T(8,128)S(1)}, f32[512,512]{1,0:T(8,128)S(1)}) custom-call(s32[2]{0:T(128)S(1)} %copy-done.5, bf16[512,2048]{1,0:T(8,128)(2,1)S(1)} %copy-done.2), custom_call_target="tpu_custom_call" | custom-call | tf_op jit(solution)/shard_map/gelu/pallas_call | solution.py:201
  20.1 3.4 %collective-permute-start.3 = (bf16[16,1024]{1,0:T(8,128)(2,1)S(1)}, bf16[16,1024]{1,0:T(8,128)(2,1)S(1)}, u32[]{:S(2)}, u32[]{:S(2)}) collective-permute-start(bf16[16,1024]{1,0:T(8,128)(2,1)S(1)} %join.13.a_ref), channel_id=1, source_target_pairs={{0,8},{1,9},{2,10},{3,11},{4,12},{5,13},{6,14},{7,15},{8,0},{9,1},... | collective-permute-start | bytes 98312 | tf_op jit(solution)/shard_map/ppermute | solution.py:36
  23.7 1.6 %collective-permute-start.12 = (bf16[256,1024]{1,0:T(8,128)(2,1)S(1)}, bf16[256,1024]{1,0:T(8,128)(2,1)S(1)}, u32[]{:S(2)}, u32[]{:S(2)}) collective-permute-start(bf16[256,1024]{1,0:T(8,128)(2,1)S(1)} %join.15.a_ref), channel_id=1, source_target_pairs={{0,16},{16,0},{1,17},{17,1},{2,18},{18,2},{3,19},{19,3},{4,20},{20... | collective-permute-start | bytes 1572872 | tf_op jit(solution)/shard_map/ppermute | solution.py:552
  25.2 1.5 %collective-permute-start.10 = (bf16[256,1024]{1,0:T(8,128)(2,1)S(1)}, bf16[256,1024]{1,0:T(8,128)(2,1)S(1)}, u32[]{:S(2)}, u32[]{:S(2)}) collective-permute-start(bf16[256,1024]{1,0:T(8,128)(2,1)S(1)} %join.15.a_ref), channel_id=1, source_target_pairs={{0,2},{1,3},{2,0},{3,1},{4,6},{5,7},{6,4},{7,5},{8,10},{9,11},{10,... | collective-permute-start | bytes 1572872 | tf_op jit(solution)/shard_map/ppermute | solution.py:36
  26.8 0.1 collective-permute-start.6
  26.9 1.6 %collective-permute-start.11 = (bf16[128,1024]{1,0:T(8,128)(2,1)S(1)}, bf16[128,1024]{1,0:T(8,128)(2,1)S(1)}, u32[]{:S(2)}, u32[]{:S(2)}) collective-permute-start(bf16[128,1024]{1,0:T(8,128)(2,1)S(1)} %join.14.a_ref), channel_id=1, source_target_pairs={{0,8},{1,9},{2,10},{3,11},{4,12},{5,13},{6,14},{7,15},{8,0},{9,1},... | collective-permute-start | bytes 786440 | tf_op jit(solution)/shard_map/ppermute | solution.py:36
  28.6 3.8 %gelu.3 = (bf16[512,512]{1,0:T(8,128)(2,1)S(1)}, bf16[512,512]{1,0:T(8,128)(2,1)S(1)}, f32[512,512]{1,0:T(8,128)S(1)}, f32[512,512]{1,0:T(8,128)S(1)}) custom-call(s32[2]{0:T(128)S(1)} %copy-done.5, bf16[512,2048]{1,0:T(8,128)(2,1)} %collective-permute-done.7.in_ref), custom_call_target="tpu_custom_call" | custom-call | tf_op jit(solution)/shard_map/gelu/pallas_call | solution.py:201
  32.4 0.1 collective-permute-start.8
  32.5 1.3 %collective-permute-done.8.b_ref = bf16[64,1024]{1,0:T(8,128)(2,1)S(1)} collective-permute-done((bf16[64,1024]{1,0:T(8,128)(2,1)S(1)}, bf16[64,1024]{1,0:T(8,128)(2,1)S(1)}, u32[]{:S(2)}, u32[]{:S(2)}) %collective-permute-start.8) | collective-permute-done | bytes 131104 | tf_op jit(solution)/shard_map/ppermute | solution.py:36
  33.9 4.7 %resid_grads.1 = (bf16[2,512,1024]{2,1,0:T(8,128)(2,1)S(1)}, f32[2,1024]{1,0:T(2,128)}) custom-call(bf16[512,1024]{1,0:T(8,128)(2,1)S(1)} %copy-done.1, bf16[512,1024]{1,0:T(8,128)(2,1)} %collective-permute-done.nb_ref, bf16[128,1024]{1,0:T(8,128)(2,1)S(1)} %join.18.all_ref, f32[1,1024]{1,0:T(1,128)S(1)} %bitcast.4), custom_call_target="tpu_custom_call" | custom-call | tf_op jit(solution)/shard_map/resid_grads/pallas_call | solution.py:150
  38.7 1.3 %collective-permute-done.11.b_ref = bf16[128,1024]{1,0:T(8,128)(2,1)S(1)} collective-permute-done((bf16[128,1024]{1,0:T(8,128)(2,1)S(1)}, bf16[128,1024]{1,0:T(8,128)(2,1)S(1)}, u32[]{:S(2)}, u32[]{:S(2)}) %collective-permute-start.11) | collective-permute-done | bytes 262176 | tf_op jit(solution)/shard_map/ppermute | solution.py:36
  40.1 0.7 collective-permute-start.14
  40.8 1.8 %collective-permute-start.13 = (bf16[256,1024]{1,0:T(8,128)(2,1)S(1)}, bf16[256,1024]{1,0:T(8,128)(2,1)S(1)}, u32[]{:S(2)}, u32[]{:S(2)}) collective-permute-start(bf16[256,1024]{1,0:T(8,128)(2,1)S(1)} %collective-permute-done.10.b_ref), channel_id=1, source_target_pairs={{0,16},{16,0},{1,17},{17,1},{2,18},{18,2},{3,19},{19,3},{4,20},{20... | collective-permute-start | bytes 1572872 | tf_op jit(solution)/shard_map/ppermute | solution.py:552
  42.6 4.2 %grad_in.2 = (bf16[2,512,512]{2,1,0:T(8,128)(2,1)S(1)}, bf16[256,1024]{1,0:T(8,128)(2,1)S(1)}, bf16[256,1024]{1,0:T(8,128)(2,1)S(1)}) custom-call(bf16[2,512,1024]{2,1,0:T(8,128)(2,1)S(1)} %get-tuple-element.462.resid_ref, bf16[512,1024]{1,0:T(8,128)(2,1)S(1)} %join.19.w_ref, f32[512,512]{1,0:T(8,128)S(1)} %get-tuple-element.414.slope_own, ...), custom_call_target="tpu_custom_call" | custom-call | tf_op jit(solution)/shard_map/grad_in/pallas_call | solution.py:262
  46.8 1.6 %grad_out.2 = (bf16[256,1024]{1,0:T(8,128)(2,1)S(1)}, bf16[256,1024]{1,0:T(8,128)(2,1)S(1)}) custom-call(bf16[512,512]{1,0:T(8,128)(2,1)S(1)} %get-tuple-element.434.own_ref, bf16[512,512]{1,0:T(8,128)(2,1)S(1)} %get-tuple-element.435.nb_ref, bf16[2,512,1024]{2,1,0:T(8,128)(2,1)S(1)} %get-tuple-element.462.resid_ref), custom_call_target="tpu_custom_call" | custom-call | tf_op jit(solution)/shard_map/grad_out/pallas_call | solution.py:227
  48.4 1.6 %grad_out.3 = (bf16[256,1024]{1,0:T(8,128)(2,1)S(1)}, bf16[256,1024]{1,0:T(8,128)(2,1)S(1)}) custom-call(bf16[512,512]{1,0:T(8,128)(2,1)S(1)} %get-tuple-element.441.own_ref, bf16[512,512]{1,0:T(8,128)(2,1)S(1)} %get-tuple-element.442.nb_ref, bf16[2,512,1024]{2,1,0:T(8,128)(2,1)S(1)} %get-tuple-element.462.resid_ref), custom_call_target="tpu_custom_call" | custom-call | tf_op jit(solution)/shard_map/grad_out/pallas_call | solution.py:227
  50.0 1.6 %collective-permute-start.16 = (bf16[256,1024]{1,0:T(8,128)(2,1)S(1)}, bf16[256,1024]{1,0:T(8,128)(2,1)S(1)}, u32[]{:S(2)}, u32[]{:S(2)}) collective-permute-start(bf16[256,1024]{1,0:T(8,128)(2,1)S(1)} %get-tuple-element.481), channel_id=1, source_target_pairs={{0,2},{1,3},{2,0},{3,1},{4,6},{5,7},{6,4},{7,5},{8,10},{9,11},{10,... | collective-permute-start | bytes 1572872 | tf_op jit(solution)/shard_map/ppermute | solution.py:36
  51.6 0.1 collective-permute-start.17
  51.7 1.4 %collective-permute-done.14.b_ref = bf16[256,1024]{1,0:T(8,128)(2,1)S(1)} collective-permute-done((bf16[256,1024]{1,0:T(8,128)(2,1)S(1)}, bf16[256,1024]{1,0:T(8,128)(2,1)S(1)}, u32[]{:S(2)}, u32[]{:S(2)}) %collective-permute-start.14) | collective-permute-done | bytes 524320 | tf_op jit(solution)/shard_map/ppermute | solution.py:36
  53.2 1.4 %collective-permute-done.13.b_ref = bf16[256,1024]{1,0:T(8,128)(2,1)S(1)} collective-permute-done((bf16[256,1024]{1,0:T(8,128)(2,1)S(1)}, bf16[256,1024]{1,0:T(8,128)(2,1)S(1)}, u32[]{:S(2)}, u32[]{:S(2)}) %collective-permute-start.13) | collective-permute-done | bytes 524320 | tf_op jit(solution)/shard_map/ppermute | solution.py:552
  54.6 4.2 %grad_in.3 = (bf16[2,512,512]{2,1,0:T(8,128)(2,1)S(1)}, bf16[256,1024]{1,0:T(8,128)(2,1)S(1)}, bf16[256,1024]{1,0:T(8,128)(2,1)S(1)}) custom-call(bf16[2,512,1024]{2,1,0:T(8,128)(2,1)S(1)} %get-tuple-element.462.resid_ref, bf16[512,1024]{1,0:T(8,128)(2,1)S(1)} %join.22.w_ref, f32[512,512]{1,0:T(8,128)S(1)} %get-tuple-element.464.slope_own, ...), custom_call_target="tpu_custom_call" | custom-call | tf_op jit(solution)/shard_map/grad_in/pallas_call | solution.py:262
  58.8 1.8 %collective-permute-start.15 = (bf16[256,1024]{1,0:T(8,128)(2,1)S(1)}, bf16[256,1024]{1,0:T(8,128)(2,1)S(1)}, u32[]{:S(2)}, u32[]{:S(2)}) collective-permute-start(bf16[256,1024]{1,0:T(8,128)(2,1)S(1)} %join.20.a_ref), channel_id=1, source_target_pairs={{0,16},{16,0},{1,17},{17,1},{2,18},{18,2},{3,19},{19,3},{4,20},{20... | collective-permute-start | bytes 1572872 | tf_op jit(solution)/shard_map/ppermute | solution.py:552
  60.6 1.6 %collective-permute-start.21 = (bf16[256,1024]{1,0:T(8,128)(2,1)S(1)}, bf16[256,1024]{1,0:T(8,128)(2,1)S(1)}, u32[]{:S(2)}, u32[]{:S(2)}) collective-permute-start(bf16[256,1024]{1,0:T(8,128)(2,1)S(1)} %get-tuple-element.509), channel_id=1, source_target_pairs={{0,2},{1,3},{2,0},{3,1},{4,6},{5,7},{6,4},{7,5},{8,10},{9,11},{10,... | collective-permute-start | bytes 1572872 | tf_op jit(solution)/shard_map/ppermute | solution.py:36
  62.2 1.2 %collective-permute-start.20 = (bf16[256,1024]{1,0:T(8,128)(2,1)S(1)}, bf16[256,1024]{1,0:T(8,128)(2,1)S(1)}, u32[]{:S(2)}, u32[]{:S(2)}) collective-permute-start(bf16[256,1024]{1,0:T(8,128)(2,1)S(1)} %get-tuple-element.507), channel_id=1, source_target_pairs={{0,4},{1,5},{2,6},{3,7},{4,0},{5,1},{6,2},{7,3},{8,12},{9,13},{10,... | collective-permute-start | bytes 1572872 | tf_op jit(solution)/shard_map/ppermute | solution.py:36
  63.4 2.8 %collective-permute-done.17.b_ref = bf16[256,1024]{1,0:T(8,128)(2,1)S(1)} collective-permute-done((bf16[256,1024]{1,0:T(8,128)(2,1)S(1)}, bf16[256,1024]{1,0:T(8,128)(2,1)S(1)}, u32[]{:S(2)}, u32[]{:S(2)}) %collective-permute-start.17) | collective-permute-done | bytes 524320 | tf_op jit(solution)/shard_map/ppermute | solution.py:36
  66.2 0.1 fold.8
  66.3 0.1 fold.9
  66.4 5.3 %collective-permute-done.15.a_ref = bf16[256,1024]{1,0:T(8,128)(2,1)S(1)} collective-permute-done((bf16[256,1024]{1,0:T(8,128)(2,1)S(1)}, bf16[256,1024]{1,0:T(8,128)(2,1)S(1)}, u32[]{:S(2)}, u32[]{:S(2)}) %collective-permute-start.15) | collective-permute-done | bytes 524320 | tf_op jit(solution)/shard_map/ppermute | solution.py:552
  71.8 1.7 %collective-permute-start.18 = (bf16[256,1024]{1,0:T(8,128)(2,1)S(1)}, bf16[256,1024]{1,0:T(8,128)(2,1)S(1)}, u32[]{:S(2)}, u32[]{:S(2)}) collective-permute-start(bf16[256,1024]{1,0:T(8,128)(2,1)S(1)} %collective-permute-done.14.b_ref), channel_id=1, source_target_pairs={{0,16},{16,0},{1,17},{17,1},{2,18},{18,2},{3,19},{19,3},{4,20},{20... | collective-permute-start | bytes 1572872 | tf_op jit(solution)/shard_map/ppermute | solution.py:552
  73.5 1.6 %collective-permute-start.19 = (bf16[128,1024]{1,0:T(8,128)(2,1)S(1)}, bf16[128,1024]{1,0:T(8,128)(2,1)S(1)}, u32[]{:S(2)}, u32[]{:S(2)}) collective-permute-start(bf16[128,1024]{1,0:T(8,128)(2,1)S(1)} %get-tuple-element.505), channel_id=1, source_target_pairs={{0,2},{1,3},{2,0},{3,1},{4,6},{5,7},{6,4},{7,5},{8,10},{9,11},{10,... | collective-permute-start | bytes 786440 | tf_op jit(solution)/shard_map/ppermute | solution.py:36
  75.0 0.7 collective-permute-start.22
  75.7 0.1 fold.10
  75.9 2.3 %collective-permute-start.27 = (bf16[128,1024]{1,0:T(8,128)(2,1)S(1)}, bf16[128,1024]{1,0:T(8,128)(2,1)S(1)}, u32[]{:S(2)}, u32[]{:S(2)}) collective-permute-start(bf16[128,1024]{1,0:T(8,128)(2,1)S(1)} %get-tuple-element.559), channel_id=1, source_target_pairs={{0,8},{1,9},{2,10},{3,11},{4,12},{5,13},{6,14},{7,15},{8,0},{9,1},... | collective-permute-start | bytes 786440 | tf_op jit(solution)/shard_map/ppermute | solution.py:36
  78.1 0.1 fold.11
  78.3 1.6 %collective-permute-start.25 = (bf16[128,1024]{1,0:T(8,128)(2,1)S(1)}, bf16[128,1024]{1,0:T(8,128)(2,1)S(1)}, u32[]{:S(2)}, u32[]{:S(2)}) collective-permute-start(bf16[128,1024]{1,0:T(8,128)(2,1)S(1)} %get-tuple-element.556), channel_id=1, source_target_pairs={{0,2},{1,3},{2,0},{3,1},{4,6},{5,7},{6,4},{7,5},{8,10},{9,11},{10,... | collective-permute-start | bytes 786440 | tf_op jit(solution)/shard_map/ppermute | solution.py:36
  79.8 2.9 %collective-permute-done.19.b_ref = bf16[128,1024]{1,0:T(8,128)(2,1)S(1)} collective-permute-done((bf16[128,1024]{1,0:T(8,128)(2,1)S(1)}, bf16[128,1024]{1,0:T(8,128)(2,1)S(1)}, u32[]{:S(2)}, u32[]{:S(2)}) %collective-permute-start.19) | collective-permute-done | bytes 262176 | tf_op jit(solution)/shard_map/ppermute | solution.py:36
  82.8 3.6 %collective-permute-done.22.b_ref = bf16[128,1024]{1,0:T(8,128)(2,1)S(1)} collective-permute-done((bf16[128,1024]{1,0:T(8,128)(2,1)S(1)}, bf16[128,1024]{1,0:T(8,128)(2,1)S(1)}, u32[]{:S(2)}, u32[]{:S(2)}) %collective-permute-start.22) | collective-permute-done | bytes 262176 | tf_op jit(solution)/shard_map/ppermute | solution.py:36
  86.5 0.4 collective-permute-start.26
  86.9 0.7 input_nb.2
  87.6 2.3 %collective-permute-done.27.b_ref = bf16[128,1024]{1,0:T(8,128)(2,1)S(1)} collective-permute-done((bf16[128,1024]{1,0:T(8,128)(2,1)S(1)}, bf16[128,1024]{1,0:T(8,128)(2,1)S(1)}, u32[]{:S(2)}, u32[]{:S(2)}) %collective-permute-start.27) | collective-permute-done | bytes 262176 | tf_op jit(solution)/shard_map/ppermute | solution.py:36
  90.0 0.1 collective-permute-start.23
  90.1 0.7 input_nb.3
  90.8 0.6 collective-permute-start.28
  91.3 0.4 collective-permute-start.24
  91.7 2.4 %collective-permute-done.26.refs_1_ = bf16[64,1024]{1,0:T(8,128)(2,1)S(1)} collective-permute-done((bf16[64,1024]{1,0:T(8,128)(2,1)S(1)}, bf16[64,1024]{1,0:T(8,128)(2,1)S(1)}, u32[]{:S(2)}, u32[]{:S(2)}) %collective-permute-start.26) | collective-permute-done | bytes 131104 | tf_op jit(solution)/shard_map/ppermute | solution.py:36
  94.1 2.6 %collective-permute-start.30 = (bf16[64,1024]{1,0:T(8,128)(2,1)S(1)}, bf16[64,1024]{1,0:T(8,128)(2,1)S(1)}, u32[]{:S(2)}, u32[]{:S(2)}) collective-permute-start(bf16[64,1024]{1,0:T(8,128)(2,1)S(1)} %get-tuple-element.596), channel_id=1, source_target_pairs={{0,4},{1,5},{2,6},{3,7},{4,0},{5,1},{6,2},{7,3},{8,12},{9,13},{10,... | collective-permute-start | bytes 393224 | tf_op jit(solution)/shard_map/ppermute | solution.py:36
  96.8 3.5 %collective-permute-start.29 = (bf16[64,1024]{1,0:T(8,128)(2,1)S(1)}, bf16[64,1024]{1,0:T(8,128)(2,1)S(1)}, u32[]{:S(2)}, u32[]{:S(2)}) collective-permute-start(bf16[64,1024]{1,0:T(8,128)(2,1)S(1)} %get-tuple-element.594), channel_id=1, source_target_pairs={{0,8},{1,9},{2,10},{3,11},{4,12},{5,13},{6,14},{7,15},{8,0},{9,1},... | collective-permute-start | bytes 393224 | tf_op jit(solution)/shard_map/ppermute | solution.py:36
  100.3 0.9 collective-permute-done.24.refs_1_
  101.2 2.4 %input_own.1 = bf16[512,1024]{1,0:T(8,128)(2,1)} custom-call(bf16[2,512,512]{2,1,0:T(8,128)(2,1)S(1)} %get-tuple-element.422.pre0, bf16[2,512,512]{2,1,0:T(8,128)(2,1)S(1)} %get-tuple-element.472.pre1, bf16[512,1024]{1,0:T(8,128)(2,1)S(1)} %join.21.w0, bf16[512,1024]{1,0:T(8,128)(2,1)S(1)} %join.23.w1, ...), custom_call_target="tpu_custom_call" | custom-call | tf_op jit(solution)/shard_map/input_own/pallas_call | solution.py:331
  103.6 2.5 %collective-permute-done.29.refs_3_ = bf16[64,1024]{1,0:T(8,128)(2,1)S(1)} collective-permute-done((bf16[64,1024]{1,0:T(8,128)(2,1)S(1)}, bf16[64,1024]{1,0:T(8,128)(2,1)S(1)}, u32[]{:S(2)}, u32[]{:S(2)}) %collective-permute-start.29) | collective-permute-done | bytes 131104 | tf_op jit(solution)/shard_map/ppermute | solution.py:36
  106.1 1.4 %total.3 = f32[128,1024]{1,0:T(8,128)} custom-call(s32[2]{0:T(128)S(1)} %copy-done.6, bf16[64,1024]{1,0:T(8,128)(2,1)S(1)} %get-tuple-element.603.refs_0_, bf16[64,1024]{1,0:T(8,128)(2,1)S(1)} %collective-permute-done.26.refs_1_, bf16[64,1024]{1,0:T(8,128)(2,1)S(1)} %get-tuple-element.605.refs_2_, bf16[64,1024]{1,0:T(8,128)(2,1)S(1)} %collective-permute-done.30.refs_3_, ...), custom_call_target="tpu_custom_call" | custom-call | tf_op jit(solution)/shard_map/total/pallas_call | solution.py:446
  107.5 1.4 %total.2 = f32[128,1024]{1,0:T(8,128)} custom-call(s32[2]{0:T(128)S(1)} %copy-done.6, bf16[64,1024]{1,0:T(8,128)(2,1)S(1)} %get-tuple-element.592.refs_0_, bf16[64,1024]{1,0:T(8,128)(2,1)S(1)} %collective-permute-done.24.refs_1_, bf16[64,1024]{1,0:T(8,128)(2,1)S(1)} %get-tuple-element.600.refs_2_, bf16[64,1024]{1,0:T(8,128)(2,1)S(1)} %collective-permute-done.29.refs_3_, ...), custom_call_target="tpu_custom_call" | custom-call | tf_op jit(solution)/shard_map/total/pallas_call | solution.py:446
  (64 shorter events, 0.8 us)
Async XLA Ops:
  0.6 26.3 %collective-permute-start.7 = (bf16[512,2048]{1,0:T(8,128)(2,1)}, bf16[512,2048]{1,0:T(8,128)(2,1)}, u32[]{:S(2)}, u32[]{:S(2)}) collective-permute-start(bf16[512,2048]{1,0:T(8,128)(2,1)} %in_ref), channel_id=1, source_target_pairs={{0,1},{1,0},{2,3},{3,2},{4,5},{5,4},{6,7},{7,6},{8,9},{9,8},{10,11... | collective-permute-start | bytes 6291464 | tf_op jit(solution)/shard_map/ppermute | solution.py:36
  1.1 14.1 %collective-permute-start = (bf16[512,1024]{1,0:T(8,128)(2,1)}, bf16[512,1024]{1,0:T(8,128)(2,1)}, u32[]{:S(2)}, u32[]{:S(2)}) collective-permute-start(bf16[512,1024]{1,0:T(8,128)(2,1)} %own_ref), channel_id=1, source_target_pairs={{0,1},{1,0},{2,3},{3,2},{4,5},{5,4},{6,7},{7,6},{8,9},{9,8},{10,11... | collective-permute-start | bytes 3145736 | tf_op jit(solution)/shard_map/ppermute | solution.py:36
  2.2 10.6 %collective-permute-start.1 = (bf16[64,1024]{1,0:T(8,128)(2,1)S(1)}, bf16[64,1024]{1,0:T(8,128)(2,1)S(1)}, u32[]{:S(2)}, u32[]{:S(2)}) collective-permute-start(bf16[64,1024]{1,0:T(8,128)(2,1)S(1)} %get-tuple-element.318.a_ref), channel_id=1, source_target_pairs={{0,8},{1,9},{2,10},{3,11},{4,12},{5,13},{6,14},{7,15},{8,0},{9,1},... | collective-permute-start | bytes 393224 | tf_op jit(solution)/shard_map/ppermute | solution.py:36
  6.3 26.2 %collective-permute-start.9 = (bf16[512,1024]{1,0:T(8,128)(2,1)}, bf16[512,1024]{1,0:T(8,128)(2,1)}, u32[]{:S(2)}, u32[]{:S(2)}) collective-permute-start(bf16[512,1024]{1,0:T(8,128)(2,1)} %own_ref.2), channel_id=1, source_target_pairs={{0,1},{1,0},{2,3},{3,2},{4,5},{5,4},{6,7},{7,6},{8,9},{9,8},{10,11... | collective-permute-start | bytes 3145736 | tf_op jit(solution)/shard_map/ppermute | solution.py:36
  10.6 9.5 %copy-start.3 = (bf16[8,1024]{1,0:T(8,128)(2,1)S(1)}, bf16[8,1024]{1,0:T(8,128)(2,1)}, u32[]{:S(2)}) copy-start(bf16[8,1024]{1,0:T(8,128)(2,1)} %pack.1.a_ref) | copy-start | bytes 49156
  12.9 10.7 %collective-permute-start.4 = (bf16[128,1024]{1,0:T(8,128)(2,1)S(1)}, bf16[128,1024]{1,0:T(8,128)(2,1)S(1)}, u32[]{:S(2)}, u32[]{:S(2)}) collective-permute-start(bf16[128,1024]{1,0:T(8,128)(2,1)S(1)} %join.12.a_ref), channel_id=1, source_target_pairs={{0,4},{1,5},{2,6},{3,7},{4,0},{5,1},{6,2},{7,3},{8,12},{9,13},{10,... | collective-permute-start | bytes 786440 | tf_op jit(solution)/shard_map/ppermute | solution.py:36
  13.7 9.9 %collective-permute-start.5 = (bf16[64,1024]{1,0:T(8,128)(2,1)S(1)}, bf16[64,1024]{1,0:T(8,128)(2,1)S(1)}, u32[]{:S(2)}, u32[]{:S(2)}) collective-permute-start(bf16[64,1024]{1,0:T(8,128)(2,1)S(1)} %get-tuple-element.345.a_ref), channel_id=1, source_target_pairs={{0,2},{1,3},{2,0},{3,1},{4,6},{5,7},{6,4},{7,5},{8,10},{9,11},{10,... | collective-permute-start | bytes 393224 | tf_op jit(solution)/shard_map/ppermute | solution.py:36
  15.2 4.9 %collective-permute-start.2 = (bf16[8,1024]{1,0:T(8,128)(2,1)}, bf16[8,1024]{1,0:T(8,128)(2,1)S(1)}, u32[]{:S(2)}, u32[]{:S(2)}) collective-permute-start(bf16[8,1024]{1,0:T(8,128)(2,1)} %pack.1.a_ref), channel_id=1, source_target_pairs={{0,2},{1,3},{2,0},{3,1},{4,6},{5,7},{6,4},{7,5},{8,10},{9,11},{10,... | collective-permute-start | bytes 49160 | tf_op jit(solution)/shard_map/ppermute | solution.py:36
  15.7 1.6 %copy-start.2 = (bf16[512,2048]{1,0:T(8,128)(2,1)S(1)}, bf16[512,2048]{1,0:T(8,128)(2,1)}, u32[]{:S(2)}) copy-start(bf16[512,2048]{1,0:T(8,128)(2,1)} %in_ref) | copy-start | bytes 6291460
  17.3 0.7 copy-start.5
  20.1 6.6 %collective-permute-start.3 = (bf16[16,1024]{1,0:T(8,128)(2,1)S(1)}, bf16[16,1024]{1,0:T(8,128)(2,1)S(1)}, u32[]{:S(2)}, u32[]{:S(2)}) collective-permute-start(bf16[16,1024]{1,0:T(8,128)(2,1)S(1)} %join.13.a_ref), channel_id=1, source_target_pairs={{0,8},{1,9},{2,10},{3,11},{4,12},{5,13},{6,14},{7,15},{8,0},{9,1},... | collective-permute-start | bytes 98312 | tf_op jit(solution)/shard_map/ppermute | solution.py:36
  23.7 15.0 %collective-permute-start.12 = (bf16[256,1024]{1,0:T(8,128)(2,1)S(1)}, bf16[256,1024]{1,0:T(8,128)(2,1)S(1)}, u32[]{:S(2)}, u32[]{:S(2)}) collective-permute-start(bf16[256,1024]{1,0:T(8,128)(2,1)S(1)} %join.15.a_ref), channel_id=1, source_target_pairs={{0,16},{16,0},{1,17},{17,1},{2,18},{18,2},{3,19},{19,3},{4,20},{20... | collective-permute-start | bytes 1572872 | tf_op jit(solution)/shard_map/ppermute | solution.py:552
  25.2 13.4 %collective-permute-start.10 = (bf16[256,1024]{1,0:T(8,128)(2,1)S(1)}, bf16[256,1024]{1,0:T(8,128)(2,1)S(1)}, u32[]{:S(2)}, u32[]{:S(2)}) collective-permute-start(bf16[256,1024]{1,0:T(8,128)(2,1)S(1)} %join.15.a_ref), channel_id=1, source_target_pairs={{0,2},{1,3},{2,0},{3,1},{4,6},{5,7},{6,4},{7,5},{8,10},{9,11},{10,... | collective-permute-start | bytes 1572872 | tf_op jit(solution)/shard_map/ppermute | solution.py:36
  26.8 5.6 %collective-permute-start.6 = (bf16[32,1024]{1,0:T(8,128)(2,1)S(1)}, bf16[32,1024]{1,0:T(8,128)(2,1)S(1)}, u32[]{:S(2)}, u32[]{:S(2)}) collective-permute-start(bf16[32,1024]{1,0:T(8,128)(2,1)S(1)} %join.16.a_ref), channel_id=1, source_target_pairs={{0,4},{1,5},{2,6},{3,7},{4,0},{5,1},{6,2},{7,3},{8,12},{9,13},{10,... | collective-permute-start | bytes 196616 | tf_op jit(solution)/shard_map/ppermute | solution.py:36
  26.9 13.1 %collective-permute-start.11 = (bf16[128,1024]{1,0:T(8,128)(2,1)S(1)}, bf16[128,1024]{1,0:T(8,128)(2,1)S(1)}, u32[]{:S(2)}, u32[]{:S(2)}) collective-permute-start(bf16[128,1024]{1,0:T(8,128)(2,1)S(1)} %join.14.a_ref), channel_id=1, source_target_pairs={{0,8},{1,9},{2,10},{3,11},{4,12},{5,13},{6,14},{7,15},{8,0},{9,1},... | collective-permute-start | bytes 786440 | tf_op jit(solution)/shard_map/ppermute | solution.py:36
  32.4 1.5 %copy-start.1 = (bf16[512,1024]{1,0:T(8,128)(2,1)S(1)}, bf16[512,1024]{1,0:T(8,128)(2,1)}, u32[]{:S(2)}) copy-start(bf16[512,1024]{1,0:T(8,128)(2,1)} %own_ref) | copy-start | bytes 3145732
  32.4 1.5 %copy-start.4 = (f32[1024]{0:T(1024)S(1)}, f32[1024]{0:T(1024)}, u32[]{:S(2)}) copy-start(f32[1024]{0:T(1024)} %param.16) | copy-start | bytes 12292
  32.4 1.4 %collective-permute-start.8 = (bf16[64,1024]{1,0:T(8,128)(2,1)S(1)}, bf16[64,1024]{1,0:T(8,128)(2,1)S(1)}, u32[]{:S(2)}, u32[]{:S(2)}) collective-permute-start(bf16[64,1024]{1,0:T(8,128)(2,1)S(1)} %join.17.a_ref), channel_id=1, source_target_pairs={{0,1},{1,0},{2,3},{3,2},{4,5},{5,4},{6,7},{7,6},{8,9},{9,8},{10,11... | collective-permute-start | bytes 393224 | tf_op jit(solution)/shard_map/ppermute | solution.py:36
  38.6 4.0 %copy-start = (bf16[512,1024]{1,0:T(8,128)(2,1)S(1)}, bf16[512,1024]{1,0:T(8,128)(2,1)}, u32[]{:S(2)}) copy-start(bf16[512,1024]{1,0:T(8,128)(2,1)} %own_ref.2) | copy-start | bytes 3145732
  40.1 13.0 %collective-permute-start.14 = (bf16[256,1024]{1,0:T(8,128)(2,1)S(1)}, bf16[256,1024]{1,0:T(8,128)(2,1)S(1)}, u32[]{:S(2)}, u32[]{:S(2)}) collective-permute-start(bf16[256,1024]{1,0:T(8,128)(2,1)S(1)} %join.20.a_ref), channel_id=1, source_target_pairs={{0,4},{1,5},{2,6},{3,7},{4,0},{5,1},{6,2},{7,3},{8,12},{9,13},{10,... | collective-permute-start | bytes 1572872 | tf_op jit(solution)/shard_map/ppermute | solution.py:36
  40.8 13.7 %collective-permute-start.13 = (bf16[256,1024]{1,0:T(8,128)(2,1)S(1)}, bf16[256,1024]{1,0:T(8,128)(2,1)S(1)}, u32[]{:S(2)}, u32[]{:S(2)}) collective-permute-start(bf16[256,1024]{1,0:T(8,128)(2,1)S(1)} %collective-permute-done.10.b_ref), channel_id=1, source_target_pairs={{0,16},{16,0},{1,17},{17,1},{2,18},{18,2},{3,19},{19,3},{4,20},{20... | collective-permute-start | bytes 1572872 | tf_op jit(solution)/shard_map/ppermute | solution.py:552
  50.0 16.3 %collective-permute-start.16 = (bf16[256,1024]{1,0:T(8,128)(2,1)S(1)}, bf16[256,1024]{1,0:T(8,128)(2,1)S(1)}, u32[]{:S(2)}, u32[]{:S(2)}) collective-permute-start(bf16[256,1024]{1,0:T(8,128)(2,1)S(1)} %get-tuple-element.481), channel_id=1, source_target_pairs={{0,2},{1,3},{2,0},{3,1},{4,6},{5,7},{6,4},{7,5},{8,10},{9,11},{10,... | collective-permute-start | bytes 1572872 | tf_op jit(solution)/shard_map/ppermute | solution.py:36
  51.6 14.6 %collective-permute-start.17 = (bf16[256,1024]{1,0:T(8,128)(2,1)S(1)}, bf16[256,1024]{1,0:T(8,128)(2,1)S(1)}, u32[]{:S(2)}, u32[]{:S(2)}) collective-permute-start(bf16[256,1024]{1,0:T(8,128)(2,1)S(1)} %get-tuple-element.483), channel_id=1, source_target_pairs={{0,4},{1,5},{2,6},{3,7},{4,0},{5,1},{6,2},{7,3},{8,12},{9,13},{10,... | collective-permute-start | bytes 1572872 | tf_op jit(solution)/shard_map/ppermute | solution.py:36
  58.8 13.0 %collective-permute-start.15 = (bf16[256,1024]{1,0:T(8,128)(2,1)S(1)}, bf16[256,1024]{1,0:T(8,128)(2,1)S(1)}, u32[]{:S(2)}, u32[]{:S(2)}) collective-permute-start(bf16[256,1024]{1,0:T(8,128)(2,1)S(1)} %join.20.a_ref), channel_id=1, source_target_pairs={{0,16},{16,0},{1,17},{17,1},{2,18},{18,2},{3,19},{19,3},{4,20},{20... | collective-permute-start | bytes 1572872 | tf_op jit(solution)/shard_map/ppermute | solution.py:552
  60.6 15.1 %collective-permute-start.21 = (bf16[256,1024]{1,0:T(8,128)(2,1)S(1)}, bf16[256,1024]{1,0:T(8,128)(2,1)S(1)}, u32[]{:S(2)}, u32[]{:S(2)}) collective-permute-start(bf16[256,1024]{1,0:T(8,128)(2,1)S(1)} %get-tuple-element.509), channel_id=1, source_target_pairs={{0,2},{1,3},{2,0},{3,1},{4,6},{5,7},{6,4},{7,5},{8,10},{9,11},{10,... | collective-permute-start | bytes 1572872 | tf_op jit(solution)/shard_map/ppermute | solution.py:36
  62.2 15.9 %collective-permute-start.20 = (bf16[256,1024]{1,0:T(8,128)(2,1)S(1)}, bf16[256,1024]{1,0:T(8,128)(2,1)S(1)}, u32[]{:S(2)}, u32[]{:S(2)}) collective-permute-start(bf16[256,1024]{1,0:T(8,128)(2,1)S(1)} %get-tuple-element.507), channel_id=1, source_target_pairs={{0,4},{1,5},{2,6},{3,7},{4,0},{5,1},{6,2},{7,3},{8,12},{9,13},{10,... | collective-permute-start | bytes 1572872 | tf_op jit(solution)/shard_map/ppermute | solution.py:36
  71.8 15.1 %collective-permute-start.18 = (bf16[256,1024]{1,0:T(8,128)(2,1)S(1)}, bf16[256,1024]{1,0:T(8,128)(2,1)S(1)}, u32[]{:S(2)}, u32[]{:S(2)}) collective-permute-start(bf16[256,1024]{1,0:T(8,128)(2,1)S(1)} %collective-permute-done.14.b_ref), channel_id=1, source_target_pairs={{0,16},{16,0},{1,17},{17,1},{2,18},{18,2},{3,19},{19,3},{4,20},{20... | collective-permute-start | bytes 1572872 | tf_op jit(solution)/shard_map/ppermute | solution.py:552
  73.5 9.2 %collective-permute-start.19 = (bf16[128,1024]{1,0:T(8,128)(2,1)S(1)}, bf16[128,1024]{1,0:T(8,128)(2,1)S(1)}, u32[]{:S(2)}, u32[]{:S(2)}) collective-permute-start(bf16[128,1024]{1,0:T(8,128)(2,1)S(1)} %get-tuple-element.505), channel_id=1, source_target_pairs={{0,2},{1,3},{2,0},{3,1},{4,6},{5,7},{6,4},{7,5},{8,10},{9,11},{10,... | collective-permute-start | bytes 786440 | tf_op jit(solution)/shard_map/ppermute | solution.py:36
  75.0 11.4 %collective-permute-start.22 = (bf16[128,1024]{1,0:T(8,128)(2,1)S(1)}, bf16[128,1024]{1,0:T(8,128)(2,1)S(1)}, u32[]{:S(2)}, u32[]{:S(2)}) collective-permute-start(bf16[128,1024]{1,0:T(8,128)(2,1)S(1)} %get-tuple-element.534), channel_id=1, source_target_pairs={{0,4},{1,5},{2,6},{3,7},{4,0},{5,1},{6,2},{7,3},{8,12},{9,13},{10,... | collective-permute-start | bytes 786440 | tf_op jit(solution)/shard_map/ppermute | solution.py:36
  75.9 14.0 %collective-permute-start.27 = (bf16[128,1024]{1,0:T(8,128)(2,1)S(1)}, bf16[128,1024]{1,0:T(8,128)(2,1)S(1)}, u32[]{:S(2)}, u32[]{:S(2)}) collective-permute-start(bf16[128,1024]{1,0:T(8,128)(2,1)S(1)} %get-tuple-element.559), channel_id=1, source_target_pairs={{0,8},{1,9},{2,10},{3,11},{4,12},{5,13},{6,14},{7,15},{8,0},{9,1},... | collective-permute-start | bytes 786440 | tf_op jit(solution)/shard_map/ppermute | solution.py:36
  78.3 18.4 %collective-permute-start.25 = (bf16[128,1024]{1,0:T(8,128)(2,1)S(1)}, bf16[128,1024]{1,0:T(8,128)(2,1)S(1)}, u32[]{:S(2)}, u32[]{:S(2)}) collective-permute-start(bf16[128,1024]{1,0:T(8,128)(2,1)S(1)} %get-tuple-element.556), channel_id=1, source_target_pairs={{0,2},{1,3},{2,0},{3,1},{4,6},{5,7},{6,4},{7,5},{8,10},{9,11},{10,... | collective-permute-start | bytes 786440 | tf_op jit(solution)/shard_map/ppermute | solution.py:36
  86.5 7.6 %collective-permute-start.26 = (bf16[64,1024]{1,0:T(8,128)(2,1)S(1)}, bf16[64,1024]{1,0:T(8,128)(2,1)S(1)}, u32[]{:S(2)}, u32[]{:S(2)}) collective-permute-start(bf16[64,1024]{1,0:T(8,128)(2,1)S(1)} %get-tuple-element.557), channel_id=1, source_target_pairs={{0,8},{1,9},{2,10},{3,11},{4,12},{5,13},{6,14},{7,15},{8,0},{9,1},... | collective-permute-start | bytes 393224 | tf_op jit(solution)/shard_map/ppermute | solution.py:36
  90.0 11.2 %collective-permute-start.23 = (bf16[256,1024]{1,0:T(8,128)(2,1)S(1)}, bf16[256,1024]{1,0:T(8,128)(2,1)S(1)}, u32[]{:S(2)}, u32[]{:S(2)}) collective-permute-start(bf16[256,1024]{1,0:T(8,128)(2,1)S(1)} %input_nb.2), channel_id=1, source_target_pairs={{0,1},{1,0},{2,3},{3,2},{4,5},{5,4},{6,7},{7,6},{8,9},{9,8},{10,11... | collective-permute-start | bytes 1572872 | tf_op jit(solution)/shard_map/ppermute | solution.py:36
  90.8 10.4 %collective-permute-start.28 = (bf16[256,1024]{1,0:T(8,128)(2,1)S(1)}, bf16[256,1024]{1,0:T(8,128)(2,1)S(1)}, u32[]{:S(2)}, u32[]{:S(2)}) collective-permute-start(bf16[256,1024]{1,0:T(8,128)(2,1)S(1)} %input_nb.3), channel_id=1, source_target_pairs={{0,1},{1,0},{2,3},{3,2},{4,5},{5,4},{6,7},{7,6},{8,9},{9,8},{10,11... | collective-permute-start | bytes 1572872 | tf_op jit(solution)/shard_map/ppermute | solution.py:36
  91.3 9.8 %collective-permute-start.24 = (bf16[64,1024]{1,0:T(8,128)(2,1)S(1)}, bf16[64,1024]{1,0:T(8,128)(2,1)S(1)}, u32[]{:S(2)}, u32[]{:S(2)}) collective-permute-start(bf16[64,1024]{1,0:T(8,128)(2,1)S(1)} %get-tuple-element.554), channel_id=1, source_target_pairs={{0,8},{1,9},{2,10},{3,11},{4,12},{5,13},{6,14},{7,15},{8,0},{9,1},... | collective-permute-start | bytes 393224 | tf_op jit(solution)/shard_map/ppermute | solution.py:36
  94.1 9.5 %collective-permute-start.30 = (bf16[64,1024]{1,0:T(8,128)(2,1)S(1)}, bf16[64,1024]{1,0:T(8,128)(2,1)S(1)}, u32[]{:S(2)}, u32[]{:S(2)}) collective-permute-start(bf16[64,1024]{1,0:T(8,128)(2,1)S(1)} %get-tuple-element.596), channel_id=1, source_target_pairs={{0,4},{1,5},{2,6},{3,7},{4,0},{5,1},{6,2},{7,3},{8,12},{9,13},{10,... | collective-permute-start | bytes 393224 | tf_op jit(solution)/shard_map/ppermute | solution.py:36
  96.7 9.4 %copy-start.6 = (s32[2]{0:T(128)S(1)}, s32[2]{0:T(128)}, u32[]{:S(2)}) copy-start(s32[2]{0:T(128)} %pad_add_fusion.ids_ref) | copy-start | bytes 28
  96.8 9.4 %collective-permute-start.29 = (bf16[64,1024]{1,0:T(8,128)(2,1)S(1)}, bf16[64,1024]{1,0:T(8,128)(2,1)S(1)}, u32[]{:S(2)}, u32[]{:S(2)}) collective-permute-start(bf16[64,1024]{1,0:T(8,128)(2,1)S(1)} %get-tuple-element.594), channel_id=1, source_target_pairs={{0,8},{1,9},{2,10},{3,11},{4,12},{5,13},{6,14},{7,15},{8,0},{9,1},... | collective-permute-start | bytes 393224 | tf_op jit(solution)/shard_map/ppermute | solution.py:36

commit v4 on v3

--- a/solution.py
+++ b/solution.py
@@ -10,13 +10,13 @@
 LEN = 128
 TICK = 100_000_000
 SCHEDULE = (
-    "inp>", "pre>", "resid>", "states>", "out>", "pack", "out:1", "out>", "resid?", "small>",
-    "gelu0", "small:1", "small>", "inp:1", "out:1", "out>", "xa", "ia?", "small:30", "small>",
-    "inp>", "gelu1", "small:30", "small>", "states?", "small:1", "resid", "out:1", "xa?", "ib?",
-    "xb", "inp:1", "inp>", "gi0", "xa?", "go1", "ia?", "go0", "go0>", "gi0>", "inp:1", "wout",
-    "gi1", "go1>", "gi1>", "ia", "go0:1", "go0>", "gi0", "ia?", "gi0>", "ib", "go1:1", "go1>",
-    "gi1:1", "gi1>", "go0:1", "gi0", "gi0>", "go0>", "win", "nb0", "go1:1", "go1>", "nb1", "go0?",
-    "gi1:30", "gi1>", "gi0?", "nb?", "own", "tgo", "tgi",
+    "inp>", "pre>", "resid>", "states>", "out>", "pack", "out:30", "out>", "resid?", "small>",
+    "gelu0", "small:1", "small>", "inp:1", "out:1", "out>", "xa", "small:30", "small>", "inp>",
+    "gelu1", "small:30", "small>", "small:1", "resid", "out:1", "xa?", "xb", "inp:1", "states?",
+    "inp>", "gi0", "go1", "xa?", "ia?", "go0", "go0>", "go1>", "gi0>", "inp:1", "wout", "gi1",
+    "gi1>", "ia", "go0:1", "go0>", "gi0", "ia?", "gi0>", "ib", "go1:1", "go1>", "go0?", "gi1:1",
+    "gi1>", "go0:1", "gi0", "gi0>", "go0>", "win", "nb0", "go1:1", "go1>", "nb1", "go0?", "gi1:30",
+    "gi1>", "gi0?", "nb?", "own", "tgo", "tgi",
 )
 ORDERS = {"out": "down", "inp": "far", "go0": "side", "go1": "far", "gi0": "up", "gi1": "side"}
 BF = jnp.bfloat16
@@ -133,39 +133,42 @@
         result = jnp.dot(weights, table, preferred_element_type=F32)
         question_ref[...] = result[slots + queries :]
 
-    for k, src in enumerate((own_ref, nb_ref)):
-        x = src[...].astype(F32)
-        centre = x - jnp.mean(x, axis=-1, keepdims=True)
-        inverse = lax.rsqrt(jnp.mean(centre * centre, axis=-1, keepdims=True) + 1e-06)
-        normed = centre * inverse
-        scaled = pass_ref[pl.ds(k * slots + step, 1), :]
-        base = scaled - jnp.mean(scaled, axis=-1, keepdims=True)
-        grad = inverse * (base - normed * jnp.mean(scaled * normed, axis=-1, keepdims=True))
-        bf_ref[k] = grad.astype(BF)
+    for part in range(own_ref.shape[0] // LEN):
+        here = slice(part * LEN, (part + 1) * LEN)
+        for k, src in enumerate((own_ref, nb_ref)):
+            x = src[here].astype(F32)
+            centre = x - jnp.mean(x, axis=-1, keepdims=True)
+            inverse = lax.rsqrt(jnp.mean(centre * centre, axis=-1, keepdims=True) + 1e-06)
+            slot = k * slots + step * (own_ref.shape[0] // LEN) + part
+            scaled = pass_ref[pl.ds(slot, 1), :]
+            base = scaled - jnp.mean(scaled, axis=-1, keepdims=True)
+            along = jnp.mean(centre * scaled, axis=-1, keepdims=True) * (inverse * inverse)
+            bf_ref[k, here] = (inverse * (base - centre * along)).astype(BF)
 
 
 def resid_grads(slots, queries, own, nb, table, gain):
     tokens, width = own.shape
     total = table.shape[0]
+    block = 4 * LEN
     return pl.pallas_call(
         functools.partial(resid_kernel, slots, queries),
-        grid=(slots,),
+        grid=(tokens // block,),
         out_shape=(
             jax.ShapeDtypeStruct((2, tokens, width), BF),
             jax.ShapeDtypeStruct((queries, width), F32),
         ),
         in_specs=[
-            pl.BlockSpec((LEN, width), lambda s: (s, 0)),
-            pl.BlockSpec((LEN, width), lambda s: (s, 0)),
+            pl.BlockSpec((block, width), lambda s: (s, 0)),
+            pl.BlockSpec((block, width), lambda s: (s, 0)),
             pl.BlockSpec((total, width), lambda s: (0, 0)),
             pl.BlockSpec((1, width), lambda s: (0, 0)),
         ],
         out_specs=(
-            pl.BlockSpec((2, LEN, width), lambda s: (0, s, 0)),
+            pl.BlockSpec((2, block, width), lambda s: (0, s, 0)),
             pl.BlockSpec((queries, width), lambda s: (0, 0)),
         ),
         scratch_shapes=[pltpu.VMEM((2 * slots, width), F32)],
-        compiler_params=params(8),
+        compiler_params=params(16),
         cost_estimate=FREE,
         name="resid_grads",
     )(own, nb, table, gain)
@@ -196,7 +199,7 @@
 
 def gelu(ids, preact, units, half):
     tokens, width = preact.shape
-    block = 128
+    block = 256
     out = pl.BlockSpec((block, units // 2), lambda i, ids: (i, 0))
     return pl.pallas_call(
         functools.partial(gelu_kernel, half),
@@ -640,7 +643,8 @@
         elif name in ("tgo", "tgi"):
             pair = [chains[name[1:] + k] for k in "01"]
             pair[0].came, pair[1].came = order.gate(pair[0].came, pair[1].came)
-            v[name] = total(ids, order.mark, *pair)
+            mark = order.mark
+            v[name] = order(lambda *x: total(ids, mark, *pair), pair[0].came, ticks=0)
         else:
             raise ValueError(word)
     return (input_grad, v["tgi"], v["tgo"], question_grad)

time: 109 us -> 107 us (0.982)
  waiting for transfers between devices: 30.3 us -> 41.4 us
  starting transfers between devices: 39.9 us -> 32.6 us
  Pallas kernels: 33.7 us -> 29.9 us
  local copies, waits for them, and re-layouts: 3.26 us -> 1.41 us
    ppermute x27, waiting for transfers between devices: 23.6 us -> 37.3 us  [swap(): return lax.ppermute(x, 'psg', [(i, i ^ mask) for i in range(n)])]
    ppermute x27, starting transfers between devices: 33.1 us -> 29.3 us  [swap(): return lax.ppermute(x, 'psg', [(i, i ^ mask) for i in range(n)])]
    ppermute x4, starting transfers between devices: 6.85 us -> 3.3 us  [cross(): return lax.ppermute(x, 'groups', [(0, 1), (1, 0)])]
    ppermute x4, waiting for transfers between devices: 6.73 us -> 4.08 us  [cross(): return lax.ppermute(x, 'groups', [(0, 1), (1, 0)])]
    pallas_call x2, Pallas kernels: 8.39 us -> 6.29 us  [grad_in_part(): pl.pallas_call(functools.partial(grad_in_kernel, rows), grid=(units // bl...]
    unnamed x14 -> x12, local copies, waits for them, and re-layouts: 2.27 us -> 0.42 us
  transfers between devices with their start and end apart: 31 -> 31, of which waited for: 13 -> 15; matrix products, arithmetic and copies ran while one was open for 1% -> 1% of each run, Pallas kernels for 28% -> 27%
where the time goes in v4:
time: 107 us
  waiting for transfers between devices  41.4 us (39%)
  starting transfers between devices  32.6 us (30%)
  Pallas kernels  29.9 us (28%)
  local copies, waits for them, and re-layouts  1.41 us (1%)
  between operations  1.11 us (1%)
    ppermute x27, waiting for transfers between devices, swap(): return lax.ppermute(x, 'psg', [(i, i ^ mask) for i in range(n)])  37.3 us
    ppermute x27, starting transfers between devices, swap(): return lax.ppermute(x, 'psg', [(i, i ^ mask) for i in range(n)])  29.3 us
    pallas_call x2, Pallas kernels, grad_in_part(): pl.pallas_call(functools.partial(grad_in_kernel, rows), grid=(units // bl...  6.29 us
    pallas_call x2, Pallas kernels, gelu(): pl.pallas_call(functools.partial(gelu_kernel, half), grid_spec=pltpu.Pref...  5.21 us
    ppermute x4, waiting for transfers between devices, cross(): return lax.ppermute(x, 'groups', [(0, 1), (1, 0)])  4.08 us
    pallas_call x1, Pallas kernels, resid_grads(): pl.pallas_call(functools.partial(resid_kernel, slots, queries), grid=(tok...  3.77 us
    pallas_call x1, Pallas kernels, pack(): pl.pallas_call(functools.partial(pack_kernel, slots), out_shape=jax.Shape...  3.66 us
    ppermute x4, starting transfers between devices, cross(): return lax.ppermute(x, 'groups', [(0, 1), (1, 0)])  3.3 us
  transfers between devices with their start and end apart: 31, of which 15 were waited for; matrix products, arithmetic and copies ran while one was open for 1% of the time, Pallas kernels for 27%

profile of v4, /device:TPU:0, one launch (start us, length us, event | category | flops | bytes accessed | tf_op | source)
XLA Modules:
  0.0 107.0 jit_solution(15377142950199120013)
XLA Ops:
  0.6 0.5 collective-permute-start.7
  1.1 0.1 collective-permute-start
  1.2 1.0 constant_dynamic-slice_fusion
  2.2 4.1 %collective-permute-start.1 = (bf16[64,1024]{1,0:T(8,128)(2,1)S(1)}, bf16[64,1024]{1,0:T(8,128)(2,1)S(1)}, u32[]{:S(2)}, u32[]{:S(2)}) collective-permute-start(bf16[64,1024]{1,0:T(8,128)(2,1)S(1)} %get-tuple-element.323.a_ref), channel_id=1, source_target_pairs={{0,8},{1,9},{2,10},{3,11},{4,12},{5,13},{6,14},{7,15},{8,0},{9,1},... | collective-permute-start | bytes 393224 | tf_op jit(solution)/shard_map/ppermute | solution.py:36
  6.3 0.6 pad_add_fusion.ids_ref
  6.9 3.7 %pack.1.a_ref = bf16[8,1024]{1,0:T(8,128)(2,1)} custom-call(s32[2]{0:T(128)} %pad_add_fusion.ids_ref, s32[64]{0:T(128)} %place_in, s32[16]{0:T(128)} %live_in, bf16[512,1024]{1,0:T(8,128)(2,1)} %own_ref, f32[1,1024]{1,0:T(1,128)} %bitcast.3, bf16[2,1024]{1,0:T(2,128)(2,1)} %query_in, bf16[2,32]{1,0:T(2,128)(2,1)} %score_in, s32[2,32]{1,0:T(2,128)} %ret_in), custom_call_target="tpu_custom_call" | custom-call | tf_op jit(solution)/shard_map/pack/pallas_call | solution.py:90
  10.6 2.3 %collective-permute-done.1.b_ref = bf16[64,1024]{1,0:T(8,128)(2,1)S(1)} collective-permute-done((bf16[64,1024]{1,0:T(8,128)(2,1)S(1)}, bf16[64,1024]{1,0:T(8,128)(2,1)S(1)}, u32[]{:S(2)}, u32[]{:S(2)}) %collective-permute-start.1) | collective-permute-done | bytes 131104 | tf_op jit(solution)/shard_map/ppermute | solution.py:36
  12.9 0.8 collective-permute-start.4
  13.7 0.4 copy-done
  14.1 1.6 %collective-permute-start.5 = (bf16[64,1024]{1,0:T(8,128)(2,1)S(1)}, bf16[64,1024]{1,0:T(8,128)(2,1)S(1)}, u32[]{:S(2)}, u32[]{:S(2)}) collective-permute-start(bf16[64,1024]{1,0:T(8,128)(2,1)S(1)} %get-tuple-element.350.a_ref), channel_id=1, source_target_pairs={{0,2},{1,3},{2,0},{3,1},{4,6},{5,7},{6,4},{7,5},{8,10},{9,11},{10,... | collective-permute-start | bytes 393224 | tf_op jit(solution)/shard_map/ppermute | solution.py:36
  15.7 0.5 collective-permute-start.2
  16.2 2.0 %gelu.2 = (bf16[512,512]{1,0:T(8,128)(2,1)S(1)}, bf16[512,512]{1,0:T(8,128)(2,1)S(1)}, f32[512,512]{1,0:T(8,128)S(1)}, f32[512,512]{1,0:T(8,128)S(1)}) custom-call(s32[2]{0:T(128)S(1)} %copy-done.5, bf16[512,2048]{1,0:T(8,128)(2,1)S(1)} %copy-done.2), custom_call_target="tpu_custom_call" | custom-call | tf_op jit(solution)/shard_map/gelu/pallas_call | solution.py:204
  18.2 2.2 %collective-permute-done.2.b_ref = bf16[8,1024]{1,0:T(8,128)(2,1)S(1)} collective-permute-done((bf16[8,1024]{1,0:T(8,128)(2,1)S(1)}, bf16[8,1024]{1,0:T(8,128)(2,1)S(1)}, u32[]{:S(2)}, u32[]{:S(2)}) %collective-permute-start.2) | collective-permute-done | bytes 16416 | tf_op jit(solution)/shard_map/ppermute | solution.py:36
  20.4 3.0 %collective-permute-start.3 = (bf16[16,1024]{1,0:T(8,128)(2,1)S(1)}, bf16[16,1024]{1,0:T(8,128)(2,1)S(1)}, u32[]{:S(2)}, u32[]{:S(2)}) collective-permute-start(bf16[16,1024]{1,0:T(8,128)(2,1)S(1)} %join.13.a_ref), channel_id=1, source_target_pairs={{0,8},{1,9},{2,10},{3,11},{4,12},{5,13},{6,14},{7,15},{8,0},{9,1},... | collective-permute-start | bytes 98312 | tf_op jit(solution)/shard_map/ppermute | solution.py:36
  23.5 1.6 %collective-permute-start.12 = (bf16[256,1024]{1,0:T(8,128)(2,1)S(1)}, bf16[256,1024]{1,0:T(8,128)(2,1)S(1)}, u32[]{:S(2)}, u32[]{:S(2)}) collective-permute-start(bf16[256,1024]{1,0:T(8,128)(2,1)S(1)} %join.15.a_ref), channel_id=1, source_target_pairs={{0,16},{16,0},{1,17},{17,1},{2,18},{18,2},{3,19},{19,3},{4,20},{20... | collective-permute-start | bytes 1572872 | tf_op jit(solution)/shard_map/ppermute | solution.py:555
  25.0 1.5 %collective-permute-start.9 = (bf16[256,1024]{1,0:T(8,128)(2,1)S(1)}, bf16[256,1024]{1,0:T(8,128)(2,1)S(1)}, u32[]{:S(2)}, u32[]{:S(2)}) collective-permute-start(bf16[256,1024]{1,0:T(8,128)(2,1)S(1)} %join.15.a_ref), channel_id=1, source_target_pairs={{0,2},{1,3},{2,0},{3,1},{4,6},{5,7},{6,4},{7,5},{8,10},{9,11},{10,... | collective-permute-start | bytes 1572872 | tf_op jit(solution)/shard_map/ppermute | solution.py:36
  26.6 1.2 %collective-permute-start.6 = (bf16[32,1024]{1,0:T(8,128)(2,1)S(1)}, bf16[32,1024]{1,0:T(8,128)(2,1)S(1)}, u32[]{:S(2)}, u32[]{:S(2)}) collective-permute-start(bf16[32,1024]{1,0:T(8,128)(2,1)S(1)} %join.16.a_ref), channel_id=1, source_target_pairs={{0,4},{1,5},{2,6},{3,7},{4,0},{5,1},{6,2},{7,3},{8,12},{9,13},{10,... | collective-permute-start | bytes 196616 | tf_op jit(solution)/shard_map/ppermute | solution.py:36
  27.8 1.6 %collective-permute-start.11 = (bf16[128,1024]{1,0:T(8,128)(2,1)S(1)}, bf16[128,1024]{1,0:T(8,128)(2,1)S(1)}, u32[]{:S(2)}, u32[]{:S(2)}) collective-permute-start(bf16[128,1024]{1,0:T(8,128)(2,1)S(1)} %join.14.a_ref), channel_id=1, source_target_pairs={{0,8},{1,9},{2,10},{3,11},{4,12},{5,13},{6,14},{7,15},{8,0},{9,1},... | collective-permute-start | bytes 786440 | tf_op jit(solution)/shard_map/ppermute | solution.py:36
  29.4 3.2 %gelu.3 = (bf16[512,512]{1,0:T(8,128)(2,1)S(1)}, bf16[512,512]{1,0:T(8,128)(2,1)S(1)}, f32[512,512]{1,0:T(8,128)S(1)}, f32[512,512]{1,0:T(8,128)S(1)}) custom-call(s32[2]{0:T(128)S(1)} %copy-done.5, bf16[512,2048]{1,0:T(8,128)(2,1)} %collective-permute-done.7.in_ref), custom_call_target="tpu_custom_call" | custom-call | tf_op jit(solution)/shard_map/gelu/pallas_call | solution.py:204
  32.7 0.1 collective-permute-start.8
  32.7 1.3 %collective-permute-done.8.b_ref = bf16[64,1024]{1,0:T(8,128)(2,1)S(1)} collective-permute-done((bf16[64,1024]{1,0:T(8,128)(2,1)S(1)}, bf16[64,1024]{1,0:T(8,128)(2,1)S(1)}, u32[]{:S(2)}, u32[]{:S(2)}) %collective-permute-start.8) | collective-permute-done | bytes 131104 | tf_op jit(solution)/shard_map/ppermute | solution.py:36
  34.1 3.8 %resid_grads.1 = (bf16[2,512,1024]{2,1,0:T(8,128)(2,1)S(1)}, f32[2,1024]{1,0:T(2,128)}) custom-call(bf16[512,1024]{1,0:T(8,128)(2,1)S(1)} %copy-done.1, bf16[512,1024]{1,0:T(8,128)(2,1)} %collective-permute-done.nb_ref, bf16[128,1024]{1,0:T(8,128)(2,1)S(1)} %join.18.all_ref, f32[1,1024]{1,0:T(1,128)S(1)} %bitcast.4), custom_call_target="tpu_custom_call" | custom-call | tf_op jit(solution)/shard_map/resid_grads/pallas_call | solution.py:153
  37.9 0.1 collective-permute-done.9.b_ref
  38.1 2.9 %collective-permute-done.11.b_ref = bf16[128,1024]{1,0:T(8,128)(2,1)S(1)} collective-permute-done((bf16[128,1024]{1,0:T(8,128)(2,1)S(1)}, bf16[128,1024]{1,0:T(8,128)(2,1)S(1)}, u32[]{:S(2)}, u32[]{:S(2)}) %collective-permute-start.11) | collective-permute-done | bytes 262176 | tf_op jit(solution)/shard_map/ppermute | solution.py:36
  41.1 0.1 collective-permute-start.14
  41.2 0.6 collective-permute-start.13
  41.8 3.0 %grad_in.2 = (bf16[2,512,512]{2,1,0:T(8,128)(2,1)S(1)}, bf16[256,1024]{1,0:T(8,128)(2,1)S(1)}, bf16[256,1024]{1,0:T(8,128)(2,1)S(1)}) custom-call(bf16[2,512,1024]{2,1,0:T(8,128)(2,1)S(1)} %get-tuple-element.469.resid_ref, bf16[512,1024]{1,0:T(8,128)(2,1)S(1)} %join.19.w_ref, f32[512,512]{1,0:T(8,128)S(1)} %get-tuple-element.419.slope_own, ...), custom_call_target="tpu_custom_call" | custom-call | tf_op jit(solution)/shard_map/grad_in/pallas_call | solution.py:265
  44.9 1.6 %grad_out.2 = (bf16[256,1024]{1,0:T(8,128)(2,1)S(1)}, bf16[256,1024]{1,0:T(8,128)(2,1)S(1)}) custom-call(bf16[512,512]{1,0:T(8,128)(2,1)S(1)} %get-tuple-element.432.own_ref, bf16[512,512]{1,0:T(8,128)(2,1)S(1)} %get-tuple-element.433.nb_ref, bf16[2,512,1024]{2,1,0:T(8,128)(2,1)S(1)} %get-tuple-element.469.resid_ref), custom_call_target="tpu_custom_call" | custom-call | tf_op jit(solution)/shard_map/grad_out/pallas_call | solution.py:230
  46.5 1.6 %grad_out.3 = (bf16[256,1024]{1,0:T(8,128)(2,1)S(1)}, bf16[256,1024]{1,0:T(8,128)(2,1)S(1)}) custom-call(bf16[512,512]{1,0:T(8,128)(2,1)S(1)} %get-tuple-element.447.own_ref, bf16[512,512]{1,0:T(8,128)(2,1)S(1)} %get-tuple-element.448.nb_ref, bf16[2,512,1024]{2,1,0:T(8,128)(2,1)S(1)} %get-tuple-element.469.resid_ref), custom_call_target="tpu_custom_call" | custom-call | tf_op jit(solution)/shard_map/grad_out/pallas_call | solution.py:230
  48.0 1.3 %collective-permute-start.16 = (bf16[256,1024]{1,0:T(8,128)(2,1)S(1)}, bf16[256,1024]{1,0:T(8,128)(2,1)S(1)}, u32[]{:S(2)}, u32[]{:S(2)}) collective-permute-start(bf16[256,1024]{1,0:T(8,128)(2,1)S(1)} %get-tuple-element.486), channel_id=1, source_target_pairs={{0,2},{1,3},{2,0},{3,1},{4,6},{5,7},{6,4},{7,5},{8,10},{9,11},{10,... | collective-permute-start | bytes 1572872 | tf_op jit(solution)/shard_map/ppermute | solution.py:36
  49.4 1.8 %collective-permute-start.17 = (bf16[256,1024]{1,0:T(8,128)(2,1)S(1)}, bf16[256,1024]{1,0:T(8,128)(2,1)S(1)}, u32[]{:S(2)}, u32[]{:S(2)}) collective-permute-start(bf16[256,1024]{1,0:T(8,128)(2,1)S(1)} %get-tuple-element.488), channel_id=1, source_target_pairs={{0,4},{1,5},{2,6},{3,7},{4,0},{5,1},{6,2},{7,3},{8,12},{9,13},{10,... | collective-permute-start | bytes 1572872 | tf_op jit(solution)/shard_map/ppermute | solution.py:36
  51.2 4.9 %collective-permute-done.14.b_ref = bf16[256,1024]{1,0:T(8,128)(2,1)S(1)} collective-permute-done((bf16[256,1024]{1,0:T(8,128)(2,1)S(1)}, bf16[256,1024]{1,0:T(8,128)(2,1)S(1)}, u32[]{:S(2)}, u32[]{:S(2)}) %collective-permute-start.14) | collective-permute-done | bytes 524320 | tf_op jit(solution)/shard_map/ppermute | solution.py:36
  56.2 3.2 %grad_in.3 = (bf16[2,512,512]{2,1,0:T(8,128)(2,1)S(1)}, bf16[256,1024]{1,0:T(8,128)(2,1)S(1)}, bf16[256,1024]{1,0:T(8,128)(2,1)S(1)}) custom-call(bf16[2,512,1024]{2,1,0:T(8,128)(2,1)S(1)} %get-tuple-element.469.resid_ref, bf16[512,1024]{1,0:T(8,128)(2,1)S(1)} %join.22.w_ref, f32[512,512]{1,0:T(8,128)S(1)} %get-tuple-element.471.slope_own, ...), custom_call_target="tpu_custom_call" | custom-call | tf_op jit(solution)/shard_map/grad_in/pallas_call | solution.py:265
  59.5 0.6 collective-permute-start.15
  60.1 1.1 %collective-permute-start.20 = (bf16[256,1024]{1,0:T(8,128)(2,1)S(1)}, bf16[256,1024]{1,0:T(8,128)(2,1)S(1)}, u32[]{:S(2)}, u32[]{:S(2)}) collective-permute-start(bf16[256,1024]{1,0:T(8,128)(2,1)S(1)} %get-tuple-element.512), channel_id=1, source_target_pairs={{0,2},{1,3},{2,0},{3,1},{4,6},{5,7},{6,4},{7,5},{8,10},{9,11},{10,... | collective-permute-start | bytes 1572872 | tf_op jit(solution)/shard_map/ppermute | solution.py:36
  61.2 6.1 %collective-permute-done.17.b_ref = bf16[256,1024]{1,0:T(8,128)(2,1)S(1)} collective-permute-done((bf16[256,1024]{1,0:T(8,128)(2,1)S(1)}, bf16[256,1024]{1,0:T(8,128)(2,1)S(1)}, u32[]{:S(2)}, u32[]{:S(2)}) %collective-permute-start.17) | collective-permute-done | bytes 524320 | tf_op jit(solution)/shard_map/ppermute | solution.py:36
  67.3 0.1 fold.8
  67.4 0.1 fold.9
  67.6 4.1 %collective-permute-done.15.a_ref = bf16[256,1024]{1,0:T(8,128)(2,1)S(1)} collective-permute-done((bf16[256,1024]{1,0:T(8,128)(2,1)S(1)}, bf16[256,1024]{1,0:T(8,128)(2,1)S(1)}, u32[]{:S(2)}, u32[]{:S(2)}) %collective-permute-start.15) | collective-permute-done | bytes 524320 | tf_op jit(solution)/shard_map/ppermute | solution.py:555
  71.6 0.5 collective-permute-start.18
  72.2 1.0 collective-permute-start.19
  73.1 1.8 %collective-permute-done.20.b_ref = bf16[256,1024]{1,0:T(8,128)(2,1)S(1)} collective-permute-done((bf16[256,1024]{1,0:T(8,128)(2,1)S(1)}, bf16[256,1024]{1,0:T(8,128)(2,1)S(1)}, u32[]{:S(2)}, u32[]{:S(2)}) %collective-permute-start.20) | collective-permute-done | bytes 524320 | tf_op jit(solution)/shard_map/ppermute | solution.py:36
  74.9 0.1 fold.10
  75.1 1.1 %collective-permute-start.22 = (bf16[128,1024]{1,0:T(8,128)(2,1)S(1)}, bf16[128,1024]{1,0:T(8,128)(2,1)S(1)}, u32[]{:S(2)}, u32[]{:S(2)}) collective-permute-start(bf16[128,1024]{1,0:T(8,128)(2,1)S(1)} %get-tuple-element.541), channel_id=1, source_target_pairs={{0,4},{1,5},{2,6},{3,7},{4,0},{5,1},{6,2},{7,3},{8,12},{9,13},{10,... | collective-permute-start | bytes 786440 | tf_op jit(solution)/shard_map/ppermute | solution.py:36
  76.2 1.7 %collective-permute-start.27 = (bf16[128,1024]{1,0:T(8,128)(2,1)S(1)}, bf16[128,1024]{1,0:T(8,128)(2,1)S(1)}, u32[]{:S(2)}, u32[]{:S(2)}) collective-permute-start(bf16[128,1024]{1,0:T(8,128)(2,1)S(1)} %get-tuple-element.566), channel_id=1, source_target_pairs={{0,8},{1,9},{2,10},{3,11},{4,12},{5,13},{6,14},{7,15},{8,0},{9,1},... | collective-permute-start | bytes 786440 | tf_op jit(solution)/shard_map/ppermute | solution.py:36
  77.9 1.2 %collective-permute-done.19.b_ref = bf16[128,1024]{1,0:T(8,128)(2,1)S(1)} collective-permute-done((bf16[128,1024]{1,0:T(8,128)(2,1)S(1)}, bf16[128,1024]{1,0:T(8,128)(2,1)S(1)}, u32[]{:S(2)}, u32[]{:S(2)}) %collective-permute-start.19) | collective-permute-done | bytes 262176 | tf_op jit(solution)/shard_map/ppermute | solution.py:36
  79.2 2.8 %collective-permute-done.21.b_ref = bf16[256,1024]{1,0:T(8,128)(2,1)S(1)} collective-permute-done((bf16[256,1024]{1,0:T(8,128)(2,1)S(1)}, bf16[256,1024]{1,0:T(8,128)(2,1)S(1)}, u32[]{:S(2)}, u32[]{:S(2)}) %collective-permute-start.21) | collective-permute-done | bytes 524320 | tf_op jit(solution)/shard_map/ppermute | solution.py:36
  82.0 0.1 fold.11
  82.1 0.1 collective-permute-start.25
  82.3 5.5 %collective-permute-done.22.b_ref = bf16[128,1024]{1,0:T(8,128)(2,1)S(1)} collective-permute-done((bf16[128,1024]{1,0:T(8,128)(2,1)S(1)}, bf16[128,1024]{1,0:T(8,128)(2,1)S(1)}, u32[]{:S(2)}, u32[]{:S(2)}) %collective-permute-start.22) | collective-permute-done | bytes 262176 | tf_op jit(solution)/shard_map/ppermute | solution.py:36
  87.9 0.1 collective-permute-start.26
  88.1 0.7 input_nb.2
  88.9 0.1 collective-permute-start.23
  88.9 0.7 input_nb.3
  89.7 0.6 collective-permute-start.28
  90.2 2.9 %collective-permute-start.24 = (bf16[64,1024]{1,0:T(8,128)(2,1)S(1)}, bf16[64,1024]{1,0:T(8,128)(2,1)S(1)}, u32[]{:S(2)}, u32[]{:S(2)}) collective-permute-start(bf16[64,1024]{1,0:T(8,128)(2,1)S(1)} %get-tuple-element.561), channel_id=1, source_target_pairs={{0,8},{1,9},{2,10},{3,11},{4,12},{5,13},{6,14},{7,15},{8,0},{9,1},... | collective-permute-start | bytes 393224 | tf_op jit(solution)/shard_map/ppermute | solution.py:36
  93.1 1.4 %collective-permute-done.26.refs_1_ = bf16[64,1024]{1,0:T(8,128)(2,1)S(1)} collective-permute-done((bf16[64,1024]{1,0:T(8,128)(2,1)S(1)}, bf16[64,1024]{1,0:T(8,128)(2,1)S(1)}, u32[]{:S(2)}, u32[]{:S(2)}) %collective-permute-start.26) | collective-permute-done | bytes 131104 | tf_op jit(solution)/shard_map/ppermute | solution.py:36
  94.5 0.3 collective-permute-start.30
  94.9 2.2 %collective-permute-start.29 = (bf16[64,1024]{1,0:T(8,128)(2,1)S(1)}, bf16[64,1024]{1,0:T(8,128)(2,1)S(1)}, u32[]{:S(2)}, u32[]{:S(2)}) collective-permute-start(bf16[64,1024]{1,0:T(8,128)(2,1)S(1)} %get-tuple-element.601), channel_id=1, source_target_pairs={{0,8},{1,9},{2,10},{3,11},{4,12},{5,13},{6,14},{7,15},{8,0},{9,1},... | collective-permute-start | bytes 393224 | tf_op jit(solution)/shard_map/ppermute | solution.py:36
  97.1 3.2 %collective-permute-done.24.refs_1_ = bf16[64,1024]{1,0:T(8,128)(2,1)S(1)} collective-permute-done((bf16[64,1024]{1,0:T(8,128)(2,1)S(1)}, bf16[64,1024]{1,0:T(8,128)(2,1)S(1)}, u32[]{:S(2)}, u32[]{:S(2)}) %collective-permute-start.24) | collective-permute-done | bytes 131104 | tf_op jit(solution)/shard_map/ppermute | solution.py:36
  100.3 2.4 %input_own.1 = bf16[512,1024]{1,0:T(8,128)(2,1)} custom-call(bf16[2,512,512]{2,1,0:T(8,128)(2,1)S(1)} %get-tuple-element.427.pre0, bf16[2,512,512]{2,1,0:T(8,128)(2,1)S(1)} %get-tuple-element.479.pre1, bf16[512,1024]{1,0:T(8,128)(2,1)S(1)} %join.21.w0, bf16[512,1024]{1,0:T(8,128)(2,1)S(1)} %join.23.w1, ...), custom_call_target="tpu_custom_call" | custom-call | tf_op jit(solution)/shard_map/input_own/pallas_call | solution.py:334
  102.8 1.4 %total.2 = f32[128,1024]{1,0:T(8,128)} custom-call(s32[2]{0:T(128)S(1)} %copy-done.5, bf16[64,1024]{1,0:T(8,128)(2,1)S(1)} %get-tuple-element.602.refs_0_, bf16[64,1024]{1,0:T(8,128)(2,1)S(1)} %collective-permute-done.26.refs_1_, bf16[64,1024]{1,0:T(8,128)(2,1)S(1)} %get-tuple-element.607.refs_2_, bf16[64,1024]{1,0:T(8,128)(2,1)S(1)} %collective-permute-done.30.refs_3_, ...), custom_call_target="tpu_custom_call" | custom-call | tf_op jit(solution)/shard_map/total/pallas_call | solution.py:449
  104.2 1.4 %collective-permute-done.29.refs_3_ = bf16[64,1024]{1,0:T(8,128)(2,1)S(1)} collective-permute-done((bf16[64,1024]{1,0:T(8,128)(2,1)S(1)}, bf16[64,1024]{1,0:T(8,128)(2,1)S(1)}, u32[]{:S(2)}, u32[]{:S(2)}) %collective-permute-start.29) | collective-permute-done | bytes 131104 | tf_op jit(solution)/shard_map/ppermute | solution.py:36
  105.6 1.4 %total.3 = f32[128,1024]{1,0:T(8,128)} custom-call(s32[2]{0:T(128)S(1)} %copy-done.5, bf16[64,1024]{1,0:T(8,128)(2,1)S(1)} %get-tuple-element.599.refs_0_, bf16[64,1024]{1,0:T(8,128)(2,1)S(1)} %collective-permute-done.24.refs_1_, bf16[64,1024]{1,0:T(8,128)(2,1)S(1)} %get-tuple-element.613.refs_2_, bf16[64,1024]{1,0:T(8,128)(2,1)S(1)} %collective-permute-done.29.refs_3_, ...), custom_call_target="tpu_custom_call" | custom-call | tf_op jit(solution)/shard_map/total/pallas_call | solution.py:449
  (62 shorter events, 0.8 us)
Async XLA Ops:
  0.6 27.1 %collective-permute-start.7 = (bf16[512,2048]{1,0:T(8,128)(2,1)}, bf16[512,2048]{1,0:T(8,128)(2,1)}, u32[]{:S(2)}, u32[]{:S(2)}) collective-permute-start(bf16[512,2048]{1,0:T(8,128)(2,1)} %in_ref), channel_id=1, source_target_pairs={{0,1},{1,0},{2,3},{3,2},{4,5},{5,4},{6,7},{7,6},{8,9},{9,8},{10,11... | collective-permute-start | bytes 6291464 | tf_op jit(solution)/shard_map/ppermute | solution.py:36
  1.1 14.5 %collective-permute-start = (bf16[512,1024]{1,0:T(8,128)(2,1)}, bf16[512,1024]{1,0:T(8,128)(2,1)}, u32[]{:S(2)}, u32[]{:S(2)}) collective-permute-start(bf16[512,1024]{1,0:T(8,128)(2,1)} %own_ref), channel_id=1, source_target_pairs={{0,1},{1,0},{2,3},{3,2},{4,5},{5,4},{6,7},{7,6},{8,9},{9,8},{10,11... | collective-permute-start | bytes 3145736 | tf_op jit(solution)/shard_map/ppermute | solution.py:36
  2.2 10.6 %collective-permute-start.1 = (bf16[64,1024]{1,0:T(8,128)(2,1)S(1)}, bf16[64,1024]{1,0:T(8,128)(2,1)S(1)}, u32[]{:S(2)}, u32[]{:S(2)}) collective-permute-start(bf16[64,1024]{1,0:T(8,128)(2,1)S(1)} %get-tuple-element.323.a_ref), channel_id=1, source_target_pairs={{0,8},{1,9},{2,10},{3,11},{4,12},{5,13},{6,14},{7,15},{8,0},{9,1},... | collective-permute-start | bytes 393224 | tf_op jit(solution)/shard_map/ppermute | solution.py:36
  12.9 1.2 %copy-start = (bf16[512,1024]{1,0:T(8,128)(2,1)S(1)}, bf16[512,1024]{1,0:T(8,128)(2,1)}, u32[]{:S(2)}) copy-start(bf16[512,1024]{1,0:T(8,128)(2,1)} %own_ref.2) | copy-start | bytes 3145732
  12.9 2.8 %copy-start.3 = (bf16[8,1024]{1,0:T(8,128)(2,1)S(1)}, bf16[8,1024]{1,0:T(8,128)(2,1)}, u32[]{:S(2)}) copy-start(bf16[8,1024]{1,0:T(8,128)(2,1)} %pack.1.a_ref) | copy-start | bytes 49156
  12.9 3.2 %copy-start.2 = (bf16[512,2048]{1,0:T(8,128)(2,1)S(1)}, bf16[512,2048]{1,0:T(8,128)(2,1)}, u32[]{:S(2)}) copy-start(bf16[512,2048]{1,0:T(8,128)(2,1)} %in_ref) | copy-start | bytes 6291460
  12.9 3.2 %copy-start.5 = (s32[2]{0:T(128)S(1)}, s32[2]{0:T(128)}, u32[]{:S(2)}) copy-start(s32[2]{0:T(128)} %pad_add_fusion.ids_ref) | copy-start | bytes 28
  12.9 10.5 %collective-permute-start.4 = (bf16[128,1024]{1,0:T(8,128)(2,1)S(1)}, bf16[128,1024]{1,0:T(8,128)(2,1)S(1)}, u32[]{:S(2)}, u32[]{:S(2)}) collective-permute-start(bf16[128,1024]{1,0:T(8,128)(2,1)S(1)} %join.12.a_ref), channel_id=1, source_target_pairs={{0,4},{1,5},{2,6},{3,7},{4,0},{5,1},{6,2},{7,3},{8,12},{9,13},{10,... | collective-permute-start | bytes 786440 | tf_op jit(solution)/shard_map/ppermute | solution.py:36
  14.1 27.0 %collective-permute-start.10 = (bf16[512,1024]{1,0:T(8,128)(2,1)S(1)}, bf16[512,1024]{1,0:T(8,128)(2,1)S(1)}, u32[]{:S(2)}, u32[]{:S(2)}) collective-permute-start(bf16[512,1024]{1,0:T(8,128)(2,1)S(1)} %copy-done), channel_id=1, source_target_pairs={{0,1},{1,0},{2,3},{3,2},{4,5},{5,4},{6,7},{7,6},{8,9},{9,8},{10,11... | collective-permute-start | bytes 3145736 | tf_op jit(solution)/shard_map/ppermute | solution.py:36
  14.1 9.3 %collective-permute-start.5 = (bf16[64,1024]{1,0:T(8,128)(2,1)S(1)}, bf16[64,1024]{1,0:T(8,128)(2,1)S(1)}, u32[]{:S(2)}, u32[]{:S(2)}) collective-permute-start(bf16[64,1024]{1,0:T(8,128)(2,1)S(1)} %get-tuple-element.350.a_ref), channel_id=1, source_target_pairs={{0,2},{1,3},{2,0},{3,1},{4,6},{5,7},{6,4},{7,5},{8,10},{9,11},{10,... | collective-permute-start | bytes 393224 | tf_op jit(solution)/shard_map/ppermute | solution.py:36
  15.7 4.7 %collective-permute-start.2 = (bf16[8,1024]{1,0:T(8,128)(2,1)S(1)}, bf16[8,1024]{1,0:T(8,128)(2,1)S(1)}, u32[]{:S(2)}, u32[]{:S(2)}) collective-permute-start(bf16[8,1024]{1,0:T(8,128)(2,1)S(1)} %copy-done.3), channel_id=1, source_target_pairs={{0,2},{1,3},{2,0},{3,1},{4,6},{5,7},{6,4},{7,5},{8,10},{9,11},{10,... | collective-permute-start | bytes 49160 | tf_op jit(solution)/shard_map/ppermute | solution.py:36
  20.4 6.2 %collective-permute-start.3 = (bf16[16,1024]{1,0:T(8,128)(2,1)S(1)}, bf16[16,1024]{1,0:T(8,128)(2,1)S(1)}, u32[]{:S(2)}, u32[]{:S(2)}) collective-permute-start(bf16[16,1024]{1,0:T(8,128)(2,1)S(1)} %join.13.a_ref), channel_id=1, source_target_pairs={{0,8},{1,9},{2,10},{3,11},{4,12},{5,13},{6,14},{7,15},{8,0},{9,1},... | collective-permute-start | bytes 98312 | tf_op jit(solution)/shard_map/ppermute | solution.py:36
  23.5 14.6 %collective-permute-start.12 = (bf16[256,1024]{1,0:T(8,128)(2,1)S(1)}, bf16[256,1024]{1,0:T(8,128)(2,1)S(1)}, u32[]{:S(2)}, u32[]{:S(2)}) collective-permute-start(bf16[256,1024]{1,0:T(8,128)(2,1)S(1)} %join.15.a_ref), channel_id=1, source_target_pairs={{0,16},{16,0},{1,17},{17,1},{2,18},{18,2},{3,19},{19,3},{4,20},{20... | collective-permute-start | bytes 1572872 | tf_op jit(solution)/shard_map/ppermute | solution.py:555
  25.0 13.0 %collective-permute-start.9 = (bf16[256,1024]{1,0:T(8,128)(2,1)S(1)}, bf16[256,1024]{1,0:T(8,128)(2,1)S(1)}, u32[]{:S(2)}, u32[]{:S(2)}) collective-permute-start(bf16[256,1024]{1,0:T(8,128)(2,1)S(1)} %join.15.a_ref), channel_id=1, source_target_pairs={{0,2},{1,3},{2,0},{3,1},{4,6},{5,7},{6,4},{7,5},{8,10},{9,11},{10,... | collective-permute-start | bytes 1572872 | tf_op jit(solution)/shard_map/ppermute | solution.py:36
  26.6 6.0 %collective-permute-start.6 = (bf16[32,1024]{1,0:T(8,128)(2,1)S(1)}, bf16[32,1024]{1,0:T(8,128)(2,1)S(1)}, u32[]{:S(2)}, u32[]{:S(2)}) collective-permute-start(bf16[32,1024]{1,0:T(8,128)(2,1)S(1)} %join.16.a_ref), channel_id=1, source_target_pairs={{0,4},{1,5},{2,6},{3,7},{4,0},{5,1},{6,2},{7,3},{8,12},{9,13},{10,... | collective-permute-start | bytes 196616 | tf_op jit(solution)/shard_map/ppermute | solution.py:36
  27.8 13.3 %collective-permute-start.11 = (bf16[128,1024]{1,0:T(8,128)(2,1)S(1)}, bf16[128,1024]{1,0:T(8,128)(2,1)S(1)}, u32[]{:S(2)}, u32[]{:S(2)}) collective-permute-start(bf16[128,1024]{1,0:T(8,128)(2,1)S(1)} %join.14.a_ref), channel_id=1, source_target_pairs={{0,8},{1,9},{2,10},{3,11},{4,12},{5,13},{6,14},{7,15},{8,0},{9,1},... | collective-permute-start | bytes 786440 | tf_op jit(solution)/shard_map/ppermute | solution.py:36
  32.6 1.5 %copy-start.1 = (bf16[512,1024]{1,0:T(8,128)(2,1)S(1)}, bf16[512,1024]{1,0:T(8,128)(2,1)}, u32[]{:S(2)}) copy-start(bf16[512,1024]{1,0:T(8,128)(2,1)} %own_ref) | copy-start | bytes 3145732
  32.6 1.5 %copy-start.4 = (f32[1024]{0:T(1024)S(1)}, f32[1024]{0:T(1024)}, u32[]{:S(2)}) copy-start(f32[1024]{0:T(1024)} %param.16) | copy-start | bytes 12292
  32.7 1.4 %collective-permute-start.8 = (bf16[64,1024]{1,0:T(8,128)(2,1)S(1)}, bf16[64,1024]{1,0:T(8,128)(2,1)S(1)}, u32[]{:S(2)}, u32[]{:S(2)}) collective-permute-start(bf16[64,1024]{1,0:T(8,128)(2,1)S(1)} %join.17.a_ref), channel_id=1, source_target_pairs={{0,1},{1,0},{2,3},{3,2},{4,5},{5,4},{6,7},{7,6},{8,9},{9,8},{10,11... | collective-permute-start | bytes 393224 | tf_op jit(solution)/shard_map/ppermute | solution.py:36
  41.1 14.9 %collective-permute-start.14 = (bf16[256,1024]{1,0:T(8,128)(2,1)S(1)}, bf16[256,1024]{1,0:T(8,128)(2,1)S(1)}, u32[]{:S(2)}, u32[]{:S(2)}) collective-permute-start(bf16[256,1024]{1,0:T(8,128)(2,1)S(1)} %join.20.a_ref), channel_id=1, source_target_pairs={{0,4},{1,5},{2,6},{3,7},{4,0},{5,1},{6,2},{7,3},{8,12},{9,13},{10,... | collective-permute-start | bytes 1572872 | tf_op jit(solution)/shard_map/ppermute | solution.py:36
  41.2 14.9 %collective-permute-start.13 = (bf16[256,1024]{1,0:T(8,128)(2,1)S(1)}, bf16[256,1024]{1,0:T(8,128)(2,1)S(1)}, u32[]{:S(2)}, u32[]{:S(2)}) collective-permute-start(bf16[256,1024]{1,0:T(8,128)(2,1)S(1)} %collective-permute-done.9.b_ref), channel_id=1, source_target_pairs={{0,16},{16,0},{1,17},{17,1},{2,18},{18,2},{3,19},{19,3},{4,20},{20... | collective-permute-start | bytes 1572872 | tf_op jit(solution)/shard_map/ppermute | solution.py:555
  48.0 19.4 %collective-permute-start.16 = (bf16[256,1024]{1,0:T(8,128)(2,1)S(1)}, bf16[256,1024]{1,0:T(8,128)(2,1)S(1)}, u32[]{:S(2)}, u32[]{:S(2)}) collective-permute-start(bf16[256,1024]{1,0:T(8,128)(2,1)S(1)} %get-tuple-element.486), channel_id=1, source_target_pairs={{0,2},{1,3},{2,0},{3,1},{4,6},{5,7},{6,4},{7,5},{8,10},{9,11},{10,... | collective-permute-start | bytes 1572872 | tf_op jit(solution)/shard_map/ppermute | solution.py:36
  49.4 17.9 %collective-permute-start.17 = (bf16[256,1024]{1,0:T(8,128)(2,1)S(1)}, bf16[256,1024]{1,0:T(8,128)(2,1)S(1)}, u32[]{:S(2)}, u32[]{:S(2)}) collective-permute-start(bf16[256,1024]{1,0:T(8,128)(2,1)S(1)} %get-tuple-element.488), channel_id=1, source_target_pairs={{0,4},{1,5},{2,6},{3,7},{4,0},{5,1},{6,2},{7,3},{8,12},{9,13},{10,... | collective-permute-start | bytes 1572872 | tf_op jit(solution)/shard_map/ppermute | solution.py:36
  59.5 12.2 %collective-permute-start.15 = (bf16[256,1024]{1,0:T(8,128)(2,1)S(1)}, bf16[256,1024]{1,0:T(8,128)(2,1)S(1)}, u32[]{:S(2)}, u32[]{:S(2)}) collective-permute-start(bf16[256,1024]{1,0:T(8,128)(2,1)S(1)} %join.20.a_ref), channel_id=1, source_target_pairs={{0,16},{16,0},{1,17},{17,1},{2,18},{18,2},{3,19},{19,3},{4,20},{20... | collective-permute-start | bytes 1572872 | tf_op jit(solution)/shard_map/ppermute | solution.py:555
  60.1 14.9 %collective-permute-start.20 = (bf16[256,1024]{1,0:T(8,128)(2,1)S(1)}, bf16[256,1024]{1,0:T(8,128)(2,1)S(1)}, u32[]{:S(2)}, u32[]{:S(2)}) collective-permute-start(bf16[256,1024]{1,0:T(8,128)(2,1)S(1)} %get-tuple-element.512), channel_id=1, source_target_pairs={{0,2},{1,3},{2,0},{3,1},{4,6},{5,7},{6,4},{7,5},{8,10},{9,11},{10,... | collective-permute-start | bytes 1572872 | tf_op jit(solution)/shard_map/ppermute | solution.py:36
  61.2 20.8 %collective-permute-start.21 = (bf16[256,1024]{1,0:T(8,128)(2,1)S(1)}, bf16[256,1024]{1,0:T(8,128)(2,1)S(1)}, u32[]{:S(2)}, u32[]{:S(2)}) collective-permute-start(bf16[256,1024]{1,0:T(8,128)(2,1)S(1)} %get-tuple-element.524), channel_id=1, source_target_pairs={{0,4},{1,5},{2,6},{3,7},{4,0},{5,1},{6,2},{7,3},{8,12},{9,13},{10,... | collective-permute-start | bytes 1572872 | tf_op jit(solution)/shard_map/ppermute | solution.py:36
  71.6 16.3 %collective-permute-start.18 = (bf16[256,1024]{1,0:T(8,128)(2,1)S(1)}, bf16[256,1024]{1,0:T(8,128)(2,1)S(1)}, u32[]{:S(2)}, u32[]{:S(2)}) collective-permute-start(bf16[256,1024]{1,0:T(8,128)(2,1)S(1)} %collective-permute-done.14.b_ref), channel_id=1, source_target_pairs={{0,16},{16,0},{1,17},{17,1},{2,18},{18,2},{3,19},{19,3},{4,20},{20... | collective-permute-start | bytes 1572872 | tf_op jit(solution)/shard_map/ppermute | solution.py:555
  72.2 7.0 %collective-permute-start.19 = (bf16[128,1024]{1,0:T(8,128)(2,1)S(1)}, bf16[128,1024]{1,0:T(8,128)(2,1)S(1)}, u32[]{:S(2)}, u32[]{:S(2)}) collective-permute-start(bf16[128,1024]{1,0:T(8,128)(2,1)S(1)} %get-tuple-element.510), channel_id=1, source_target_pairs={{0,2},{1,3},{2,0},{3,1},{4,6},{5,7},{6,4},{7,5},{8,10},{9,11},{10,... | collective-permute-start | bytes 786440 | tf_op jit(solution)/shard_map/ppermute | solution.py:36
  75.1 12.8 %collective-permute-start.22 = (bf16[128,1024]{1,0:T(8,128)(2,1)S(1)}, bf16[128,1024]{1,0:T(8,128)(2,1)S(1)}, u32[]{:S(2)}, u32[]{:S(2)}) collective-permute-start(bf16[128,1024]{1,0:T(8,128)(2,1)S(1)} %get-tuple-element.541), channel_id=1, source_target_pairs={{0,4},{1,5},{2,6},{3,7},{4,0},{5,1},{6,2},{7,3},{8,12},{9,13},{10,... | collective-permute-start | bytes 786440 | tf_op jit(solution)/shard_map/ppermute | solution.py:36
  76.2 12.6 %collective-permute-start.27 = (bf16[128,1024]{1,0:T(8,128)(2,1)S(1)}, bf16[128,1024]{1,0:T(8,128)(2,1)S(1)}, u32[]{:S(2)}, u32[]{:S(2)}) collective-permute-start(bf16[128,1024]{1,0:T(8,128)(2,1)S(1)} %get-tuple-element.566), channel_id=1, source_target_pairs={{0,8},{1,9},{2,10},{3,11},{4,12},{5,13},{6,14},{7,15},{8,0},{9,1},... | collective-permute-start | bytes 786440 | tf_op jit(solution)/shard_map/ppermute | solution.py:36
  82.1 12.7 %collective-permute-start.25 = (bf16[128,1024]{1,0:T(8,128)(2,1)S(1)}, bf16[128,1024]{1,0:T(8,128)(2,1)S(1)}, u32[]{:S(2)}, u32[]{:S(2)}) collective-permute-start(bf16[128,1024]{1,0:T(8,128)(2,1)S(1)} %get-tuple-element.563), channel_id=1, source_target_pairs={{0,2},{1,3},{2,0},{3,1},{4,6},{5,7},{6,4},{7,5},{8,10},{9,11},{10,... | collective-permute-start | bytes 786440 | tf_op jit(solution)/shard_map/ppermute | solution.py:36
  87.9 6.6 %collective-permute-start.26 = (bf16[64,1024]{1,0:T(8,128)(2,1)S(1)}, bf16[64,1024]{1,0:T(8,128)(2,1)S(1)}, u32[]{:S(2)}, u32[]{:S(2)}) collective-permute-start(bf16[64,1024]{1,0:T(8,128)(2,1)S(1)} %get-tuple-element.564), channel_id=1, source_target_pairs={{0,8},{1,9},{2,10},{3,11},{4,12},{5,13},{6,14},{7,15},{8,0},{9,1},... | collective-permute-start | bytes 393224 | tf_op jit(solution)/shard_map/ppermute | solution.py:36
  88.9 11.5 %collective-permute-start.23 = (bf16[256,1024]{1,0:T(8,128)(2,1)S(1)}, bf16[256,1024]{1,0:T(8,128)(2,1)S(1)}, u32[]{:S(2)}, u32[]{:S(2)}) collective-permute-start(bf16[256,1024]{1,0:T(8,128)(2,1)S(1)} %input_nb.2), channel_id=1, source_target_pairs={{0,1},{1,0},{2,3},{3,2},{4,5},{5,4},{6,7},{7,6},{8,9},{9,8},{10,11... | collective-permute-start | bytes 1572872 | tf_op jit(solution)/shard_map/ppermute | solution.py:36
  89.7 10.7 %collective-permute-start.28 = (bf16[256,1024]{1,0:T(8,128)(2,1)S(1)}, bf16[256,1024]{1,0:T(8,128)(2,1)S(1)}, u32[]{:S(2)}, u32[]{:S(2)}) collective-permute-start(bf16[256,1024]{1,0:T(8,128)(2,1)S(1)} %input_nb.3), channel_id=1, source_target_pairs={{0,1},{1,0},{2,3},{3,2},{4,5},{5,4},{6,7},{7,6},{8,9},{9,8},{10,11... | collective-permute-start | bytes 1572872 | tf_op jit(solution)/shard_map/ppermute | solution.py:36
  90.2 10.1 %collective-permute-start.24 = (bf16[64,1024]{1,0:T(8,128)(2,1)S(1)}, bf16[64,1024]{1,0:T(8,128)(2,1)S(1)}, u32[]{:S(2)}, u32[]{:S(2)}) collective-permute-start(bf16[64,1024]{1,0:T(8,128)(2,1)S(1)} %get-tuple-element.561), channel_id=1, source_target_pairs={{0,8},{1,9},{2,10},{3,11},{4,12},{5,13},{6,14},{7,15},{8,0},{9,1},... | collective-permute-start | bytes 393224 | tf_op jit(solution)/shard_map/ppermute | solution.py:36
  94.5 8.2 %collective-permute-start.30 = (bf16[64,1024]{1,0:T(8,128)(2,1)S(1)}, bf16[64,1024]{1,0:T(8,128)(2,1)S(1)}, u32[]{:S(2)}, u32[]{:S(2)}) collective-permute-start(bf16[64,1024]{1,0:T(8,128)(2,1)S(1)} %get-tuple-element.604), channel_id=1, source_target_pairs={{0,4},{1,5},{2,6},{3,7},{4,0},{5,1},{6,2},{7,3},{8,12},{9,13},{10,... | collective-permute-start | bytes 393224 | tf_op jit(solution)/shard_map/ppermute | solution.py:36
  94.9 10.7 %collective-permute-start.29 = (bf16[64,1024]{1,0:T(8,128)(2,1)S(1)}, bf16[64,1024]{1,0:T(8,128)(2,1)S(1)}, u32[]{:S(2)}, u32[]{:S(2)}) collective-permute-start(bf16[64,1024]{1,0:T(8,128)(2,1)S(1)} %get-tuple-element.601), channel_id=1, source_target_pairs={{0,8},{1,9},{2,10},{3,11},{4,12},{5,13},{6,14},{7,15},{8,0},{9,1},... | collective-permute-start | bytes 393224 | tf_op jit(solution)/shard_map/ppermute | solution.py:36

commit v5 on v4

--- a/solution.py
+++ b/solution.py
@@ -12,13 +12,13 @@
 SCHEDULE = (
     "inp>", "pre>", "resid>", "states>", "out>", "pack", "out:30", "out>", "resid?", "small>",
     "gelu0", "small:1", "small>", "inp:1", "out:1", "out>", "xa", "small:30", "small>", "inp>",
-    "gelu1", "small:30", "small>", "small:1", "resid", "out:1", "xa?", "xb", "inp:1", "states?",
-    "inp>", "gi0", "go1", "xa?", "ia?", "go0", "go0>", "go1>", "gi0>", "inp:1", "wout", "gi1",
-    "gi1>", "ia", "go0:1", "go0>", "gi0", "ia?", "gi0>", "ib", "go1:1", "go1>", "go0?", "gi1:1",
-    "gi1>", "go0:1", "gi0", "gi0>", "go0>", "win", "nb0", "go1:1", "go1>", "nb1", "go0?", "gi1:30",
-    "gi1>", "gi0?", "nb?", "own", "tgo", "tgi",
+    "gelu1", "small:30", "states?", "small>", "small:1", "ia?", "resid", "out:1", "xb", "xa?",
+    "inp:1", "xa?", "inp>", "go1", "ia?", "gi0", "go0", "go0>", "go1>", "gi0>", "inp:1", "wout",
+    "gi1:30", "gi1>", "ia", "go0:1", "go0>", "gi0:1", "ia?", "gi0>", "ib", "go1:1", "go1>", "gi1:1",
+    "gi1>", "go0:1", "go0>", "gi0:10", "gi0>", "win", "nb0", "go1:1", "go1>", "nb1", "go0?", "tgo",
+    "gi1:30", "gi1>", "own", "nb?", "tgi",
 )
-ORDERS = {"out": "down", "inp": "far", "go0": "side", "go1": "far", "gi0": "up", "gi1": "side"}
+ORDERS = {"out": "down", "inp": "far", "go0": "side", "go1": "up", "gi0": "far", "gi1": "side"}
 BF = jnp.bfloat16
 F32 = jnp.float32
 PACK_MIB = 63

time: 107 us -> 105 us (0.981)
  waiting for transfers between devices: 41.4 us -> 34.8 us
  starting transfers between devices: 32.6 us -> 35 us
  Pallas kernels: 29.9 us -> 32.2 us
    ppermute x27, waiting for transfers between devices: 37.3 us -> 30.8 us  [swap(): return lax.ppermute(x, 'psg', [(i, i ^ mask) for i in range(n)])]
    pallas_call x2, Pallas kernels: 6.29 us -> 8.58 us  [grad_in_part(): pl.pallas_call(functools.partial(grad_in_kernel, rows), grid=(units // bl...]
    ppermute x4, starting transfers between devices: 3.3 us -> 4.84 us  [cross(): return lax.ppermute(x, 'groups', [(0, 1), (1, 0)])]
  transfers between devices with their start and end apart: 31 -> 31, of which waited for: 15 -> 12; matrix products, arithmetic and copies ran while one was open for 1% -> 2% of each run, Pallas kernels for 27% -> 29%
where the time goes in v5:
time: 105 us
  starting transfers between devices  35 us (33%)
  waiting for transfers between devices  34.8 us (33%)
  Pallas kernels  32.2 us (31%)
  between operations  1.13 us (1%)
    ppermute x27, waiting for transfers between devices, swap(): return lax.ppermute(x, 'psg', [(i, i ^ mask) for i in range(n)])  30.8 us
    ppermute x27, starting transfers between devices, swap(): return lax.ppermute(x, 'psg', [(i, i ^ mask) for i in range(n)])  30.2 us
    pallas_call x2, Pallas kernels, grad_in_part(): pl.pallas_call(functools.partial(grad_in_kernel, rows), grid=(units // bl...  8.58 us
    pallas_call x2, Pallas kernels, gelu(): pl.pallas_call(functools.partial(gelu_kernel, half), grid_spec=pltpu.Pref...  5.21 us
    ppermute x4, starting transfers between devices, cross(): return lax.ppermute(x, 'groups', [(0, 1), (1, 0)])  4.84 us
    ppermute x4, waiting for transfers between devices, cross(): return lax.ppermute(x, 'groups', [(0, 1), (1, 0)])  4.04 us
    pallas_call x1, Pallas kernels, resid_grads(): pl.pallas_call(functools.partial(resid_kernel, slots, queries), grid=(tok...  3.77 us
    pallas_call x1, Pallas kernels, pack(): pl.pallas_call(functools.partial(pack_kernel, slots), out_shape=jax.Shape...  3.69 us
  transfers between devices with their start and end apart: 31, of which 12 were waited for; matrix products, arithmetic and copies ran while one was open for 2% of the time, Pallas kernels for 29%

profile of v5, /device:TPU:0, one launch (start us, length us, event | category | flops | bytes accessed | tf_op | source)
XLA Modules:
  0.0 104.8 jit_solution(18234046363477428230)
XLA Ops:
  0.6 0.5 collective-permute-start.7
  1.1 0.1 collective-permute-start
  1.2 1.0 constant_dynamic-slice_fusion
  2.2 4.1 %collective-permute-start.1 = (bf16[64,1024]{1,0:T(8,128)(2,1)S(1)}, bf16[64,1024]{1,0:T(8,128)(2,1)S(1)}, u32[]{:S(2)}, u32[]{:S(2)}) collective-permute-start(bf16[64,1024]{1,0:T(8,128)(2,1)S(1)} %get-tuple-element.317.a_ref), channel_id=1, source_target_pairs={{0,8},{1,9},{2,10},{3,11},{4,12},{5,13},{6,14},{7,15},{8,0},{9,1},... | collective-permute-start | bytes 393224 | tf_op jit(solution)/shard_map/ppermute | solution.py:36
  6.3 0.6 pad_add_fusion.ids_ref
  6.9 3.7 %pack.1.a_ref = bf16[8,1024]{1,0:T(8,128)(2,1)} custom-call(s32[2]{0:T(128)} %pad_add_fusion.ids_ref, s32[64]{0:T(128)} %place_in, s32[16]{0:T(128)} %live_in, bf16[512,1024]{1,0:T(8,128)(2,1)} %own_ref, f32[1,1024]{1,0:T(1,128)} %bitcast.3, bf16[2,1024]{1,0:T(2,128)(2,1)} %query_in, bf16[2,32]{1,0:T(2,128)(2,1)} %score_in, s32[2,32]{1,0:T(2,128)} %ret_in), custom_call_target="tpu_custom_call" | custom-call | tf_op jit(solution)/shard_map/pack/pallas_call | solution.py:90
  10.6 2.3 %collective-permute-done.1.b_ref = bf16[64,1024]{1,0:T(8,128)(2,1)S(1)} collective-permute-done((bf16[64,1024]{1,0:T(8,128)(2,1)S(1)}, bf16[64,1024]{1,0:T(8,128)(2,1)S(1)}, u32[]{:S(2)}, u32[]{:S(2)}) %collective-permute-start.1) | collective-permute-done | bytes 131104 | tf_op jit(solution)/shard_map/ppermute | solution.py:36
  12.9 0.8 collective-permute-start.4
  13.7 1.5 %collective-permute-start.5 = (bf16[64,1024]{1,0:T(8,128)(2,1)S(1)}, bf16[64,1024]{1,0:T(8,128)(2,1)S(1)}, u32[]{:S(2)}, u32[]{:S(2)}) collective-permute-start(bf16[64,1024]{1,0:T(8,128)(2,1)S(1)} %get-tuple-element.344.a_ref), channel_id=1, source_target_pairs={{0,2},{1,3},{2,0},{3,1},{4,6},{5,7},{6,4},{7,5},{8,10},{9,11},{10,... | collective-permute-start | bytes 393224 | tf_op jit(solution)/shard_map/ppermute | solution.py:36
  15.2 0.5 collective-permute-start.2
  15.8 2.0 %gelu.2 = (bf16[512,512]{1,0:T(8,128)(2,1)S(1)}, bf16[512,512]{1,0:T(8,128)(2,1)S(1)}, f32[512,512]{1,0:T(8,128)S(1)}, f32[512,512]{1,0:T(8,128)S(1)}) custom-call(s32[2]{0:T(128)S(1)} %copy-done.5, bf16[512,2048]{1,0:T(8,128)(2,1)S(1)} %copy-done.2), custom_call_target="tpu_custom_call" | custom-call | tf_op jit(solution)/shard_map/gelu/pallas_call | solution.py:204
  17.8 1.5 %collective-permute-done.2.b_ref = bf16[8,1024]{1,0:T(8,128)(2,1)S(1)} collective-permute-done((bf16[8,1024]{1,0:T(8,128)(2,1)S(1)}, bf16[8,1024]{1,0:T(8,128)(2,1)S(1)}, u32[]{:S(2)}, u32[]{:S(2)}) %collective-permute-start.2) | collective-permute-done | bytes 16416 | tf_op jit(solution)/shard_map/ppermute | solution.py:36
  19.2 3.4 %collective-permute-start.3 = (bf16[16,1024]{1,0:T(8,128)(2,1)S(1)}, bf16[16,1024]{1,0:T(8,128)(2,1)S(1)}, u32[]{:S(2)}, u32[]{:S(2)}) collective-permute-start(bf16[16,1024]{1,0:T(8,128)(2,1)S(1)} %join.13.a_ref), channel_id=1, source_target_pairs={{0,8},{1,9},{2,10},{3,11},{4,12},{5,13},{6,14},{7,15},{8,0},{9,1},... | collective-permute-start | bytes 98312 | tf_op jit(solution)/shard_map/ppermute | solution.py:36
  22.7 1.6 %collective-permute-start.12 = (bf16[256,1024]{1,0:T(8,128)(2,1)S(1)}, bf16[256,1024]{1,0:T(8,128)(2,1)S(1)}, u32[]{:S(2)}, u32[]{:S(2)}) collective-permute-start(bf16[256,1024]{1,0:T(8,128)(2,1)S(1)} %join.15.a_ref), channel_id=1, source_target_pairs={{0,16},{16,0},{1,17},{17,1},{2,18},{18,2},{3,19},{19,3},{4,20},{20... | collective-permute-start | bytes 1572872 | tf_op jit(solution)/shard_map/ppermute | solution.py:555
  24.3 1.5 %collective-permute-start.10 = (bf16[256,1024]{1,0:T(8,128)(2,1)S(1)}, bf16[256,1024]{1,0:T(8,128)(2,1)S(1)}, u32[]{:S(2)}, u32[]{:S(2)}) collective-permute-start(bf16[256,1024]{1,0:T(8,128)(2,1)S(1)} %join.15.a_ref), channel_id=1, source_target_pairs={{0,2},{1,3},{2,0},{3,1},{4,6},{5,7},{6,4},{7,5},{8,10},{9,11},{10,... | collective-permute-start | bytes 1572872 | tf_op jit(solution)/shard_map/ppermute | solution.py:36
  25.8 0.4 collective-permute-start.6
  26.2 2.3 %collective-permute-start.11 = (bf16[128,1024]{1,0:T(8,128)(2,1)S(1)}, bf16[128,1024]{1,0:T(8,128)(2,1)S(1)}, u32[]{:S(2)}, u32[]{:S(2)}) collective-permute-start(bf16[128,1024]{1,0:T(8,128)(2,1)S(1)} %join.14.a_ref), channel_id=1, source_target_pairs={{0,8},{1,9},{2,10},{3,11},{4,12},{5,13},{6,14},{7,15},{8,0},{9,1},... | collective-permute-start | bytes 786440 | tf_op jit(solution)/shard_map/ppermute | solution.py:36
  28.6 3.2 %gelu.3 = (bf16[512,512]{1,0:T(8,128)(2,1)S(1)}, bf16[512,512]{1,0:T(8,128)(2,1)S(1)}, f32[512,512]{1,0:T(8,128)S(1)}, f32[512,512]{1,0:T(8,128)S(1)}) custom-call(s32[2]{0:T(128)S(1)} %copy-done.5, bf16[512,2048]{1,0:T(8,128)(2,1)} %collective-permute-done.7.in_ref), custom_call_target="tpu_custom_call" | custom-call | tf_op jit(solution)/shard_map/gelu/pallas_call | solution.py:204
  31.8 0.1 collective-permute-start.9
  31.9 1.3 %collective-permute-done.9.b_ref = bf16[64,1024]{1,0:T(8,128)(2,1)S(1)} collective-permute-done((bf16[64,1024]{1,0:T(8,128)(2,1)S(1)}, bf16[64,1024]{1,0:T(8,128)(2,1)S(1)}, u32[]{:S(2)}, u32[]{:S(2)}) %collective-permute-start.9) | collective-permute-done | bytes 131104 | tf_op jit(solution)/shard_map/ppermute | solution.py:36
  33.3 3.8 %resid_grads.1 = (bf16[2,512,1024]{2,1,0:T(8,128)(2,1)S(1)}, f32[2,1024]{1,0:T(2,128)}) custom-call(bf16[512,1024]{1,0:T(8,128)(2,1)S(1)} %copy-done.1, bf16[512,1024]{1,0:T(8,128)(2,1)} %collective-permute-done.nb_ref, bf16[128,1024]{1,0:T(8,128)(2,1)S(1)} %join.18.all_ref, f32[1,1024]{1,0:T(1,128)S(1)} %bitcast.4), custom_call_target="tpu_custom_call" | custom-call | tf_op jit(solution)/shard_map/resid_grads/pallas_call | solution.py:153
  37.1 0.1 join.19.w_ref
  37.2 1.8 %collective-permute-done.11.b_ref = bf16[128,1024]{1,0:T(8,128)(2,1)S(1)} collective-permute-done((bf16[128,1024]{1,0:T(8,128)(2,1)S(1)}, bf16[128,1024]{1,0:T(8,128)(2,1)S(1)}, u32[]{:S(2)}, u32[]{:S(2)}) %collective-permute-start.11) | collective-permute-done | bytes 262176 | tf_op jit(solution)/shard_map/ppermute | solution.py:36
  39.1 0.1 collective-permute-start.14
  39.2 0.9 collective-permute-start.13
  40.1 1.6 %grad_out.2 = (bf16[256,1024]{1,0:T(8,128)(2,1)S(1)}, bf16[256,1024]{1,0:T(8,128)(2,1)S(1)}) custom-call(bf16[512,512]{1,0:T(8,128)(2,1)S(1)} %get-tuple-element.415.own_ref, bf16[512,512]{1,0:T(8,128)(2,1)S(1)} %get-tuple-element.416.nb_ref, bf16[2,512,1024]{2,1,0:T(8,128)(2,1)S(1)} %get-tuple-element.463.resid_ref), custom_call_target="tpu_custom_call" | custom-call | tf_op jit(solution)/shard_map/grad_out/pallas_call | solution.py:230
  41.6 4.2 %grad_in.2 = (bf16[2,512,512]{2,1,0:T(8,128)(2,1)S(1)}, bf16[256,1024]{1,0:T(8,128)(2,1)S(1)}, bf16[256,1024]{1,0:T(8,128)(2,1)S(1)}) custom-call(bf16[2,512,1024]{2,1,0:T(8,128)(2,1)S(1)} %get-tuple-element.463.resid_ref, bf16[512,1024]{1,0:T(8,128)(2,1)S(1)} %join.19.w_ref, f32[512,512]{1,0:T(8,128)S(1)} %get-tuple-element.424.slope_own, ...), custom_call_target="tpu_custom_call" | custom-call | tf_op jit(solution)/shard_map/grad_in/pallas_call | solution.py:265
  45.8 1.6 %grad_out.3 = (bf16[256,1024]{1,0:T(8,128)(2,1)S(1)}, bf16[256,1024]{1,0:T(8,128)(2,1)S(1)}) custom-call(bf16[512,512]{1,0:T(8,128)(2,1)S(1)} %get-tuple-element.441.own_ref, bf16[512,512]{1,0:T(8,128)(2,1)S(1)} %get-tuple-element.442.nb_ref, bf16[2,512,1024]{2,1,0:T(8,128)(2,1)S(1)} %get-tuple-element.463.resid_ref), custom_call_target="tpu_custom_call" | custom-call | tf_op jit(solution)/shard_map/grad_out/pallas_call | solution.py:230
  47.4 1.8 %collective-permute-start.17 = (bf16[256,1024]{1,0:T(8,128)(2,1)S(1)}, bf16[256,1024]{1,0:T(8,128)(2,1)S(1)}, u32[]{:S(2)}, u32[]{:S(2)}) collective-permute-start(bf16[256,1024]{1,0:T(8,128)(2,1)S(1)} %get-tuple-element.482), channel_id=1, source_target_pairs={{0,4},{1,5},{2,6},{3,7},{4,0},{5,1},{6,2},{7,3},{8,12},{9,13},{10,... | collective-permute-start | bytes 1572872 | tf_op jit(solution)/shard_map/ppermute | solution.py:36
  49.2 1.5 %collective-permute-start.16 = (bf16[256,1024]{1,0:T(8,128)(2,1)S(1)}, bf16[256,1024]{1,0:T(8,128)(2,1)S(1)}, u32[]{:S(2)}, u32[]{:S(2)}) collective-permute-start(bf16[256,1024]{1,0:T(8,128)(2,1)S(1)} %get-tuple-element.480), channel_id=1, source_target_pairs={{0,2},{1,3},{2,0},{3,1},{4,6},{5,7},{6,4},{7,5},{8,10},{9,11},{10,... | collective-permute-start | bytes 1572872 | tf_op jit(solution)/shard_map/ppermute | solution.py:36
  50.7 3.3 %collective-permute-done.14.b_ref = bf16[256,1024]{1,0:T(8,128)(2,1)S(1)} collective-permute-done((bf16[256,1024]{1,0:T(8,128)(2,1)S(1)}, bf16[256,1024]{1,0:T(8,128)(2,1)S(1)}, u32[]{:S(2)}, u32[]{:S(2)}) %collective-permute-start.14) | collective-permute-done | bytes 524320 | tf_op jit(solution)/shard_map/ppermute | solution.py:36
  54.0 0.1 join.21.w0
  54.1 0.1 join.22.w_ref
  54.2 4.4 %grad_in.3 = (bf16[2,512,512]{2,1,0:T(8,128)(2,1)S(1)}, bf16[256,1024]{1,0:T(8,128)(2,1)S(1)}, bf16[256,1024]{1,0:T(8,128)(2,1)S(1)}) custom-call(bf16[2,512,1024]{2,1,0:T(8,128)(2,1)S(1)} %get-tuple-element.463.resid_ref, bf16[512,1024]{1,0:T(8,128)(2,1)S(1)} %join.22.w_ref, f32[512,512]{1,0:T(8,128)S(1)} %get-tuple-element.465.slope_own, ...), custom_call_target="tpu_custom_call" | custom-call | tf_op jit(solution)/shard_map/grad_in/pallas_call | solution.py:265
  58.6 0.6 collective-permute-start.15
  59.2 1.5 %collective-permute-start.22 = (bf16[256,1024]{1,0:T(8,128)(2,1)S(1)}, bf16[256,1024]{1,0:T(8,128)(2,1)S(1)}, u32[]{:S(2)}, u32[]{:S(2)}) collective-permute-start(bf16[256,1024]{1,0:T(8,128)(2,1)S(1)} %get-tuple-element.510), channel_id=1, source_target_pairs={{0,2},{1,3},{2,0},{3,1},{4,6},{5,7},{6,4},{7,5},{8,10},{9,11},{10,... | collective-permute-start | bytes 1572872 | tf_op jit(solution)/shard_map/ppermute | solution.py:36
  60.7 0.2 collective-permute-start.21
  61.0 4.3 %collective-permute-done.17.b_ref = bf16[256,1024]{1,0:T(8,128)(2,1)S(1)} collective-permute-done((bf16[256,1024]{1,0:T(8,128)(2,1)S(1)}, bf16[256,1024]{1,0:T(8,128)(2,1)S(1)}, u32[]{:S(2)}, u32[]{:S(2)}) %collective-permute-start.17) | collective-permute-done | bytes 524320 | tf_op jit(solution)/shard_map/ppermute | solution.py:36
  65.2 0.1 fold.8
  65.4 0.1 fold.9
  65.5 4.0 %collective-permute-done.15.a_ref = bf16[256,1024]{1,0:T(8,128)(2,1)S(1)} collective-permute-done((bf16[256,1024]{1,0:T(8,128)(2,1)S(1)}, bf16[256,1024]{1,0:T(8,128)(2,1)S(1)}, u32[]{:S(2)}, u32[]{:S(2)}) %collective-permute-start.15) | collective-permute-done | bytes 524320 | tf_op jit(solution)/shard_map/ppermute | solution.py:555
  69.6 1.7 %collective-permute-start.18 = (bf16[256,1024]{1,0:T(8,128)(2,1)S(1)}, bf16[256,1024]{1,0:T(8,128)(2,1)S(1)}, u32[]{:S(2)}, u32[]{:S(2)}) collective-permute-start(bf16[256,1024]{1,0:T(8,128)(2,1)S(1)} %collective-permute-done.14.b_ref), channel_id=1, source_target_pairs={{0,16},{16,0},{1,17},{17,1},{2,18},{18,2},{3,19},{19,3},{4,20},{20... | collective-permute-start | bytes 1572872 | tf_op jit(solution)/shard_map/ppermute | solution.py:555
  71.3 1.5 %collective-permute-start.20 = (bf16[128,1024]{1,0:T(8,128)(2,1)S(1)}, bf16[128,1024]{1,0:T(8,128)(2,1)S(1)}, u32[]{:S(2)}, u32[]{:S(2)}) collective-permute-start(bf16[128,1024]{1,0:T(8,128)(2,1)S(1)} %get-tuple-element.506), channel_id=1, source_target_pairs={{0,2},{1,3},{2,0},{3,1},{4,6},{5,7},{6,4},{7,5},{8,10},{9,11},{10,... | collective-permute-start | bytes 786440 | tf_op jit(solution)/shard_map/ppermute | solution.py:36
  72.8 1.6 %collective-permute-start.19 = (bf16[128,1024]{1,0:T(8,128)(2,1)S(1)}, bf16[128,1024]{1,0:T(8,128)(2,1)S(1)}, u32[]{:S(2)}, u32[]{:S(2)}) collective-permute-start(bf16[128,1024]{1,0:T(8,128)(2,1)S(1)} %get-tuple-element.504), channel_id=1, source_target_pairs={{0,8},{1,9},{2,10},{3,11},{4,12},{5,13},{6,14},{7,15},{8,0},{9,1},... | collective-permute-start | bytes 786440 | tf_op jit(solution)/shard_map/ppermute | solution.py:36
  74.4 0.1 fold.10
  74.5 2.1 %collective-permute-start.24 = (bf16[128,1024]{1,0:T(8,128)(2,1)S(1)}, bf16[128,1024]{1,0:T(8,128)(2,1)S(1)}, u32[]{:S(2)}, u32[]{:S(2)}) collective-permute-start(bf16[128,1024]{1,0:T(8,128)(2,1)S(1)} %get-tuple-element.554), channel_id=1, source_target_pairs={{0,4},{1,5},{2,6},{3,7},{4,0},{5,1},{6,2},{7,3},{8,12},{9,13},{10,... | collective-permute-start | bytes 786440 | tf_op jit(solution)/shard_map/ppermute | solution.py:36
  76.6 2.4 %collective-permute-done.21.b_ref = bf16[256,1024]{1,0:T(8,128)(2,1)S(1)} collective-permute-done((bf16[256,1024]{1,0:T(8,128)(2,1)S(1)}, bf16[256,1024]{1,0:T(8,128)(2,1)S(1)}, u32[]{:S(2)}, u32[]{:S(2)}) %collective-permute-start.21) | collective-permute-done | bytes 524320 | tf_op jit(solution)/shard_map/ppermute | solution.py:36
  79.0 0.1 fold.11
  79.1 0.1 collective-permute-start.26
  79.3 2.7 %collective-permute-start.27 = (bf16[64,1024]{1,0:T(8,128)(2,1)S(1)}, bf16[64,1024]{1,0:T(8,128)(2,1)S(1)}, u32[]{:S(2)}, u32[]{:S(2)}) collective-permute-start(bf16[64,1024]{1,0:T(8,128)(2,1)S(1)} %get-tuple-element.571), channel_id=1, source_target_pairs={{0,8},{1,9},{2,10},{3,11},{4,12},{5,13},{6,14},{7,15},{8,0},{9,1},... | collective-permute-start | bytes 393224 | tf_op jit(solution)/shard_map/ppermute | solution.py:36
  82.0 5.2 %collective-permute-done.19.b_ref = bf16[128,1024]{1,0:T(8,128)(2,1)S(1)} collective-permute-done((bf16[128,1024]{1,0:T(8,128)(2,1)S(1)}, bf16[128,1024]{1,0:T(8,128)(2,1)S(1)}, u32[]{:S(2)}, u32[]{:S(2)}) %collective-permute-start.19) | collective-permute-done | bytes 262176 | tf_op jit(solution)/shard_map/ppermute | solution.py:36
  87.3 0.1 join.23.w1
  87.3 0.7 input_nb.2
  88.1 1.2 %collective-permute-start.28 = (bf16[64,1024]{1,0:T(8,128)(2,1)S(1)}, bf16[64,1024]{1,0:T(8,128)(2,1)S(1)}, u32[]{:S(2)}, u32[]{:S(2)}) collective-permute-start(bf16[64,1024]{1,0:T(8,128)(2,1)S(1)} %get-tuple-element.574), channel_id=1, source_target_pairs={{0,8},{1,9},{2,10},{3,11},{4,12},{5,13},{6,14},{7,15},{8,0},{9,1},... | collective-permute-start | bytes 393224 | tf_op jit(solution)/shard_map/ppermute | solution.py:36
  89.4 0.7 input_nb.3
  90.1 0.1 collective-permute-start.25
  90.2 0.5 collective-permute-start.23
  90.7 1.4 %collective-permute-done.27.refs_1_ = bf16[64,1024]{1,0:T(8,128)(2,1)S(1)} collective-permute-done((bf16[64,1024]{1,0:T(8,128)(2,1)S(1)}, bf16[64,1024]{1,0:T(8,128)(2,1)S(1)}, u32[]{:S(2)}, u32[]{:S(2)}) %collective-permute-start.27) | collective-permute-done | bytes 131104 | tf_op jit(solution)/shard_map/ppermute | solution.py:36
  92.1 3.2 %collective-permute-done.28.refs_3_ = bf16[64,1024]{1,0:T(8,128)(2,1)S(1)} collective-permute-done((bf16[64,1024]{1,0:T(8,128)(2,1)S(1)}, bf16[64,1024]{1,0:T(8,128)(2,1)S(1)}, u32[]{:S(2)}, u32[]{:S(2)}) %collective-permute-start.28) | collective-permute-done | bytes 131104 | tf_op jit(solution)/shard_map/ppermute | solution.py:36
  95.3 1.4 %total.2 = f32[128,1024]{1,0:T(8,128)} custom-call(s32[2]{0:T(128)S(1)} %copy-done.5, bf16[64,1024]{1,0:T(8,128)(2,1)S(1)} %get-tuple-element.570.refs_0_, bf16[64,1024]{1,0:T(8,128)(2,1)S(1)} %collective-permute-done.27.refs_1_, bf16[64,1024]{1,0:T(8,128)(2,1)S(1)} %get-tuple-element.577.refs_2_, bf16[64,1024]{1,0:T(8,128)(2,1)S(1)} %collective-permute-done.28.refs_3_, ...), custom_call_target="tpu_custom_call" | custom-call | tf_op jit(solution)/shard_map/total/pallas_call | solution.py:449
  96.8 0.1 collective-permute-start.30
  96.9 2.4 %input_own.1 = bf16[512,1024]{1,0:T(8,128)(2,1)} custom-call(bf16[2,512,512]{2,1,0:T(8,128)(2,1)S(1)} %get-tuple-element.432.pre0, bf16[2,512,512]{2,1,0:T(8,128)(2,1)S(1)} %get-tuple-element.473.pre1, bf16[512,1024]{1,0:T(8,128)(2,1)S(1)} %join.21.w0, bf16[512,1024]{1,0:T(8,128)(2,1)S(1)} %join.23.w1, ...), custom_call_target="tpu_custom_call" | custom-call | tf_op jit(solution)/shard_map/input_own/pallas_call | solution.py:334
  99.3 4.1 %collective-permute-done.30.refs_3_ = bf16[64,1024]{1,0:T(8,128)(2,1)S(1)} collective-permute-done((bf16[64,1024]{1,0:T(8,128)(2,1)S(1)}, bf16[64,1024]{1,0:T(8,128)(2,1)S(1)}, u32[]{:S(2)}, u32[]{:S(2)}) %collective-permute-start.30) | collective-permute-done | bytes 131104 | tf_op jit(solution)/shard_map/ppermute | solution.py:36
  103.4 1.4 %total.3 = f32[128,1024]{1,0:T(8,128)} custom-call(s32[2]{0:T(128)S(1)} %copy-done.5, bf16[64,1024]{1,0:T(8,128)(2,1)S(1)} %get-tuple-element.594.refs_0_, bf16[64,1024]{1,0:T(8,128)(2,1)S(1)} %collective-permute-done.29.refs_1_, bf16[64,1024]{1,0:T(8,128)(2,1)S(1)} %get-tuple-element.601.refs_2_, bf16[64,1024]{1,0:T(8,128)(2,1)S(1)} %collective-permute-done.30.refs_3_, ...), custom_call_target="tpu_custom_call" | custom-call | tf_op jit(solution)/shard_map/total/pallas_call | solution.py:449
  (64 shorter events, 0.5 us)
Async XLA Ops:
  0.6 25.6 %collective-permute-start.7 = (bf16[512,2048]{1,0:T(8,128)(2,1)}, bf16[512,2048]{1,0:T(8,128)(2,1)}, u32[]{:S(2)}, u32[]{:S(2)}) collective-permute-start(bf16[512,2048]{1,0:T(8,128)(2,1)} %in_ref), channel_id=1, source_target_pairs={{0,1},{1,0},{2,3},{3,2},{4,5},{5,4},{6,7},{7,6},{8,9},{9,8},{10,11... | collective-permute-start | bytes 6291464 | tf_op jit(solution)/shard_map/ppermute | solution.py:36
  1.1 14.1 %collective-permute-start = (bf16[512,1024]{1,0:T(8,128)(2,1)}, bf16[512,1024]{1,0:T(8,128)(2,1)}, u32[]{:S(2)}, u32[]{:S(2)}) collective-permute-start(bf16[512,1024]{1,0:T(8,128)(2,1)} %own_ref), channel_id=1, source_target_pairs={{0,1},{1,0},{2,3},{3,2},{4,5},{5,4},{6,7},{7,6},{8,9},{9,8},{10,11... | collective-permute-start | bytes 3145736 | tf_op jit(solution)/shard_map/ppermute | solution.py:36
  2.2 10.6 %collective-permute-start.1 = (bf16[64,1024]{1,0:T(8,128)(2,1)S(1)}, bf16[64,1024]{1,0:T(8,128)(2,1)S(1)}, u32[]{:S(2)}, u32[]{:S(2)}) collective-permute-start(bf16[64,1024]{1,0:T(8,128)(2,1)S(1)} %get-tuple-element.317.a_ref), channel_id=1, source_target_pairs={{0,8},{1,9},{2,10},{3,11},{4,12},{5,13},{6,14},{7,15},{8,0},{9,1},... | collective-permute-start | bytes 393224 | tf_op jit(solution)/shard_map/ppermute | solution.py:36
  6.3 25.5 %collective-permute-start.8 = (bf16[512,1024]{1,0:T(8,128)(2,1)}, bf16[512,1024]{1,0:T(8,128)(2,1)}, u32[]{:S(2)}, u32[]{:S(2)}) collective-permute-start(bf16[512,1024]{1,0:T(8,128)(2,1)} %own_ref.2), channel_id=1, source_target_pairs={{0,1},{1,0},{2,3},{3,2},{4,5},{5,4},{6,7},{7,6},{8,9},{9,8},{10,11... | collective-permute-start | bytes 3145736 | tf_op jit(solution)/shard_map/ppermute | solution.py:36
  12.9 2.4 %copy-start.3 = (bf16[8,1024]{1,0:T(8,128)(2,1)S(1)}, bf16[8,1024]{1,0:T(8,128)(2,1)}, u32[]{:S(2)}) copy-start(bf16[8,1024]{1,0:T(8,128)(2,1)} %pack.1.a_ref) | copy-start | bytes 49156
  12.9 2.9 %copy-start.2 = (bf16[512,2048]{1,0:T(8,128)(2,1)S(1)}, bf16[512,2048]{1,0:T(8,128)(2,1)}, u32[]{:S(2)}) copy-start(bf16[512,2048]{1,0:T(8,128)(2,1)} %in_ref) | copy-start | bytes 6291460
  12.9 2.8 %copy-start.5 = (s32[2]{0:T(128)S(1)}, s32[2]{0:T(128)}, u32[]{:S(2)}) copy-start(s32[2]{0:T(128)} %pad_add_fusion.ids_ref) | copy-start | bytes 28
  12.9 9.7 %collective-permute-start.4 = (bf16[128,1024]{1,0:T(8,128)(2,1)S(1)}, bf16[128,1024]{1,0:T(8,128)(2,1)S(1)}, u32[]{:S(2)}, u32[]{:S(2)}) collective-permute-start(bf16[128,1024]{1,0:T(8,128)(2,1)S(1)} %join.12.a_ref), channel_id=1, source_target_pairs={{0,4},{1,5},{2,6},{3,7},{4,0},{5,1},{6,2},{7,3},{8,12},{9,13},{10,... | collective-permute-start | bytes 786440 | tf_op jit(solution)/shard_map/ppermute | solution.py:36
  13.7 8.9 %collective-permute-start.5 = (bf16[64,1024]{1,0:T(8,128)(2,1)S(1)}, bf16[64,1024]{1,0:T(8,128)(2,1)S(1)}, u32[]{:S(2)}, u32[]{:S(2)}) collective-permute-start(bf16[64,1024]{1,0:T(8,128)(2,1)S(1)} %get-tuple-element.344.a_ref), channel_id=1, source_target_pairs={{0,2},{1,3},{2,0},{3,1},{4,6},{5,7},{6,4},{7,5},{8,10},{9,11},{10,... | collective-permute-start | bytes 393224 | tf_op jit(solution)/shard_map/ppermute | solution.py:36
  15.2 4.0 %collective-permute-start.2 = (bf16[8,1024]{1,0:T(8,128)(2,1)S(1)}, bf16[8,1024]{1,0:T(8,128)(2,1)S(1)}, u32[]{:S(2)}, u32[]{:S(2)}) collective-permute-start(bf16[8,1024]{1,0:T(8,128)(2,1)S(1)} %copy-done.3), channel_id=1, source_target_pairs={{0,2},{1,3},{2,0},{3,1},{4,6},{5,7},{6,4},{7,5},{8,10},{9,11},{10,... | collective-permute-start | bytes 49160 | tf_op jit(solution)/shard_map/ppermute | solution.py:36
  19.2 6.6 %collective-permute-start.3 = (bf16[16,1024]{1,0:T(8,128)(2,1)S(1)}, bf16[16,1024]{1,0:T(8,128)(2,1)S(1)}, u32[]{:S(2)}, u32[]{:S(2)}) collective-permute-start(bf16[16,1024]{1,0:T(8,128)(2,1)S(1)} %join.13.a_ref), channel_id=1, source_target_pairs={{0,8},{1,9},{2,10},{3,11},{4,12},{5,13},{6,14},{7,15},{8,0},{9,1},... | collective-permute-start | bytes 98312 | tf_op jit(solution)/shard_map/ppermute | solution.py:36
  22.7 14.5 %collective-permute-start.12 = (bf16[256,1024]{1,0:T(8,128)(2,1)S(1)}, bf16[256,1024]{1,0:T(8,128)(2,1)S(1)}, u32[]{:S(2)}, u32[]{:S(2)}) collective-permute-start(bf16[256,1024]{1,0:T(8,128)(2,1)S(1)} %join.15.a_ref), channel_id=1, source_target_pairs={{0,16},{16,0},{1,17},{17,1},{2,18},{18,2},{3,19},{19,3},{4,20},{20... | collective-permute-start | bytes 1572872 | tf_op jit(solution)/shard_map/ppermute | solution.py:555
  24.3 12.8 %collective-permute-start.10 = (bf16[256,1024]{1,0:T(8,128)(2,1)S(1)}, bf16[256,1024]{1,0:T(8,128)(2,1)S(1)}, u32[]{:S(2)}, u32[]{:S(2)}) collective-permute-start(bf16[256,1024]{1,0:T(8,128)(2,1)S(1)} %join.15.a_ref), channel_id=1, source_target_pairs={{0,2},{1,3},{2,0},{3,1},{4,6},{5,7},{6,4},{7,5},{8,10},{9,11},{10,... | collective-permute-start | bytes 1572872 | tf_op jit(solution)/shard_map/ppermute | solution.py:36
  25.8 6.0 %collective-permute-start.6 = (bf16[32,1024]{1,0:T(8,128)(2,1)S(1)}, bf16[32,1024]{1,0:T(8,128)(2,1)S(1)}, u32[]{:S(2)}, u32[]{:S(2)}) collective-permute-start(bf16[32,1024]{1,0:T(8,128)(2,1)S(1)} %join.16.a_ref), channel_id=1, source_target_pairs={{0,4},{1,5},{2,6},{3,7},{4,0},{5,1},{6,2},{7,3},{8,12},{9,13},{10,... | collective-permute-start | bytes 196616 | tf_op jit(solution)/shard_map/ppermute | solution.py:36
  26.2 12.8 %collective-permute-start.11 = (bf16[128,1024]{1,0:T(8,128)(2,1)S(1)}, bf16[128,1024]{1,0:T(8,128)(2,1)S(1)}, u32[]{:S(2)}, u32[]{:S(2)}) collective-permute-start(bf16[128,1024]{1,0:T(8,128)(2,1)S(1)} %join.14.a_ref), channel_id=1, source_target_pairs={{0,8},{1,9},{2,10},{3,11},{4,12},{5,13},{6,14},{7,15},{8,0},{9,1},... | collective-permute-start | bytes 786440 | tf_op jit(solution)/shard_map/ppermute | solution.py:36
  31.8 1.5 %copy-start.1 = (bf16[512,1024]{1,0:T(8,128)(2,1)S(1)}, bf16[512,1024]{1,0:T(8,128)(2,1)}, u32[]{:S(2)}) copy-start(bf16[512,1024]{1,0:T(8,128)(2,1)} %own_ref) | copy-start | bytes 3145732
  31.8 1.5 %copy-start.4 = (f32[1024]{0:T(1024)S(1)}, f32[1024]{0:T(1024)}, u32[]{:S(2)}) copy-start(f32[1024]{0:T(1024)} %param.16) | copy-start | bytes 12292
  31.8 1.4 %collective-permute-start.9 = (bf16[64,1024]{1,0:T(8,128)(2,1)S(1)}, bf16[64,1024]{1,0:T(8,128)(2,1)S(1)}, u32[]{:S(2)}, u32[]{:S(2)}) collective-permute-start(bf16[64,1024]{1,0:T(8,128)(2,1)S(1)} %join.17.a_ref), channel_id=1, source_target_pairs={{0,1},{1,0},{2,3},{3,2},{4,5},{5,4},{6,7},{7,6},{8,9},{9,8},{10,11... | collective-permute-start | bytes 393224 | tf_op jit(solution)/shard_map/ppermute | solution.py:36
  37.2 4.5 %copy-start = (bf16[512,1024]{1,0:T(8,128)(2,1)S(1)}, bf16[512,1024]{1,0:T(8,128)(2,1)}, u32[]{:S(2)}) copy-start(bf16[512,1024]{1,0:T(8,128)(2,1)} %own_ref.2) | copy-start | bytes 3145732
  39.1 14.9 %collective-permute-start.14 = (bf16[256,1024]{1,0:T(8,128)(2,1)S(1)}, bf16[256,1024]{1,0:T(8,128)(2,1)S(1)}, u32[]{:S(2)}, u32[]{:S(2)}) collective-permute-start(bf16[256,1024]{1,0:T(8,128)(2,1)S(1)} %join.20.a_ref), channel_id=1, source_target_pairs={{0,4},{1,5},{2,6},{3,7},{4,0},{5,1},{6,2},{7,3},{8,12},{9,13},{10,... | collective-permute-start | bytes 1572872 | tf_op jit(solution)/shard_map/ppermute | solution.py:36
  39.2 14.9 %collective-permute-start.13 = (bf16[256,1024]{1,0:T(8,128)(2,1)S(1)}, bf16[256,1024]{1,0:T(8,128)(2,1)S(1)}, u32[]{:S(2)}, u32[]{:S(2)}) collective-permute-start(bf16[256,1024]{1,0:T(8,128)(2,1)S(1)} %collective-permute-done.10.b_ref), channel_id=1, source_target_pairs={{0,16},{16,0},{1,17},{17,1},{2,18},{18,2},{3,19},{19,3},{4,20},{20... | collective-permute-start | bytes 1572872 | tf_op jit(solution)/shard_map/ppermute | solution.py:555
  47.4 17.8 %collective-permute-start.17 = (bf16[256,1024]{1,0:T(8,128)(2,1)S(1)}, bf16[256,1024]{1,0:T(8,128)(2,1)S(1)}, u32[]{:S(2)}, u32[]{:S(2)}) collective-permute-start(bf16[256,1024]{1,0:T(8,128)(2,1)S(1)} %get-tuple-element.482), channel_id=1, source_target_pairs={{0,4},{1,5},{2,6},{3,7},{4,0},{5,1},{6,2},{7,3},{8,12},{9,13},{10,... | collective-permute-start | bytes 1572872 | tf_op jit(solution)/shard_map/ppermute | solution.py:36
  49.2 16.2 %collective-permute-start.16 = (bf16[256,1024]{1,0:T(8,128)(2,1)S(1)}, bf16[256,1024]{1,0:T(8,128)(2,1)S(1)}, u32[]{:S(2)}, u32[]{:S(2)}) collective-permute-start(bf16[256,1024]{1,0:T(8,128)(2,1)S(1)} %get-tuple-element.480), channel_id=1, source_target_pairs={{0,2},{1,3},{2,0},{3,1},{4,6},{5,7},{6,4},{7,5},{8,10},{9,11},{10,... | collective-permute-start | bytes 1572872 | tf_op jit(solution)/shard_map/ppermute | solution.py:36
  58.6 11.0 %collective-permute-start.15 = (bf16[256,1024]{1,0:T(8,128)(2,1)S(1)}, bf16[256,1024]{1,0:T(8,128)(2,1)S(1)}, u32[]{:S(2)}, u32[]{:S(2)}) collective-permute-start(bf16[256,1024]{1,0:T(8,128)(2,1)S(1)} %join.20.a_ref), channel_id=1, source_target_pairs={{0,16},{16,0},{1,17},{17,1},{2,18},{18,2},{3,19},{19,3},{4,20},{20... | collective-permute-start | bytes 1572872 | tf_op jit(solution)/shard_map/ppermute | solution.py:555
  59.2 15.2 %collective-permute-start.22 = (bf16[256,1024]{1,0:T(8,128)(2,1)S(1)}, bf16[256,1024]{1,0:T(8,128)(2,1)S(1)}, u32[]{:S(2)}, u32[]{:S(2)}) collective-permute-start(bf16[256,1024]{1,0:T(8,128)(2,1)S(1)} %get-tuple-element.510), channel_id=1, source_target_pairs={{0,2},{1,3},{2,0},{3,1},{4,6},{5,7},{6,4},{7,5},{8,10},{9,11},{10,... | collective-permute-start | bytes 1572872 | tf_op jit(solution)/shard_map/ppermute | solution.py:36
  60.7 18.3 %collective-permute-start.21 = (bf16[256,1024]{1,0:T(8,128)(2,1)S(1)}, bf16[256,1024]{1,0:T(8,128)(2,1)S(1)}, u32[]{:S(2)}, u32[]{:S(2)}) collective-permute-start(bf16[256,1024]{1,0:T(8,128)(2,1)S(1)} %get-tuple-element.508), channel_id=1, source_target_pairs={{0,4},{1,5},{2,6},{3,7},{4,0},{5,1},{6,2},{7,3},{8,12},{9,13},{10,... | collective-permute-start | bytes 1572872 | tf_op jit(solution)/shard_map/ppermute | solution.py:36
  69.6 17.7 %collective-permute-start.18 = (bf16[256,1024]{1,0:T(8,128)(2,1)S(1)}, bf16[256,1024]{1,0:T(8,128)(2,1)S(1)}, u32[]{:S(2)}, u32[]{:S(2)}) collective-permute-start(bf16[256,1024]{1,0:T(8,128)(2,1)S(1)} %collective-permute-done.14.b_ref), channel_id=1, source_target_pairs={{0,16},{16,0},{1,17},{17,1},{2,18},{18,2},{3,19},{19,3},{4,20},{20... | collective-permute-start | bytes 1572872 | tf_op jit(solution)/shard_map/ppermute | solution.py:555
  71.3 7.9 %collective-permute-start.20 = (bf16[128,1024]{1,0:T(8,128)(2,1)S(1)}, bf16[128,1024]{1,0:T(8,128)(2,1)S(1)}, u32[]{:S(2)}, u32[]{:S(2)}) collective-permute-start(bf16[128,1024]{1,0:T(8,128)(2,1)S(1)} %get-tuple-element.506), channel_id=1, source_target_pairs={{0,2},{1,3},{2,0},{3,1},{4,6},{5,7},{6,4},{7,5},{8,10},{9,11},{10,... | collective-permute-start | bytes 786440 | tf_op jit(solution)/shard_map/ppermute | solution.py:36
  72.8 14.3 %collective-permute-start.19 = (bf16[128,1024]{1,0:T(8,128)(2,1)S(1)}, bf16[128,1024]{1,0:T(8,128)(2,1)S(1)}, u32[]{:S(2)}, u32[]{:S(2)}) collective-permute-start(bf16[128,1024]{1,0:T(8,128)(2,1)S(1)} %get-tuple-element.504), channel_id=1, source_target_pairs={{0,8},{1,9},{2,10},{3,11},{4,12},{5,13},{6,14},{7,15},{8,0},{9,1},... | collective-permute-start | bytes 786440 | tf_op jit(solution)/shard_map/ppermute | solution.py:36
  74.5 13.5 %collective-permute-start.24 = (bf16[128,1024]{1,0:T(8,128)(2,1)S(1)}, bf16[128,1024]{1,0:T(8,128)(2,1)S(1)}, u32[]{:S(2)}, u32[]{:S(2)}) collective-permute-start(bf16[128,1024]{1,0:T(8,128)(2,1)S(1)} %get-tuple-element.554), channel_id=1, source_target_pairs={{0,4},{1,5},{2,6},{3,7},{4,0},{5,1},{6,2},{7,3},{8,12},{9,13},{10,... | collective-permute-start | bytes 786440 | tf_op jit(solution)/shard_map/ppermute | solution.py:36
  79.1 17.5 %collective-permute-start.26 = (bf16[128,1024]{1,0:T(8,128)(2,1)S(1)}, bf16[128,1024]{1,0:T(8,128)(2,1)S(1)}, u32[]{:S(2)}, u32[]{:S(2)}) collective-permute-start(bf16[128,1024]{1,0:T(8,128)(2,1)S(1)} %get-tuple-element.569), channel_id=1, source_target_pairs={{0,2},{1,3},{2,0},{3,1},{4,6},{5,7},{6,4},{7,5},{8,10},{9,11},{10,... | collective-permute-start | bytes 786440 | tf_op jit(solution)/shard_map/ppermute | solution.py:36
  79.3 12.8 %collective-permute-start.27 = (bf16[64,1024]{1,0:T(8,128)(2,1)S(1)}, bf16[64,1024]{1,0:T(8,128)(2,1)S(1)}, u32[]{:S(2)}, u32[]{:S(2)}) collective-permute-start(bf16[64,1024]{1,0:T(8,128)(2,1)S(1)} %get-tuple-element.571), channel_id=1, source_target_pairs={{0,8},{1,9},{2,10},{3,11},{4,12},{5,13},{6,14},{7,15},{8,0},{9,1},... | collective-permute-start | bytes 393224 | tf_op jit(solution)/shard_map/ppermute | solution.py:36
  88.1 7.1 %collective-permute-start.28 = (bf16[64,1024]{1,0:T(8,128)(2,1)S(1)}, bf16[64,1024]{1,0:T(8,128)(2,1)S(1)}, u32[]{:S(2)}, u32[]{:S(2)}) collective-permute-start(bf16[64,1024]{1,0:T(8,128)(2,1)S(1)} %get-tuple-element.574), channel_id=1, source_target_pairs={{0,8},{1,9},{2,10},{3,11},{4,12},{5,13},{6,14},{7,15},{8,0},{9,1},... | collective-permute-start | bytes 393224 | tf_op jit(solution)/shard_map/ppermute | solution.py:36
  90.1 6.8 %collective-permute-start.25 = (bf16[256,1024]{1,0:T(8,128)(2,1)S(1)}, bf16[256,1024]{1,0:T(8,128)(2,1)S(1)}, u32[]{:S(2)}, u32[]{:S(2)}) collective-permute-start(bf16[256,1024]{1,0:T(8,128)(2,1)S(1)} %input_nb.3), channel_id=1, source_target_pairs={{0,1},{1,0},{2,3},{3,2},{4,5},{5,4},{6,7},{7,6},{8,9},{9,8},{10,11... | collective-permute-start | bytes 1572872 | tf_op jit(solution)/shard_map/ppermute | solution.py:36
  90.2 6.7 %collective-permute-start.23 = (bf16[256,1024]{1,0:T(8,128)(2,1)S(1)}, bf16[256,1024]{1,0:T(8,128)(2,1)S(1)}, u32[]{:S(2)}, u32[]{:S(2)}) collective-permute-start(bf16[256,1024]{1,0:T(8,128)(2,1)S(1)} %input_nb.2), channel_id=1, source_target_pairs={{0,1},{1,0},{2,3},{3,2},{4,5},{5,4},{6,7},{7,6},{8,9},{9,8},{10,11... | collective-permute-start | bytes 1572872 | tf_op jit(solution)/shard_map/ppermute | solution.py:36
  92.1 7.2 %collective-permute-start.29 = (bf16[64,1024]{1,0:T(8,128)(2,1)S(1)}, bf16[64,1024]{1,0:T(8,128)(2,1)S(1)}, u32[]{:S(2)}, u32[]{:S(2)}) collective-permute-start(bf16[64,1024]{1,0:T(8,128)(2,1)S(1)} %get-tuple-element.595), channel_id=1, source_target_pairs={{0,4},{1,5},{2,6},{3,7},{4,0},{5,1},{6,2},{7,3},{8,12},{9,13},{10,... | collective-permute-start | bytes 393224 | tf_op jit(solution)/shard_map/ppermute | solution.py:36
  96.8 6.7 %collective-permute-start.30 = (bf16[64,1024]{1,0:T(8,128)(2,1)S(1)}, bf16[64,1024]{1,0:T(8,128)(2,1)S(1)}, u32[]{:S(2)}, u32[]{:S(2)}) collective-permute-start(bf16[64,1024]{1,0:T(8,128)(2,1)S(1)} %get-tuple-element.596), channel_id=1, source_target_pairs={{0,8},{1,9},{2,10},{3,11},{4,12},{5,13},{6,14},{7,15},{8,0},{9,1},... | collective-permute-start | bytes 393224 | tf_op jit(solution)/shard_map/ppermute | solution.py:36

commit v6 on v5

--- a/solution.py
+++ b/solution.py
@@ -432,14 +432,17 @@
 
 
 def total_kernel(ids_ref, *refs):
-    *parts, mark_ref, out_ref = refs
-    rows = out_ref.shape[0] // 2
-    sums = [a[...].astype(F32) + b[...].astype(F32) for a, b in zip(parts[::2], parts[1::2])]
-    if len(sums) == 1:
-        sums = [sums[0][:rows], sums[0][rows:]]
-    for k, x in enumerate(sums):
+    *parts, mark_ref, out_ref, sum_ref, sems = refs
+    rows = sum_ref.shape[1]
+    copies = []
+    for k in range(2):
+        sum_ref[k] = parts[2 * k][...].astype(F32) + parts[2 * k + 1][...].astype(F32)
         start = k * rows + (1 - 2 * k) * ids_ref[1] * rows
-        out_ref[pl.ds(pl.multiple_of(start, rows), rows)] = x
+        there = out_ref.at[pl.ds(pl.multiple_of(start, rows), rows)]
+        copies.append(pltpu.make_async_copy(sum_ref.at[k], there, sems.at[k]))
+        copies[k].start()
+    for copy in copies:
+        copy.wait()
 
 
 def total(ids, mark, *chains):
@@ -449,6 +452,8 @@
     return pl.pallas_call(
         total_kernel,
         in_specs=[pl.BlockSpec(memory_space=pltpu.SMEM)] + [vmem] * (len(parts) + 1),
+        out_specs=pl.BlockSpec(memory_space=pl.ANY),
+        scratch_shapes=[pltpu.VMEM((2, rows // 2, parts[0].shape[1]), F32), pltpu.SemaphoreType.DMA((2,))],
         out_shape=jax.ShapeDtypeStruct((rows, parts[0].shape[1]), F32),
         compiler_params=params(6),
         cost_estimate=FREE,

time: 105 us -> 105 us (level)
  no operation moved by 1% of the time
where the time goes in v6:
time: 105 us
  starting transfers between devices  35 us (33%)
  waiting for transfers between devices  34.8 us (33%)
  Pallas kernels  32.2 us (31%)
  between operations  1.31 us (1%)
    ppermute x27, waiting for transfers between devices, swap(): return lax.ppermute(x, 'psg', [(i, i ^ mask) for i in range(n)])  30.8 us
    ppermute x27, starting transfers between devices, swap(): return lax.ppermute(x, 'psg', [(i, i ^ mask) for i in range(n)])  30.2 us
    pallas_call x2, Pallas kernels, grad_in_part(): pl.pallas_call(functools.partial(grad_in_kernel, rows), grid=(units // bl...  8.58 us
    pallas_call x2, Pallas kernels, gelu(): pl.pallas_call(functools.partial(gelu_kernel, half), grid_spec=pltpu.Pref...  5.21 us
    ppermute x4, starting transfers between devices, cross(): return lax.ppermute(x, 'groups', [(0, 1), (1, 0)])  4.84 us
    ppermute x4, waiting for transfers between devices, cross(): return lax.ppermute(x, 'groups', [(0, 1), (1, 0)])  4.04 us
    pallas_call x1, Pallas kernels, resid_grads(): pl.pallas_call(functools.partial(resid_kernel, slots, queries), grid=(tok...  3.77 us
    pallas_call x1, Pallas kernels, pack(): pl.pallas_call(functools.partial(pack_kernel, slots), out_shape=jax.Shape...  3.69 us
  transfers between devices with their start and end apart: 31, of which 12 were waited for; matrix products, arithmetic and copies ran while one was open for 2% of the time, Pallas kernels for 29%

profile of v6, /device:TPU:0, one launch (start us, length us, event | category | flops | bytes accessed | tf_op | source)
XLA Modules:
  0.0 104.9 jit_solution(1889185183543831208)
XLA Ops:
  0.6 0.5 collective-permute-start.7
  1.1 0.1 collective-permute-start
  1.2 1.0 constant_dynamic-slice_fusion
  2.2 4.1 %collective-permute-start.1 = (bf16[64,1024]{1,0:T(8,128)(2,1)S(1)}, bf16[64,1024]{1,0:T(8,128)(2,1)S(1)}, u32[]{:S(2)}, u32[]{:S(2)}) collective-permute-start(bf16[64,1024]{1,0:T(8,128)(2,1)S(1)} %get-tuple-element.317.a_ref), channel_id=1, source_target_pairs={{0,8},{1,9},{2,10},{3,11},{4,12},{5,13},{6,14},{7,15},{8,0},{9,1},... | collective-permute-start | bytes 393224 | tf_op jit(solution)/shard_map/ppermute | solution.py:36
  6.3 0.6 pad_add_fusion.ids_ref
  6.9 3.7 %pack.1.a_ref = bf16[8,1024]{1,0:T(8,128)(2,1)} custom-call(s32[2]{0:T(128)} %pad_add_fusion.ids_ref, s32[64]{0:T(128)} %place_in, s32[16]{0:T(128)} %live_in, bf16[512,1024]{1,0:T(8,128)(2,1)} %own_ref, f32[1,1024]{1,0:T(1,128)} %bitcast.3, bf16[2,1024]{1,0:T(2,128)(2,1)} %query_in, bf16[2,32]{1,0:T(2,128)(2,1)} %score_in, s32[2,32]{1,0:T(2,128)} %ret_in), custom_call_target="tpu_custom_call" | custom-call | tf_op jit(solution)/shard_map/pack/pallas_call | solution.py:90
  10.6 2.3 %collective-permute-done.1.b_ref = bf16[64,1024]{1,0:T(8,128)(2,1)S(1)} collective-permute-done((bf16[64,1024]{1,0:T(8,128)(2,1)S(1)}, bf16[64,1024]{1,0:T(8,128)(2,1)S(1)}, u32[]{:S(2)}, u32[]{:S(2)}) %collective-permute-start.1) | collective-permute-done | bytes 131104 | tf_op jit(solution)/shard_map/ppermute | solution.py:36
  12.9 0.8 collective-permute-start.4
  13.7 1.5 %collective-permute-start.5 = (bf16[64,1024]{1,0:T(8,128)(2,1)S(1)}, bf16[64,1024]{1,0:T(8,128)(2,1)S(1)}, u32[]{:S(2)}, u32[]{:S(2)}) collective-permute-start(bf16[64,1024]{1,0:T(8,128)(2,1)S(1)} %get-tuple-element.344.a_ref), channel_id=1, source_target_pairs={{0,2},{1,3},{2,0},{3,1},{4,6},{5,7},{6,4},{7,5},{8,10},{9,11},{10,... | collective-permute-start | bytes 393224 | tf_op jit(solution)/shard_map/ppermute | solution.py:36
  15.2 0.5 collective-permute-start.2
  15.8 2.0 %gelu.2 = (bf16[512,512]{1,0:T(8,128)(2,1)S(1)}, bf16[512,512]{1,0:T(8,128)(2,1)S(1)}, f32[512,512]{1,0:T(8,128)S(1)}, f32[512,512]{1,0:T(8,128)S(1)}) custom-call(s32[2]{0:T(128)S(1)} %copy-done.5, bf16[512,2048]{1,0:T(8,128)(2,1)S(1)} %copy-done.2), custom_call_target="tpu_custom_call" | custom-call | tf_op jit(solution)/shard_map/gelu/pallas_call | solution.py:204
  17.8 1.5 %collective-permute-done.2.b_ref = bf16[8,1024]{1,0:T(8,128)(2,1)S(1)} collective-permute-done((bf16[8,1024]{1,0:T(8,128)(2,1)S(1)}, bf16[8,1024]{1,0:T(8,128)(2,1)S(1)}, u32[]{:S(2)}, u32[]{:S(2)}) %collective-permute-start.2) | collective-permute-done | bytes 16416 | tf_op jit(solution)/shard_map/ppermute | solution.py:36
  19.2 3.4 %collective-permute-start.3 = (bf16[16,1024]{1,0:T(8,128)(2,1)S(1)}, bf16[16,1024]{1,0:T(8,128)(2,1)S(1)}, u32[]{:S(2)}, u32[]{:S(2)}) collective-permute-start(bf16[16,1024]{1,0:T(8,128)(2,1)S(1)} %join.13.a_ref), channel_id=1, source_target_pairs={{0,8},{1,9},{2,10},{3,11},{4,12},{5,13},{6,14},{7,15},{8,0},{9,1},... | collective-permute-start | bytes 98312 | tf_op jit(solution)/shard_map/ppermute | solution.py:36
  22.7 1.6 %collective-permute-start.12 = (bf16[256,1024]{1,0:T(8,128)(2,1)S(1)}, bf16[256,1024]{1,0:T(8,128)(2,1)S(1)}, u32[]{:S(2)}, u32[]{:S(2)}) collective-permute-start(bf16[256,1024]{1,0:T(8,128)(2,1)S(1)} %join.15.a_ref), channel_id=1, source_target_pairs={{0,16},{16,0},{1,17},{17,1},{2,18},{18,2},{3,19},{19,3},{4,20},{20... | collective-permute-start | bytes 1572872 | tf_op jit(solution)/shard_map/ppermute | solution.py:560
  24.3 1.5 %collective-permute-start.10 = (bf16[256,1024]{1,0:T(8,128)(2,1)S(1)}, bf16[256,1024]{1,0:T(8,128)(2,1)S(1)}, u32[]{:S(2)}, u32[]{:S(2)}) collective-permute-start(bf16[256,1024]{1,0:T(8,128)(2,1)S(1)} %join.15.a_ref), channel_id=1, source_target_pairs={{0,2},{1,3},{2,0},{3,1},{4,6},{5,7},{6,4},{7,5},{8,10},{9,11},{10,... | collective-permute-start | bytes 1572872 | tf_op jit(solution)/shard_map/ppermute | solution.py:36
  25.8 0.4 collective-permute-start.6
  26.2 2.3 %collective-permute-start.11 = (bf16[128,1024]{1,0:T(8,128)(2,1)S(1)}, bf16[128,1024]{1,0:T(8,128)(2,1)S(1)}, u32[]{:S(2)}, u32[]{:S(2)}) collective-permute-start(bf16[128,1024]{1,0:T(8,128)(2,1)S(1)} %join.14.a_ref), channel_id=1, source_target_pairs={{0,8},{1,9},{2,10},{3,11},{4,12},{5,13},{6,14},{7,15},{8,0},{9,1},... | collective-permute-start | bytes 786440 | tf_op jit(solution)/shard_map/ppermute | solution.py:36
  28.6 3.2 %gelu.3 = (bf16[512,512]{1,0:T(8,128)(2,1)S(1)}, bf16[512,512]{1,0:T(8,128)(2,1)S(1)}, f32[512,512]{1,0:T(8,128)S(1)}, f32[512,512]{1,0:T(8,128)S(1)}) custom-call(s32[2]{0:T(128)S(1)} %copy-done.5, bf16[512,2048]{1,0:T(8,128)(2,1)} %collective-permute-done.7.in_ref), custom_call_target="tpu_custom_call" | custom-call | tf_op jit(solution)/shard_map/gelu/pallas_call | solution.py:204
  31.8 0.1 collective-permute-start.9
  31.9 1.3 %collective-permute-done.9.b_ref = bf16[64,1024]{1,0:T(8,128)(2,1)S(1)} collective-permute-done((bf16[64,1024]{1,0:T(8,128)(2,1)S(1)}, bf16[64,1024]{1,0:T(8,128)(2,1)S(1)}, u32[]{:S(2)}, u32[]{:S(2)}) %collective-permute-start.9) | collective-permute-done | bytes 131104 | tf_op jit(solution)/shard_map/ppermute | solution.py:36
  33.3 3.8 %resid_grads.1 = (bf16[2,512,1024]{2,1,0:T(8,128)(2,1)S(1)}, f32[2,1024]{1,0:T(2,128)}) custom-call(bf16[512,1024]{1,0:T(8,128)(2,1)S(1)} %copy-done.1, bf16[512,1024]{1,0:T(8,128)(2,1)} %collective-permute-done.nb_ref, bf16[128,1024]{1,0:T(8,128)(2,1)S(1)} %join.18.all_ref, f32[1,1024]{1,0:T(1,128)S(1)} %bitcast.4), custom_call_target="tpu_custom_call" | custom-call | tf_op jit(solution)/shard_map/resid_grads/pallas_call | solution.py:153
  37.1 0.1 join.19.w_ref
  37.2 1.8 %collective-permute-done.11.b_ref = bf16[128,1024]{1,0:T(8,128)(2,1)S(1)} collective-permute-done((bf16[128,1024]{1,0:T(8,128)(2,1)S(1)}, bf16[128,1024]{1,0:T(8,128)(2,1)S(1)}, u32[]{:S(2)}, u32[]{:S(2)}) %collective-permute-start.11) | collective-permute-done | bytes 262176 | tf_op jit(solution)/shard_map/ppermute | solution.py:36
  39.1 0.1 collective-permute-start.14
  39.2 0.9 collective-permute-start.13
  40.1 1.6 %grad_out.2 = (bf16[256,1024]{1,0:T(8,128)(2,1)S(1)}, bf16[256,1024]{1,0:T(8,128)(2,1)S(1)}) custom-call(bf16[512,512]{1,0:T(8,128)(2,1)S(1)} %get-tuple-element.415.own_ref, bf16[512,512]{1,0:T(8,128)(2,1)S(1)} %get-tuple-element.416.nb_ref, bf16[2,512,1024]{2,1,0:T(8,128)(2,1)S(1)} %get-tuple-element.463.resid_ref), custom_call_target="tpu_custom_call" | custom-call | tf_op jit(solution)/shard_map/grad_out/pallas_call | solution.py:230
  41.6 4.2 %grad_in.2 = (bf16[2,512,512]{2,1,0:T(8,128)(2,1)S(1)}, bf16[256,1024]{1,0:T(8,128)(2,1)S(1)}, bf16[256,1024]{1,0:T(8,128)(2,1)S(1)}) custom-call(bf16[2,512,1024]{2,1,0:T(8,128)(2,1)S(1)} %get-tuple-element.463.resid_ref, bf16[512,1024]{1,0:T(8,128)(2,1)S(1)} %join.19.w_ref, f32[512,512]{1,0:T(8,128)S(1)} %get-tuple-element.424.slope_own, ...), custom_call_target="tpu_custom_call" | custom-call | tf_op jit(solution)/shard_map/grad_in/pallas_call | solution.py:265
  45.8 1.6 %grad_out.3 = (bf16[256,1024]{1,0:T(8,128)(2,1)S(1)}, bf16[256,1024]{1,0:T(8,128)(2,1)S(1)}) custom-call(bf16[512,512]{1,0:T(8,128)(2,1)S(1)} %get-tuple-element.441.own_ref, bf16[512,512]{1,0:T(8,128)(2,1)S(1)} %get-tuple-element.442.nb_ref, bf16[2,512,1024]{2,1,0:T(8,128)(2,1)S(1)} %get-tuple-element.463.resid_ref), custom_call_target="tpu_custom_call" | custom-call | tf_op jit(solution)/shard_map/grad_out/pallas_call | solution.py:230
  47.4 1.8 %collective-permute-start.17 = (bf16[256,1024]{1,0:T(8,128)(2,1)S(1)}, bf16[256,1024]{1,0:T(8,128)(2,1)S(1)}, u32[]{:S(2)}, u32[]{:S(2)}) collective-permute-start(bf16[256,1024]{1,0:T(8,128)(2,1)S(1)} %get-tuple-element.482), channel_id=1, source_target_pairs={{0,4},{1,5},{2,6},{3,7},{4,0},{5,1},{6,2},{7,3},{8,12},{9,13},{10,... | collective-permute-start | bytes 1572872 | tf_op jit(solution)/shard_map/ppermute | solution.py:36
  49.2 1.5 %collective-permute-start.16 = (bf16[256,1024]{1,0:T(8,128)(2,1)S(1)}, bf16[256,1024]{1,0:T(8,128)(2,1)S(1)}, u32[]{:S(2)}, u32[]{:S(2)}) collective-permute-start(bf16[256,1024]{1,0:T(8,128)(2,1)S(1)} %get-tuple-element.480), channel_id=1, source_target_pairs={{0,2},{1,3},{2,0},{3,1},{4,6},{5,7},{6,4},{7,5},{8,10},{9,11},{10,... | collective-permute-start | bytes 1572872 | tf_op jit(solution)/shard_map/ppermute | solution.py:36
  50.7 3.3 %collective-permute-done.14.b_ref = bf16[256,1024]{1,0:T(8,128)(2,1)S(1)} collective-permute-done((bf16[256,1024]{1,0:T(8,128)(2,1)S(1)}, bf16[256,1024]{1,0:T(8,128)(2,1)S(1)}, u32[]{:S(2)}, u32[]{:S(2)}) %collective-permute-start.14) | collective-permute-done | bytes 524320 | tf_op jit(solution)/shard_map/ppermute | solution.py:36
  54.0 0.1 join.21.w0
  54.1 0.1 join.22.w_ref
  54.2 4.4 %grad_in.3 = (bf16[2,512,512]{2,1,0:T(8,128)(2,1)S(1)}, bf16[256,1024]{1,0:T(8,128)(2,1)S(1)}, bf16[256,1024]{1,0:T(8,128)(2,1)S(1)}) custom-call(bf16[2,512,1024]{2,1,0:T(8,128)(2,1)S(1)} %get-tuple-element.463.resid_ref, bf16[512,1024]{1,0:T(8,128)(2,1)S(1)} %join.22.w_ref, f32[512,512]{1,0:T(8,128)S(1)} %get-tuple-element.465.slope_own, ...), custom_call_target="tpu_custom_call" | custom-call | tf_op jit(solution)/shard_map/grad_in/pallas_call | solution.py:265
  58.6 0.6 collective-permute-start.15
  59.2 1.5 %collective-permute-start.22 = (bf16[256,1024]{1,0:T(8,128)(2,1)S(1)}, bf16[256,1024]{1,0:T(8,128)(2,1)S(1)}, u32[]{:S(2)}, u32[]{:S(2)}) collective-permute-start(bf16[256,1024]{1,0:T(8,128)(2,1)S(1)} %get-tuple-element.510), channel_id=1, source_target_pairs={{0,2},{1,3},{2,0},{3,1},{4,6},{5,7},{6,4},{7,5},{8,10},{9,11},{10,... | collective-permute-start | bytes 1572872 | tf_op jit(solution)/shard_map/ppermute | solution.py:36
  60.7 0.2 collective-permute-start.21
  61.0 4.3 %collective-permute-done.17.b_ref = bf16[256,1024]{1,0:T(8,128)(2,1)S(1)} collective-permute-done((bf16[256,1024]{1,0:T(8,128)(2,1)S(1)}, bf16[256,1024]{1,0:T(8,128)(2,1)S(1)}, u32[]{:S(2)}, u32[]{:S(2)}) %collective-permute-start.17) | collective-permute-done | bytes 524320 | tf_op jit(solution)/shard_map/ppermute | solution.py:36
  65.2 0.1 fold.8
  65.4 0.1 fold.9
  65.5 4.0 %collective-permute-done.15.a_ref = bf16[256,1024]{1,0:T(8,128)(2,1)S(1)} collective-permute-done((bf16[256,1024]{1,0:T(8,128)(2,1)S(1)}, bf16[256,1024]{1,0:T(8,128)(2,1)S(1)}, u32[]{:S(2)}, u32[]{:S(2)}) %collective-permute-start.15) | collective-permute-done | bytes 524320 | tf_op jit(solution)/shard_map/ppermute | solution.py:560
  69.6 1.7 %collective-permute-start.18 = (bf16[256,1024]{1,0:T(8,128)(2,1)S(1)}, bf16[256,1024]{1,0:T(8,128)(2,1)S(1)}, u32[]{:S(2)}, u32[]{:S(2)}) collective-permute-start(bf16[256,1024]{1,0:T(8,128)(2,1)S(1)} %collective-permute-done.14.b_ref), channel_id=1, source_target_pairs={{0,16},{16,0},{1,17},{17,1},{2,18},{18,2},{3,19},{19,3},{4,20},{20... | collective-permute-start | bytes 1572872 | tf_op jit(solution)/shard_map/ppermute | solution.py:560
  71.3 1.5 %collective-permute-start.20 = (bf16[128,1024]{1,0:T(8,128)(2,1)S(1)}, bf16[128,1024]{1,0:T(8,128)(2,1)S(1)}, u32[]{:S(2)}, u32[]{:S(2)}) collective-permute-start(bf16[128,1024]{1,0:T(8,128)(2,1)S(1)} %get-tuple-element.506), channel_id=1, source_target_pairs={{0,2},{1,3},{2,0},{3,1},{4,6},{5,7},{6,4},{7,5},{8,10},{9,11},{10,... | collective-permute-start | bytes 786440 | tf_op jit(solution)/shard_map/ppermute | solution.py:36
  72.8 1.6 %collective-permute-start.19 = (bf16[128,1024]{1,0:T(8,128)(2,1)S(1)}, bf16[128,1024]{1,0:T(8,128)(2,1)S(1)}, u32[]{:S(2)}, u32[]{:S(2)}) collective-permute-start(bf16[128,1024]{1,0:T(8,128)(2,1)S(1)} %get-tuple-element.504), channel_id=1, source_target_pairs={{0,8},{1,9},{2,10},{3,11},{4,12},{5,13},{6,14},{7,15},{8,0},{9,1},... | collective-permute-start | bytes 786440 | tf_op jit(solution)/shard_map/ppermute | solution.py:36
  74.4 0.1 fold.10
  74.5 2.1 %collective-permute-start.24 = (bf16[128,1024]{1,0:T(8,128)(2,1)S(1)}, bf16[128,1024]{1,0:T(8,128)(2,1)S(1)}, u32[]{:S(2)}, u32[]{:S(2)}) collective-permute-start(bf16[128,1024]{1,0:T(8,128)(2,1)S(1)} %get-tuple-element.554), channel_id=1, source_target_pairs={{0,4},{1,5},{2,6},{3,7},{4,0},{5,1},{6,2},{7,3},{8,12},{9,13},{10,... | collective-permute-start | bytes 786440 | tf_op jit(solution)/shard_map/ppermute | solution.py:36
  76.6 2.4 %collective-permute-done.21.b_ref = bf16[256,1024]{1,0:T(8,128)(2,1)S(1)} collective-permute-done((bf16[256,1024]{1,0:T(8,128)(2,1)S(1)}, bf16[256,1024]{1,0:T(8,128)(2,1)S(1)}, u32[]{:S(2)}, u32[]{:S(2)}) %collective-permute-start.21) | collective-permute-done | bytes 524320 | tf_op jit(solution)/shard_map/ppermute | solution.py:36
  79.0 0.1 fold.11
  79.1 0.1 collective-permute-start.26
  79.3 2.7 %collective-permute-start.27 = (bf16[64,1024]{1,0:T(8,128)(2,1)S(1)}, bf16[64,1024]{1,0:T(8,128)(2,1)S(1)}, u32[]{:S(2)}, u32[]{:S(2)}) collective-permute-start(bf16[64,1024]{1,0:T(8,128)(2,1)S(1)} %get-tuple-element.571), channel_id=1, source_target_pairs={{0,8},{1,9},{2,10},{3,11},{4,12},{5,13},{6,14},{7,15},{8,0},{9,1},... | collective-permute-start | bytes 393224 | tf_op jit(solution)/shard_map/ppermute | solution.py:36
  82.0 5.2 %collective-permute-done.19.b_ref = bf16[128,1024]{1,0:T(8,128)(2,1)S(1)} collective-permute-done((bf16[128,1024]{1,0:T(8,128)(2,1)S(1)}, bf16[128,1024]{1,0:T(8,128)(2,1)S(1)}, u32[]{:S(2)}, u32[]{:S(2)}) %collective-permute-start.19) | collective-permute-done | bytes 262176 | tf_op jit(solution)/shard_map/ppermute | solution.py:36
  87.3 0.1 join.23.w1
  87.3 0.7 input_nb.2
  88.1 1.2 %collective-permute-start.28 = (bf16[64,1024]{1,0:T(8,128)(2,1)S(1)}, bf16[64,1024]{1,0:T(8,128)(2,1)S(1)}, u32[]{:S(2)}, u32[]{:S(2)}) collective-permute-start(bf16[64,1024]{1,0:T(8,128)(2,1)S(1)} %get-tuple-element.574), channel_id=1, source_target_pairs={{0,8},{1,9},{2,10},{3,11},{4,12},{5,13},{6,14},{7,15},{8,0},{9,1},... | collective-permute-start | bytes 393224 | tf_op jit(solution)/shard_map/ppermute | solution.py:36
  89.4 0.7 input_nb.3
  90.1 0.1 collective-permute-start.25
  90.2 0.5 collective-permute-start.23
  90.7 1.4 %collective-permute-done.27.refs_1_ = bf16[64,1024]{1,0:T(8,128)(2,1)S(1)} collective-permute-done((bf16[64,1024]{1,0:T(8,128)(2,1)S(1)}, bf16[64,1024]{1,0:T(8,128)(2,1)S(1)}, u32[]{:S(2)}, u32[]{:S(2)}) %collective-permute-start.27) | collective-permute-done | bytes 131104 | tf_op jit(solution)/shard_map/ppermute | solution.py:36
  92.1 3.2 %collective-permute-done.28.refs_3_ = bf16[64,1024]{1,0:T(8,128)(2,1)S(1)} collective-permute-done((bf16[64,1024]{1,0:T(8,128)(2,1)S(1)}, bf16[64,1024]{1,0:T(8,128)(2,1)S(1)}, u32[]{:S(2)}, u32[]{:S(2)}) %collective-permute-start.28) | collective-permute-done | bytes 131104 | tf_op jit(solution)/shard_map/ppermute | solution.py:36
  95.3 1.4 %total.2 = f32[128,1024]{1,0:T(8,128)} custom-call(s32[2]{0:T(128)S(1)} %copy-done.5, bf16[64,1024]{1,0:T(8,128)(2,1)S(1)} %get-tuple-element.570.refs_0_, bf16[64,1024]{1,0:T(8,128)(2,1)S(1)} %collective-permute-done.27.refs_1_, bf16[64,1024]{1,0:T(8,128)(2,1)S(1)} %get-tuple-element.577.refs_2_, bf16[64,1024]{1,0:T(8,128)(2,1)S(1)} %collective-permute-done.28.refs_3_, ...), custom_call_target="tpu_custom_call" | custom-call | tf_op jit(solution)/shard_map/total/pallas_call | solution.py:452
  96.8 0.1 collective-permute-start.30
  96.9 2.4 %input_own.1 = bf16[512,1024]{1,0:T(8,128)(2,1)} custom-call(bf16[2,512,512]{2,1,0:T(8,128)(2,1)S(1)} %get-tuple-element.432.pre0, bf16[2,512,512]{2,1,0:T(8,128)(2,1)S(1)} %get-tuple-element.473.pre1, bf16[512,1024]{1,0:T(8,128)(2,1)S(1)} %join.21.w0, bf16[512,1024]{1,0:T(8,128)(2,1)S(1)} %join.23.w1, ...), custom_call_target="tpu_custom_call" | custom-call | tf_op jit(solution)/shard_map/input_own/pallas_call | solution.py:334
  99.3 4.1 %collective-permute-done.30.refs_3_ = bf16[64,1024]{1,0:T(8,128)(2,1)S(1)} collective-permute-done((bf16[64,1024]{1,0:T(8,128)(2,1)S(1)}, bf16[64,1024]{1,0:T(8,128)(2,1)S(1)}, u32[]{:S(2)}, u32[]{:S(2)}) %collective-permute-start.30) | collective-permute-done | bytes 131104 | tf_op jit(solution)/shard_map/ppermute | solution.py:36
  103.4 1.4 %total.3 = f32[128,1024]{1,0:T(8,128)} custom-call(s32[2]{0:T(128)S(1)} %copy-done.5, bf16[64,1024]{1,0:T(8,128)(2,1)S(1)} %get-tuple-element.594.refs_0_, bf16[64,1024]{1,0:T(8,128)(2,1)S(1)} %collective-permute-done.29.refs_1_, bf16[64,1024]{1,0:T(8,128)(2,1)S(1)} %get-tuple-element.601.refs_2_, bf16[64,1024]{1,0:T(8,128)(2,1)S(1)} %collective-permute-done.30.refs_3_, ...), custom_call_target="tpu_custom_call" | custom-call | tf_op jit(solution)/shard_map/total/pallas_call | solution.py:452
  (64 shorter events, 0.5 us)
Async XLA Ops:
  0.6 25.6 %collective-permute-start.7 = (bf16[512,2048]{1,0:T(8,128)(2,1)}, bf16[512,2048]{1,0:T(8,128)(2,1)}, u32[]{:S(2)}, u32[]{:S(2)}) collective-permute-start(bf16[512,2048]{1,0:T(8,128)(2,1)} %in_ref), channel_id=1, source_target_pairs={{0,1},{1,0},{2,3},{3,2},{4,5},{5,4},{6,7},{7,6},{8,9},{9,8},{10,11... | collective-permute-start | bytes 6291464 | tf_op jit(solution)/shard_map/ppermute | solution.py:36
  1.1 14.1 %collective-permute-start = (bf16[512,1024]{1,0:T(8,128)(2,1)}, bf16[512,1024]{1,0:T(8,128)(2,1)}, u32[]{:S(2)}, u32[]{:S(2)}) collective-permute-start(bf16[512,1024]{1,0:T(8,128)(2,1)} %own_ref), channel_id=1, source_target_pairs={{0,1},{1,0},{2,3},{3,2},{4,5},{5,4},{6,7},{7,6},{8,9},{9,8},{10,11... | collective-permute-start | bytes 3145736 | tf_op jit(solution)/shard_map/ppermute | solution.py:36
  2.2 10.6 %collective-permute-start.1 = (bf16[64,1024]{1,0:T(8,128)(2,1)S(1)}, bf16[64,1024]{1,0:T(8,128)(2,1)S(1)}, u32[]{:S(2)}, u32[]{:S(2)}) collective-permute-start(bf16[64,1024]{1,0:T(8,128)(2,1)S(1)} %get-tuple-element.317.a_ref), channel_id=1, source_target_pairs={{0,8},{1,9},{2,10},{3,11},{4,12},{5,13},{6,14},{7,15},{8,0},{9,1},... | collective-permute-start | bytes 393224 | tf_op jit(solution)/shard_map/ppermute | solution.py:36
  6.3 25.5 %collective-permute-start.8 = (bf16[512,1024]{1,0:T(8,128)(2,1)}, bf16[512,1024]{1,0:T(8,128)(2,1)}, u32[]{:S(2)}, u32[]{:S(2)}) collective-permute-start(bf16[512,1024]{1,0:T(8,128)(2,1)} %own_ref.2), channel_id=1, source_target_pairs={{0,1},{1,0},{2,3},{3,2},{4,5},{5,4},{6,7},{7,6},{8,9},{9,8},{10,11... | collective-permute-start | bytes 3145736 | tf_op jit(solution)/shard_map/ppermute | solution.py:36
  12.9 2.4 %copy-start.3 = (bf16[8,1024]{1,0:T(8,128)(2,1)S(1)}, bf16[8,1024]{1,0:T(8,128)(2,1)}, u32[]{:S(2)}) copy-start(bf16[8,1024]{1,0:T(8,128)(2,1)} %pack.1.a_ref) | copy-start | bytes 49156
  12.9 2.9 %copy-start.2 = (bf16[512,2048]{1,0:T(8,128)(2,1)S(1)}, bf16[512,2048]{1,0:T(8,128)(2,1)}, u32[]{:S(2)}) copy-start(bf16[512,2048]{1,0:T(8,128)(2,1)} %in_ref) | copy-start | bytes 6291460
  12.9 2.8 %copy-start.5 = (s32[2]{0:T(128)S(1)}, s32[2]{0:T(128)}, u32[]{:S(2)}) copy-start(s32[2]{0:T(128)} %pad_add_fusion.ids_ref) | copy-start | bytes 28
  12.9 9.7 %collective-permute-start.4 = (bf16[128,1024]{1,0:T(8,128)(2,1)S(1)}, bf16[128,1024]{1,0:T(8,128)(2,1)S(1)}, u32[]{:S(2)}, u32[]{:S(2)}) collective-permute-start(bf16[128,1024]{1,0:T(8,128)(2,1)S(1)} %join.12.a_ref), channel_id=1, source_target_pairs={{0,4},{1,5},{2,6},{3,7},{4,0},{5,1},{6,2},{7,3},{8,12},{9,13},{10,... | collective-permute-start | bytes 786440 | tf_op jit(solution)/shard_map/ppermute | solution.py:36
  13.7 8.9 %collective-permute-start.5 = (bf16[64,1024]{1,0:T(8,128)(2,1)S(1)}, bf16[64,1024]{1,0:T(8,128)(2,1)S(1)}, u32[]{:S(2)}, u32[]{:S(2)}) collective-permute-start(bf16[64,1024]{1,0:T(8,128)(2,1)S(1)} %get-tuple-element.344.a_ref), channel_id=1, source_target_pairs={{0,2},{1,3},{2,0},{3,1},{4,6},{5,7},{6,4},{7,5},{8,10},{9,11},{10,... | collective-permute-start | bytes 393224 | tf_op jit(solution)/shard_map/ppermute | solution.py:36
  15.2 4.0 %collective-permute-start.2 = (bf16[8,1024]{1,0:T(8,128)(2,1)S(1)}, bf16[8,1024]{1,0:T(8,128)(2,1)S(1)}, u32[]{:S(2)}, u32[]{:S(2)}) collective-permute-start(bf16[8,1024]{1,0:T(8,128)(2,1)S(1)} %copy-done.3), channel_id=1, source_target_pairs={{0,2},{1,3},{2,0},{3,1},{4,6},{5,7},{6,4},{7,5},{8,10},{9,11},{10,... | collective-permute-start | bytes 49160 | tf_op jit(solution)/shard_map/ppermute | solution.py:36
  19.2 6.6 %collective-permute-start.3 = (bf16[16,1024]{1,0:T(8,128)(2,1)S(1)}, bf16[16,1024]{1,0:T(8,128)(2,1)S(1)}, u32[]{:S(2)}, u32[]{:S(2)}) collective-permute-start(bf16[16,1024]{1,0:T(8,128)(2,1)S(1)} %join.13.a_ref), channel_id=1, source_target_pairs={{0,8},{1,9},{2,10},{3,11},{4,12},{5,13},{6,14},{7,15},{8,0},{9,1},... | collective-permute-start | bytes 98312 | tf_op jit(solution)/shard_map/ppermute | solution.py:36
  22.7 14.5 %collective-permute-start.12 = (bf16[256,1024]{1,0:T(8,128)(2,1)S(1)}, bf16[256,1024]{1,0:T(8,128)(2,1)S(1)}, u32[]{:S(2)}, u32[]{:S(2)}) collective-permute-start(bf16[256,1024]{1,0:T(8,128)(2,1)S(1)} %join.15.a_ref), channel_id=1, source_target_pairs={{0,16},{16,0},{1,17},{17,1},{2,18},{18,2},{3,19},{19,3},{4,20},{20... | collective-permute-start | bytes 1572872 | tf_op jit(solution)/shard_map/ppermute | solution.py:560
  24.3 12.8 %collective-permute-start.10 = (bf16[256,1024]{1,0:T(8,128)(2,1)S(1)}, bf16[256,1024]{1,0:T(8,128)(2,1)S(1)}, u32[]{:S(2)}, u32[]{:S(2)}) collective-permute-start(bf16[256,1024]{1,0:T(8,128)(2,1)S(1)} %join.15.a_ref), channel_id=1, source_target_pairs={{0,2},{1,3},{2,0},{3,1},{4,6},{5,7},{6,4},{7,5},{8,10},{9,11},{10,... | collective-permute-start | bytes 1572872 | tf_op jit(solution)/shard_map/ppermute | solution.py:36
  25.8 6.0 %collective-permute-start.6 = (bf16[32,1024]{1,0:T(8,128)(2,1)S(1)}, bf16[32,1024]{1,0:T(8,128)(2,1)S(1)}, u32[]{:S(2)}, u32[]{:S(2)}) collective-permute-start(bf16[32,1024]{1,0:T(8,128)(2,1)S(1)} %join.16.a_ref), channel_id=1, source_target_pairs={{0,4},{1,5},{2,6},{3,7},{4,0},{5,1},{6,2},{7,3},{8,12},{9,13},{10,... | collective-permute-start | bytes 196616 | tf_op jit(solution)/shard_map/ppermute | solution.py:36
  26.2 12.8 %collective-permute-start.11 = (bf16[128,1024]{1,0:T(8,128)(2,1)S(1)}, bf16[128,1024]{1,0:T(8,128)(2,1)S(1)}, u32[]{:S(2)}, u32[]{:S(2)}) collective-permute-start(bf16[128,1024]{1,0:T(8,128)(2,1)S(1)} %join.14.a_ref), channel_id=1, source_target_pairs={{0,8},{1,9},{2,10},{3,11},{4,12},{5,13},{6,14},{7,15},{8,0},{9,1},... | collective-permute-start | bytes 786440 | tf_op jit(solution)/shard_map/ppermute | solution.py:36
  31.8 1.5 %copy-start.1 = (bf16[512,1024]{1,0:T(8,128)(2,1)S(1)}, bf16[512,1024]{1,0:T(8,128)(2,1)}, u32[]{:S(2)}) copy-start(bf16[512,1024]{1,0:T(8,128)(2,1)} %own_ref) | copy-start | bytes 3145732
  31.8 1.5 %copy-start.4 = (f32[1024]{0:T(1024)S(1)}, f32[1024]{0:T(1024)}, u32[]{:S(2)}) copy-start(f32[1024]{0:T(1024)} %param.16) | copy-start | bytes 12292
  31.8 1.4 %collective-permute-start.9 = (bf16[64,1024]{1,0:T(8,128)(2,1)S(1)}, bf16[64,1024]{1,0:T(8,128)(2,1)S(1)}, u32[]{:S(2)}, u32[]{:S(2)}) collective-permute-start(bf16[64,1024]{1,0:T(8,128)(2,1)S(1)} %join.17.a_ref), channel_id=1, source_target_pairs={{0,1},{1,0},{2,3},{3,2},{4,5},{5,4},{6,7},{7,6},{8,9},{9,8},{10,11... | collective-permute-start | bytes 393224 | tf_op jit(solution)/shard_map/ppermute | solution.py:36
  37.2 4.5 %copy-start = (bf16[512,1024]{1,0:T(8,128)(2,1)S(1)}, bf16[512,1024]{1,0:T(8,128)(2,1)}, u32[]{:S(2)}) copy-start(bf16[512,1024]{1,0:T(8,128)(2,1)} %own_ref.2) | copy-start | bytes 3145732
  39.1 14.9 %collective-permute-start.14 = (bf16[256,1024]{1,0:T(8,128)(2,1)S(1)}, bf16[256,1024]{1,0:T(8,128)(2,1)S(1)}, u32[]{:S(2)}, u32[]{:S(2)}) collective-permute-start(bf16[256,1024]{1,0:T(8,128)(2,1)S(1)} %join.20.a_ref), channel_id=1, source_target_pairs={{0,4},{1,5},{2,6},{3,7},{4,0},{5,1},{6,2},{7,3},{8,12},{9,13},{10,... | collective-permute-start | bytes 1572872 | tf_op jit(solution)/shard_map/ppermute | solution.py:36
  39.2 14.9 %collective-permute-start.13 = (bf16[256,1024]{1,0:T(8,128)(2,1)S(1)}, bf16[256,1024]{1,0:T(8,128)(2,1)S(1)}, u32[]{:S(2)}, u32[]{:S(2)}) collective-permute-start(bf16[256,1024]{1,0:T(8,128)(2,1)S(1)} %collective-permute-done.10.b_ref), channel_id=1, source_target_pairs={{0,16},{16,0},{1,17},{17,1},{2,18},{18,2},{3,19},{19,3},{4,20},{20... | collective-permute-start | bytes 1572872 | tf_op jit(solution)/shard_map/ppermute | solution.py:560
  47.4 17.8 %collective-permute-start.17 = (bf16[256,1024]{1,0:T(8,128)(2,1)S(1)}, bf16[256,1024]{1,0:T(8,128)(2,1)S(1)}, u32[]{:S(2)}, u32[]{:S(2)}) collective-permute-start(bf16[256,1024]{1,0:T(8,128)(2,1)S(1)} %get-tuple-element.482), channel_id=1, source_target_pairs={{0,4},{1,5},{2,6},{3,7},{4,0},{5,1},{6,2},{7,3},{8,12},{9,13},{10,... | collective-permute-start | bytes 1572872 | tf_op jit(solution)/shard_map/ppermute | solution.py:36
  49.2 16.2 %collective-permute-start.16 = (bf16[256,1024]{1,0:T(8,128)(2,1)S(1)}, bf16[256,1024]{1,0:T(8,128)(2,1)S(1)}, u32[]{:S(2)}, u32[]{:S(2)}) collective-permute-start(bf16[256,1024]{1,0:T(8,128)(2,1)S(1)} %get-tuple-element.480), channel_id=1, source_target_pairs={{0,2},{1,3},{2,0},{3,1},{4,6},{5,7},{6,4},{7,5},{8,10},{9,11},{10,... | collective-permute-start | bytes 1572872 | tf_op jit(solution)/shard_map/ppermute | solution.py:36
  58.6 11.0 %collective-permute-start.15 = (bf16[256,1024]{1,0:T(8,128)(2,1)S(1)}, bf16[256,1024]{1,0:T(8,128)(2,1)S(1)}, u32[]{:S(2)}, u32[]{:S(2)}) collective-permute-start(bf16[256,1024]{1,0:T(8,128)(2,1)S(1)} %join.20.a_ref), channel_id=1, source_target_pairs={{0,16},{16,0},{1,17},{17,1},{2,18},{18,2},{3,19},{19,3},{4,20},{20... | collective-permute-start | bytes 1572872 | tf_op jit(solution)/shard_map/ppermute | solution.py:560
  59.2 15.2 %collective-permute-start.22 = (bf16[256,1024]{1,0:T(8,128)(2,1)S(1)}, bf16[256,1024]{1,0:T(8,128)(2,1)S(1)}, u32[]{:S(2)}, u32[]{:S(2)}) collective-permute-start(bf16[256,1024]{1,0:T(8,128)(2,1)S(1)} %get-tuple-element.510), channel_id=1, source_target_pairs={{0,2},{1,3},{2,0},{3,1},{4,6},{5,7},{6,4},{7,5},{8,10},{9,11},{10,... | collective-permute-start | bytes 1572872 | tf_op jit(solution)/shard_map/ppermute | solution.py:36
  60.7 18.3 %collective-permute-start.21 = (bf16[256,1024]{1,0:T(8,128)(2,1)S(1)}, bf16[256,1024]{1,0:T(8,128)(2,1)S(1)}, u32[]{:S(2)}, u32[]{:S(2)}) collective-permute-start(bf16[256,1024]{1,0:T(8,128)(2,1)S(1)} %get-tuple-element.508), channel_id=1, source_target_pairs={{0,4},{1,5},{2,6},{3,7},{4,0},{5,1},{6,2},{7,3},{8,12},{9,13},{10,... | collective-permute-start | bytes 1572872 | tf_op jit(solution)/shard_map/ppermute | solution.py:36
  69.6 17.7 %collective-permute-start.18 = (bf16[256,1024]{1,0:T(8,128)(2,1)S(1)}, bf16[256,1024]{1,0:T(8,128)(2,1)S(1)}, u32[]{:S(2)}, u32[]{:S(2)}) collective-permute-start(bf16[256,1024]{1,0:T(8,128)(2,1)S(1)} %collective-permute-done.14.b_ref), channel_id=1, source_target_pairs={{0,16},{16,0},{1,17},{17,1},{2,18},{18,2},{3,19},{19,3},{4,20},{20... | collective-permute-start | bytes 1572872 | tf_op jit(solution)/shard_map/ppermute | solution.py:560
  71.3 7.9 %collective-permute-start.20 = (bf16[128,1024]{1,0:T(8,128)(2,1)S(1)}, bf16[128,1024]{1,0:T(8,128)(2,1)S(1)}, u32[]{:S(2)}, u32[]{:S(2)}) collective-permute-start(bf16[128,1024]{1,0:T(8,128)(2,1)S(1)} %get-tuple-element.506), channel_id=1, source_target_pairs={{0,2},{1,3},{2,0},{3,1},{4,6},{5,7},{6,4},{7,5},{8,10},{9,11},{10,... | collective-permute-start | bytes 786440 | tf_op jit(solution)/shard_map/ppermute | solution.py:36
  72.8 14.3 %collective-permute-start.19 = (bf16[128,1024]{1,0:T(8,128)(2,1)S(1)}, bf16[128,1024]{1,0:T(8,128)(2,1)S(1)}, u32[]{:S(2)}, u32[]{:S(2)}) collective-permute-start(bf16[128,1024]{1,0:T(8,128)(2,1)S(1)} %get-tuple-element.504), channel_id=1, source_target_pairs={{0,8},{1,9},{2,10},{3,11},{4,12},{5,13},{6,14},{7,15},{8,0},{9,1},... | collective-permute-start | bytes 786440 | tf_op jit(solution)/shard_map/ppermute | solution.py:36
  74.5 13.5 %collective-permute-start.24 = (bf16[128,1024]{1,0:T(8,128)(2,1)S(1)}, bf16[128,1024]{1,0:T(8,128)(2,1)S(1)}, u32[]{:S(2)}, u32[]{:S(2)}) collective-permute-start(bf16[128,1024]{1,0:T(8,128)(2,1)S(1)} %get-tuple-element.554), channel_id=1, source_target_pairs={{0,4},{1,5},{2,6},{3,7},{4,0},{5,1},{6,2},{7,3},{8,12},{9,13},{10,... | collective-permute-start | bytes 786440 | tf_op jit(solution)/shard_map/ppermute | solution.py:36
  79.1 17.5 %collective-permute-start.26 = (bf16[128,1024]{1,0:T(8,128)(2,1)S(1)}, bf16[128,1024]{1,0:T(8,128)(2,1)S(1)}, u32[]{:S(2)}, u32[]{:S(2)}) collective-permute-start(bf16[128,1024]{1,0:T(8,128)(2,1)S(1)} %get-tuple-element.569), channel_id=1, source_target_pairs={{0,2},{1,3},{2,0},{3,1},{4,6},{5,7},{6,4},{7,5},{8,10},{9,11},{10,... | collective-permute-start | bytes 786440 | tf_op jit(solution)/shard_map/ppermute | solution.py:36
  79.3 12.8 %collective-permute-start.27 = (bf16[64,1024]{1,0:T(8,128)(2,1)S(1)}, bf16[64,1024]{1,0:T(8,128)(2,1)S(1)}, u32[]{:S(2)}, u32[]{:S(2)}) collective-permute-start(bf16[64,1024]{1,0:T(8,128)(2,1)S(1)} %get-tuple-element.571), channel_id=1, source_target_pairs={{0,8},{1,9},{2,10},{3,11},{4,12},{5,13},{6,14},{7,15},{8,0},{9,1},... | collective-permute-start | bytes 393224 | tf_op jit(solution)/shard_map/ppermute | solution.py:36
  88.1 7.1 %collective-permute-start.28 = (bf16[64,1024]{1,0:T(8,128)(2,1)S(1)}, bf16[64,1024]{1,0:T(8,128)(2,1)S(1)}, u32[]{:S(2)}, u32[]{:S(2)}) collective-permute-start(bf16[64,1024]{1,0:T(8,128)(2,1)S(1)} %get-tuple-element.574), channel_id=1, source_target_pairs={{0,8},{1,9},{2,10},{3,11},{4,12},{5,13},{6,14},{7,15},{8,0},{9,1},... | collective-permute-start | bytes 393224 | tf_op jit(solution)/shard_map/ppermute | solution.py:36
  90.1 6.8 %collective-permute-start.25 = (bf16[256,1024]{1,0:T(8,128)(2,1)S(1)}, bf16[256,1024]{1,0:T(8,128)(2,1)S(1)}, u32[]{:S(2)}, u32[]{:S(2)}) collective-permute-start(bf16[256,1024]{1,0:T(8,128)(2,1)S(1)} %input_nb.3), channel_id=1, source_target_pairs={{0,1},{1,0},{2,3},{3,2},{4,5},{5,4},{6,7},{7,6},{8,9},{9,8},{10,11... | collective-permute-start | bytes 1572872 | tf_op jit(solution)/shard_map/ppermute | solution.py:36
  90.2 6.7 %collective-permute-start.23 = (bf16[256,1024]{1,0:T(8,128)(2,1)S(1)}, bf16[256,1024]{1,0:T(8,128)(2,1)S(1)}, u32[]{:S(2)}, u32[]{:S(2)}) collective-permute-start(bf16[256,1024]{1,0:T(8,128)(2,1)S(1)} %input_nb.2), channel_id=1, source_target_pairs={{0,1},{1,0},{2,3},{3,2},{4,5},{5,4},{6,7},{7,6},{8,9},{9,8},{10,11... | collective-permute-start | bytes 1572872 | tf_op jit(solution)/shard_map/ppermute | solution.py:36
  92.1 7.2 %collective-permute-start.29 = (bf16[64,1024]{1,0:T(8,128)(2,1)S(1)}, bf16[64,1024]{1,0:T(8,128)(2,1)S(1)}, u32[]{:S(2)}, u32[]{:S(2)}) collective-permute-start(bf16[64,1024]{1,0:T(8,128)(2,1)S(1)} %get-tuple-element.595), channel_id=1, source_target_pairs={{0,4},{1,5},{2,6},{3,7},{4,0},{5,1},{6,2},{7,3},{8,12},{9,13},{10,... | collective-permute-start | bytes 393224 | tf_op jit(solution)/shard_map/ppermute | solution.py:36
  96.8 6.7 %collective-permute-start.30 = (bf16[64,1024]{1,0:T(8,128)(2,1)S(1)}, bf16[64,1024]{1,0:T(8,128)(2,1)S(1)}, u32[]{:S(2)}, u32[]{:S(2)}) collective-permute-start(bf16[64,1024]{1,0:T(8,128)(2,1)S(1)} %get-tuple-element.596), channel_id=1, source_target_pairs={{0,8},{1,9},{2,10},{3,11},{4,12},{5,13},{6,14},{7,15},{8,0},{9,1},... | collective-permute-start | bytes 393224 | tf_op jit(solution)/shard_map/ppermute | solution.py:36
